TPU v7x, 256 devices: a whole 4x4x8 slice. The times are simulated.
256 devices in a mesh: dst: 32 (over y, x, core), src: 8 (over z).
Axes of the slice: x: 4, y: 4, z: 8, core: 2. Of those that a mesh axis runs over, the one named last changes fastest.
Arguments:
- inputs: float32 [32768, 256], P(('dst', 'src')), may hold values from -64 to 64
- projection: float32 [256, 512], replicated, may hold values from -0.375 to 0.375
- att_src: float32 [8, 64], replicated, may hold values from -0.75 to 0.75
- att_dst: float32 [8, 64], replicated, may hold values from -0.75 to 0.75
- blocks: int32 [32, 8, 32, 2], P('dst', 'src'), may hold values from 0 to 31, as said below
- counts: int32 [32, 8], P('dst', 'src'), may hold values from 16 to 32, as said below
- tile_masks: int32 [32, 8, 32, 128, 128], P('dst', 'src'), may hold values 0 or 1
- cotangent: float32 [32768, 512], P(('dst', 'src')), may hold values from -6 to 6
Outputs:
- output: float32 [32768, 512], P(('dst', 'src'))
- in_grad: float32 [32768, 256], P(('dst', 'src'))
- proj_grad: float32 [256, 512], replicated
- att_src_grad: float32 [8, 64], replicated
- att_dst_grad: float32 [8, 64], replicated
Inputs may be any that keep to these rules, and one draw needn't show every extreme that they name: blocks[i, j, k] = (b, c) with b below 8 and c below 32; the slots of one device name distinct blocks. Only the first counts[i, j] slots of device (i, j) hold edges; some device uses all 32.
All inputs are finite; a program needn't handle non-finite values. No bound on the sum of `tile_masks` on one device may be relied on, other than what follows from the above.
Results may differ from a plain program's by a relative error of at most 0.0029.
Values sent between devices are 32-bit elements; how exact they have to be, the bound alone decides.
A program may use at most 128 MiB of HBM per device.

v0:
```python
import jax
import jax.numpy as jnp
from jax import lax
from jax.sharding import PartitionSpec as P

HIGHEST = lax.Precision.HIGHEST
NEG_FILL = -1e30


def leaky_relu(raw):
    return jnp.where(raw > 0, raw, 0.2 * raw)


def leaky_slope(raw):
    return jnp.where(raw > 0, 1.0, 0.2)


def shards(inputs, projection, att_src, att_dst, blocks, counts, tile_masks, cotangent):
    own_rows = inputs.shape[0]
    head_count, head_width = att_src.shape
    feat_out = head_count * head_width
    tile_size = tile_masks.shape[-1]
    coords = blocks[0, 0]
    live_count = counts[0, 0]
    mask_tiles = tile_masks[0, 0]

    def head_scores(values, vector):
        return jnp.einsum(
            "rhc,hc->rh",
            values.reshape(values.shape[0], head_count, head_width),
            vector,
            precision=HIGHEST,
        )

    def spread(scores, vector):
        return (scores[:, :, None] * vector[None]).reshape(scores.shape[0], feat_out)

    h_own = jnp.dot(inputs, projection, precision=HIGHEST)
    h_panel = lax.all_gather(h_own, "dst", axis=0, tiled=True)
    src_rows = h_panel.shape[0]
    ss_panel = head_scores(h_panel, att_src)
    sd_own = head_scores(h_own, att_dst)
    ss_own = head_scores(h_own, att_src)
    sd_rows = lax.all_gather(sd_own, "src", axis=0, tiled=True)
    dst_rows = sd_rows.shape[0]
    own_start = lax.axis_index("src") * own_rows

    def tile_inputs(slot):
        dst_start = coords[slot, 0] * tile_size
        src_start = coords[slot, 1] * tile_size
        keep = lax.dynamic_index_in_dim(mask_tiles, slot, 0, keepdims=False) > 0
        sd_tile = lax.dynamic_slice_in_dim(sd_rows, dst_start, tile_size, 0)
        ss_tile = lax.dynamic_slice_in_dim(ss_panel, src_start, tile_size, 0)
        raw = sd_tile.T[:, :, None] + ss_tile.T[:, None, :]
        h_src = lax.dynamic_slice_in_dim(h_panel, src_start, tile_size, 0).reshape(
            tile_size, head_count, head_width
        )
        return (dst_start, src_start, keep[None], raw, h_src)

    self_raw = sd_own + ss_own
    self_logit = leaky_relu(self_raw)
    row_max = lax.dynamic_update_slice_in_dim(
        jnp.full((dst_rows, head_count), NEG_FILL, jnp.float32), self_logit, own_start, 0
    )
    row_sum = lax.dynamic_update_slice_in_dim(
        jnp.zeros((dst_rows, head_count), jnp.float32),
        jnp.ones((own_rows, head_count), jnp.float32),
        own_start,
        0,
    )
    row_acc = lax.dynamic_update_slice_in_dim(
        jnp.zeros((dst_rows, feat_out), jnp.float32), h_own, own_start, 0
    )

    def forward_step(slot, carry):
        row_max, row_sum, row_acc = carry
        dst_start, src_start, keep, raw, h_src = tile_inputs(slot)
        logits = leaky_relu(raw)
        tile_max = jnp.max(jnp.where(keep, logits, NEG_FILL), axis=2).T
        old_max = lax.dynamic_slice_in_dim(row_max, dst_start, tile_size, 0)
        new_max = jnp.maximum(old_max, tile_max)
        weights = jnp.exp(jnp.where(keep, logits - new_max.T[:, :, None], NEG_FILL))
        factor = jnp.exp(old_max - new_max)
        new_sum = (
            lax.dynamic_slice_in_dim(row_sum, dst_start, tile_size, 0) * factor
            + jnp.sum(weights, axis=2).T
        )
        old_acc = lax.dynamic_slice_in_dim(row_acc, dst_start, tile_size, 0).reshape(
            tile_size, head_count, head_width
        )
        new_acc = old_acc * factor[:, :, None] + jnp.einsum(
            "hds,shc->dhc", weights, h_src, precision=HIGHEST
        )
        row_max = lax.dynamic_update_slice_in_dim(row_max, new_max, dst_start, 0)
        row_sum = lax.dynamic_update_slice_in_dim(row_sum, new_sum, dst_start, 0)
        row_acc = lax.dynamic_update_slice_in_dim(
            row_acc, new_acc.reshape(tile_size, feat_out), dst_start, 0
        )
        return (row_max, row_sum, row_acc)

    row_max, row_sum, row_acc = lax.fori_loop(
        0, live_count, forward_step, (row_max, row_sum, row_acc)
    )
    full_max = lax.pmax(row_max, "src")
    shift = jnp.exp(row_max - full_max)
    shifted_acc = (row_acc.reshape(dst_rows, head_count, head_width) * shift[:, :, None]).reshape(
        dst_rows, feat_out
    )
    own_sum, own_acc = (
        lax.psum_scatter(row_sum * shift, "src", scatter_dimension=0, tiled=True),
        lax.psum_scatter(shifted_acc, "src", scatter_dimension=0, tiled=True),
    )
    own_max = lax.dynamic_slice_in_dim(full_max, own_start, own_rows, 0)
    agg = (own_acc.reshape(own_rows, head_count, head_width) / own_sum[:, :, None]).reshape(
        own_rows, feat_out
    )
    output = jax.nn.elu(agg)
    out_grad = cotangent * jnp.where(agg > 0, 1.0, jnp.exp(agg))
    grad3 = out_grad.reshape(own_rows, head_count, head_width)
    row_dot = jnp.sum(grad3 * agg.reshape(own_rows, head_count, head_width), axis=2)
    grad_rows, dot_rows, sum_rows = (
        lax.all_gather(out_grad, "src", axis=0, tiled=True),
        lax.all_gather(row_dot, "src", axis=0, tiled=True),
        lax.all_gather(own_sum, "src", axis=0, tiled=True),
    )

    def backward_step(slot, carry):
        d_dst, d_src, d_hsrc = carry
        dst_start, src_start, keep, raw, h_src = tile_inputs(slot)
        logits = leaky_relu(raw)
        max_tile = lax.dynamic_slice_in_dim(full_max, dst_start, tile_size, 0).T
        sum_tile = lax.dynamic_slice_in_dim(sum_rows, dst_start, tile_size, 0).T
        alpha = (
            jnp.exp(jnp.where(keep, logits - max_tile[:, :, None], NEG_FILL)) / sum_tile[:, :, None]
        )
        grad_tile = lax.dynamic_slice_in_dim(grad_rows, dst_start, tile_size, 0).reshape(
            tile_size, head_count, head_width
        )
        dot_tile = lax.dynamic_slice_in_dim(dot_rows, dst_start, tile_size, 0).T
        d_alpha = jnp.einsum("dhc,shc->hds", grad_tile, h_src, precision=HIGHEST)
        d_raw = alpha * (d_alpha - dot_tile[:, :, None]) * leaky_slope(raw)
        new_dst = (
            lax.dynamic_slice_in_dim(d_dst, dst_start, tile_size, 0) + jnp.sum(d_raw, axis=2).T
        )
        new_src = (
            lax.dynamic_slice_in_dim(d_src, src_start, tile_size, 0) + jnp.sum(d_raw, axis=1).T
        )
        new_hsrc = lax.dynamic_slice_in_dim(d_hsrc, src_start, tile_size, 0) + jnp.einsum(
            "hds,dhc->shc", alpha, grad_tile, precision=HIGHEST
        ).reshape(tile_size, feat_out)
        d_dst = lax.dynamic_update_slice_in_dim(d_dst, new_dst, dst_start, 0)
        d_src = lax.dynamic_update_slice_in_dim(d_src, new_src, src_start, 0)
        d_hsrc = lax.dynamic_update_slice_in_dim(d_hsrc, new_hsrc, src_start, 0)
        return (d_dst, d_src, d_hsrc)

    start_grads = (
        jnp.zeros((dst_rows, head_count), jnp.float32),
        jnp.zeros((src_rows, head_count), jnp.float32),
        jnp.zeros((src_rows, feat_out), jnp.float32),
    )
    d_dst, d_src, d_hsrc = lax.fori_loop(0, live_count, backward_step, start_grads)
    h3_own = h_own.reshape(own_rows, head_count, head_width)
    alpha_self = jnp.exp(self_logit - own_max) / own_sum
    d_alpha_self = jnp.sum(grad3 * h3_own, axis=2)
    d_self = alpha_self * (d_alpha_self - row_dot) * leaky_slope(self_raw)
    dh_self = (alpha_self[:, :, None] * grad3).reshape(own_rows, feat_out)
    dst_total = lax.psum_scatter(d_dst, "src", scatter_dimension=0, tiled=True) + d_self
    hsrc_own, src_own = (
        lax.psum_scatter(d_hsrc, "dst", scatter_dimension=0, tiled=True),
        lax.psum_scatter(d_src, "dst", scatter_dimension=0, tiled=True),
    )
    src_total = src_own + d_self
    dh_own = hsrc_own + dh_self + spread(src_total, att_src) + spread(dst_total, att_dst)
    grad_att_src = jnp.einsum("rh,rhc->hc", src_total, h3_own, precision=HIGHEST)
    grad_proj = jnp.dot(inputs.T, dh_own, precision=HIGHEST)
    in_grad = jnp.dot(dh_own, projection.T, precision=HIGHEST)
    grad_att_dst = jnp.einsum("rh,rhc->hc", dst_total, h3_own, precision=HIGHEST)
    grad_proj, grad_att_src, grad_att_dst = lax.psum(
        (grad_proj, grad_att_src, grad_att_dst), ("dst", "src")
    )
    return (output, in_grad, grad_proj, grad_att_src, grad_att_dst)


def solution(mesh):
    in_specs = (
        P(("dst", "src"), None),
        P(),
        P(),
        P(),
        P("dst", "src", None, None),
        P("dst", "src"),
        P("dst", "src", None, None, None),
        P(("dst", "src"), None),
    )
    out_specs = (P(("dst", "src"), None), P(("dst", "src"), None), P(), P(), P())
    return jax.shard_map(shards, mesh=mesh, in_specs=in_specs, out_specs=out_specs, check_vma=False)
```

profile of v0, /device:TPU:1, one launch (start us, length us, event | category | flops | bytes accessed | tf_op | source)
XLA Modules:
  0.0 1272.8 jit_solution(9109577579237082633)
XLA Ops:
  8.2 2.0 fusion.42
  12.4 22.8 %all_gather.15 = f32[1024,8]{0,1:T(8,128)S(1)} all-gather(f32[128,8]{0,1:T(8,128)S(1)} %bitcast.211), channel_id=1, replica_groups=mesh['dst'=32,'src'=8] {'src'}, dimensions={0}, use_global_device_ids=true | all-gather | bytes 36864 | tf_op jit(solution)/shard_map/all_gather | solution.py:44
  35.9 37.4 %all-gather.3.cloned.1.call-done = f32[4096,512]{1,0:T(8,128)} async-done(((f32[128,512]{1,0:T(8,128)}), f32[4096,512]{1,0:T(8,128)}) %all-gather.3.cloned.1.call-update) | async-done | bytes 8388624 | tf_op jit(solution)/shard_map/all_gather | solution.py:39
  73.3 9.0 copy.27
  82.3 6.8 fusion.45
  89.1 155.8 %while.28 = (s32[]{:T(128)}, f32[1024,8]{0,1:T(8,128)S(1)}, f32[1024,8]{0,1:T(8,128)S(1)}, f32[1024,512]{0,1:T(8,128)S(1)}, s32[]{:T(128)}, /*index=5*/s32[32,2]...) while((s32[]{:T(128)}, f32[1024,8]{0,1:T(8,128)S(1)}, ...), condition=%wide.region_3.4_spmd, body=%wide.region_0.3_spmd.sunk | while | flops 103304208 | bytes 2593103 | solution.py:101
  244.9 81.9 %pmax.7 = f32[1024,8]{0,1:T(8,128)S(1)} all-reduce(f32[1024,8]{0,1:T(8,128)S(1)} %get-tuple-element.136), channel_id=1, replica_groups=mesh['dst'=32,'src'=8] {'src'}, use_global_device_ids=true, to_apply=%region_4.5 | all-reduce | flops 8192 | bytes 65536 | tf_op jit(solution)/shard_map/pmax | solution.py:104
  330.2 32.6 %reduce-scatter.8.cloned.1.call-done = f32[128,8]{0,1:T(8,128)} async-done(((f32[1024,8]{0,1:T(8,128)}), f32[128,8]{0,1:T(8,128)}) %reduce-scatter.8.cloned.1.call-update) | async-done | bytes 4112 | tf_op jit(solution)/shard_map/reduce_scatter | solution.py:110
  362.7 44.6 %reduce-scatter.6.cloned.1.call-done = f32[128,512]{0,1:T(8,128)} async-done(((f32[1024,512]{0,1:T(8,128)}), f32[128,512]{0,1:T(8,128)}) %reduce-scatter.6.cloned.1.call-update) | async-done | bytes 262160 | tf_op jit(solution)/shard_map/reduce_scatter | solution.py:111
  409.1 18.3 %all_gather.17 = f32[1024,8]{0,1:T(8,128)S(1)} all-gather(f32[128,8]{0,1:T(8,128)} %reduce-scatter.8.cloned.1.call-done), channel_id=1, replica_groups=mesh['dst'=32,'src'=8] {'src'}, dimensions={0}, use_global_device_ids=true | all-gather | bytes 36864 | tf_op jit(solution)/shard_map/all_gather | solution.py:124
  427.4 19.3 %all_gather.19 = f32[1024,8]{0,1:T(8,128)S(1)} all-gather(f32[128,8]{0,1:T(8,128)S(1)} %get-tuple-element.202), channel_id=1, replica_groups=mesh['dst'=32,'src'=8] {'src'}, dimensions={0}, use_global_device_ids=true | all-gather | bytes 36864 | tf_op jit(solution)/shard_map/all_gather | solution.py:123
  446.7 9.8 all-gather.5.cloned.1.call-done
  456.5 4.3 broadcast_in_dim.81
  460.7 230.8 %while.29 = (s32[]{:T(128)}, f32[1024,8]{0,1:T(8,128)S(1)}, f32[4096,8]{0,1:T(8,128)S(1)}, f32[4096,512]{0,1:T(8,128)}, s32[]{:T(128)}, /*index=5*/s32[32,2]{0,1...) while((s32[]{:T(128)}, f32[1024,8]{0,1:T(8,128)S(1)}, ...), condition=%wide.region_11.12_spmd, body=%wide.region_8.11_spmd.sunk | while | flops 204029968 | bytes 3109243 | solution.py:161
  466.2 1.8 fusion.94
  476.2 1.8 fusion.94
  486.2 1.8 fusion.94
  496.2 1.8 fusion.94
  506.2 1.8 fusion.94
  516.2 1.8 fusion.94
  526.2 1.8 fusion.94
  536.2 1.8 fusion.94
  546.2 1.8 fusion.94
  556.2 1.8 fusion.94
  566.2 1.8 fusion.94
  576.2 1.8 fusion.94
  694.8 168.8 %reduce-scatter.12.cloned.1.call-done = f32[128,8]{0,1:T(8,128)} async-done(((f32[4096,8]{0,1:T(8,128)}), f32[128,8]{0,1:T(8,128)}) %reduce-scatter.12.cloned.1.call-update) | async-done | bytes 4112 | tf_op jit(solution)/shard_map/reduce_scatter | solution.py:170
  864.2 34.2 %reduce-scatter.14.cloned.1.call-done = f32[128,8]{0,1:T(8,128)} async-done(((f32[1024,8]{0,1:T(8,128)}), f32[128,8]{0,1:T(8,128)}) %reduce-scatter.14.cloned.1.call-update) | async-done | bytes 4112 | tf_op jit(solution)/shard_map/reduce_scatter | solution.py:167
  899.6 105.5 %reduce-scatter.10.cloned.1.call-done = f32[128,512]{0,1:T(8,128)} async-done(((f32[4096,512]{0,1:T(8,128)}), f32[128,512]{0,1:T(8,128)}) %reduce-scatter.10.cloned.1.call-update) | async-done | bytes 262160 | tf_op jit(solution)/shard_map/reduce_scatter | solution.py:169
  1008.2 77.3 %all-reduce = (f32[8,64]{1,0:T(8,128)}, f32[8,64]{1,0:T(8,128)}) all-reduce(f32[8,64]{1,0:T(8,128)S(1)} %bitcast.221, f32[8,64]{1,0:T(8,128)S(1)} %bitcast.222), channel_id=1, replica_groups=mesh['dst'=32,'src'=8] {'dst','src'}, use_global_device_ids=true, to_apply=%region_17.18 | all-reduce | flops 1024 | bytes 8192 | tf_op jit(solution)/shard_map/psum | solution.py:178
  1086.7 177.2 %all-reduce.3.cloned.1.call-done = f32[256,512]{0,1:T(8,128)} async-done(((f32[256,512]{0,1:T(8,128)}), f32[256,512]{0,1:T(8,128)}) %all-reduce.3.cloned.1.call-update) | async-done | bytes 524304 | tf_op jit(solution)/shard_map/psum | solution.py:178
  1263.9 2.0 copy.32
  (581 shorter events, 287.6 us)
Async XLA Ops:
  7.2 1.0 copy-start
  7.2 66.1 %all-gather.3.cloned.1.call-start = ((), (), s32[]{:S(2)}) async-start(), calls=%async_computation.5 | async-start | bytes 8650752 | tf_op jit(solution)/shard_map/all_gather | solution.py:39
  10.2 25.3 %copy-start.9 = (f32[8,64]{1,0:T(8,128)S(1)}, f32[8,64]{1,0:T(8,128)}, u32[]{:S(2)}) copy-start(f32[8,64]{1,0:T(8,128)} %param.14) | copy-start | bytes 6148
  10.3 352.5 %reduce-scatter.8.cloned.1.call-start = ((), (), s32[]{:S(2)}) async-start(), calls=%async_computation.7 | async-start | bytes 36864 | tf_op jit(solution)/shard_map/reduce_scatter | solution.py:110
  82.3 6.9 copy-start.7
  327.5 79.8 %reduce-scatter.6.cloned.1.call-start = ((), (), s32[]{:S(2)}) async-start(), calls=%async_computation.6 | async-start | bytes 2359296 | tf_op jit(solution)/shard_map/reduce_scatter | solution.py:111
  329.1 0.9 copy-start.5
  329.1 127.3 %all-gather.5.cloned.1.call-start = ((), (), s32[]{:S(2)}) async-start(), calls=%async_computation.8 | async-start | bytes 2359296 | tf_op jit(solution)/shard_map/all_gather | solution.py:122
  409.1 454.5 %reduce-scatter.12.cloned.1.call-start = ((), (), s32[]{:S(2)}) async-start(), calls=%async_computation.10 | async-start | bytes 135168 | tf_op jit(solution)/shard_map/reduce_scatter | solution.py:170
  691.6 0.7 copy-start.3
  691.6 0.7 copy-start.6
  692.2 206.2 %reduce-scatter.14.cloned.1.call-start = ((), (), s32[]{:S(2)}) async-start(), calls=%async_computation.11 | async-start | bytes 36864 | tf_op jit(solution)/shard_map/reduce_scatter | solution.py:167
  692.8 312.3 %reduce-scatter.10.cloned.1.call-start = ((), (), s32[]{:S(2)}) async-start(), calls=%async_computation.9 | async-start | bytes 8650752 | tf_op jit(solution)/shard_map/reduce_scatter | solution.py:169
  692.9 0.8 copy-start.10
  692.9 1.0 copy-start.2
  692.9 0.9 copy-start.8
  692.9 312.2 %copy-start.1 = (f32[128,512]{0,1:T(8,128)S(1)}, f32[128,512]{0,1:T(8,128)}, u32[]{:S(2)}) copy-start(f32[128,512]{0,1:T(8,128)} %get-tuple-element.258) | copy-start | bytes 786436
  693.6 312.7 %copy-start.4 = (f32[128,256]{1,0:T(8,128)S(1)}, f32[128,256]{1,0:T(8,128)}, u32[]{:S(2)}) copy-start(f32[128,256]{1,0:T(8,128)} %param.12) | copy-start | bytes 393220
  693.6 570.3 %all-reduce.3.cloned.1.call-start = ((), (), s32[]{:S(2)}) async-start(), calls=%async_computation.12 | async-start | bytes 1048576 | tf_op jit(solution)/shard_map/psum | solution.py:178
Sparse Core Ops, SparseCore 0:
  11.1 62.1 all-gather.2
  327.6 35.0 reduce-scatter.7
  365.5 41.8 reduce-scatter.5
  409.6 46.8 all-gather.4
  692.4 171.1 reduce-scatter.11
  866.0 32.3 reduce-scatter.13
  902.4 102.6 reduce-scatter.9
  1012.1 251.8 all-reduce.2
where the time goes:
time: 1280 us; the launch traced here: 1270 us
  waiting for transfers between devices  611 us (48%)
  blocking collectives  220 us (17%)
  local copies, waits for them, and re-layouts  118 us (9%)
  matrix products  108 us (8%)
  other arithmetic  107 us (8%)
  loops' own time  95.1 us (7%)
  between operations  14.4 us (1%)
    psum x1, waiting for transfers between devices, shards(): lax.psum((grad_proj, grad_att_src, grad_att_dst), ('dst', 'src'))  177 us
    reduce_scatter x1, waiting for transfers between devices, shards(): lax.psum_scatter(d_src, 'dst', scatter_dimension=0, tiled=True)  169 us
    reduce_scatter x1, waiting for transfers between devices, shards(): lax.psum_scatter(d_hsrc, 'dst', scatter_dimension=0, tiled=True)  106 us
    pmax x1, blocking collectives, shards(): full_max = lax.pmax(row_max, 'src')  81.9 us
    psum x1, blocking collectives, shards(): lax.psum((grad_proj, grad_att_src, grad_att_dst), ('dst', 'src'))  77.3 us
    another operation x1, loops' own time, shards(): lax.fori_loop(0, live_count, backward_step, start_grads)  47.7 us
    another operation x1, loops' own time, shards(): lax.fori_loop(0, live_count, forward_step, (row_max, row_sum, row_acc))  47.4 us
    reduce_scatter x1, waiting for transfers between devices, shards(): lax.psum_scatter(shifted_acc, 'src', scatter_dimension=0, tiled=True)  44.6 us
  transfers between devices with their start and end apart: 8, of which 8 were waited for; matrix products, arithmetic and copies ran while one was open for 1% of the time, Pallas kernels for 0%

commit v1 on v0

v1 whole, which is shorter than its diff:
```python
import functools

import jax
import jax.numpy as jnp
from jax import lax
from jax.experimental import pallas as pl
from jax.experimental.pallas import tpu as pltpu
from jax.sharding import PartitionSpec as P

HIGHEST = lax.Precision.HIGHEST
F32 = jnp.float32
BF16 = jnp.bfloat16
LOG2E = 1.4426950408889634
NEG = -1e30
MESH = pl.DeviceIdType.MESH
VMEM = pl.BlockSpec(memory_space=pltpu.VMEM)
SMEM = pl.BlockSpec(memory_space=pltpu.SMEM)
ANY = pl.BlockSpec(memory_space=pl.ANY)
NN = (((1,), (0,)), ((), ()))
NT = (((1,), (1,)), ((), ()))
BIG_VMEM = 60 * 1024 * 1024


def dot(a, b, dims=NN, precision=None):
    return lax.dot_general(a, b, dims, precision=precision, preferred_element_type=F32)


def split(value):
    high = value.astype(BF16)
    return high, (value - high.astype(F32)).astype(BF16)


def leaky(raw):
    return jnp.maximum(raw, 0.2 * raw)


def per_head_rows(att):
    wide = jnp.concatenate([att] * 8, axis=1)
    head = lax.broadcasted_iota(jnp.int32, wide.shape, 0)
    column = lax.broadcasted_iota(jnp.int32, wide.shape, 1)
    return jnp.where(column // 64 == head, wide, 0.0)


def score_rows(att, proj):
    return dot(per_head_rows(att), proj, NT, HIGHEST)


def lanes(shape):
    return lax.broadcasted_iota(jnp.int32, shape, len(shape) - 1)


def place():
    d = lax.axis_index("dst")
    z = lax.axis_index("src")
    return d, d // 8, lax.rem(d // 2, 4), lax.rem(d, 2), z


def node(y, x, k):
    return lax.rem(y + 8, 4) * 8 + lax.rem(x + 8, 4) * 2 + k


class Links:
    def __init__(self, send, recv):
        self.send, self.recv, self.used, self.open = send, recv, 0, []

    def push(self, source, landing, **target):
        copy = pltpu.make_async_remote_copy(
            src_ref=source,
            dst_ref=landing,
            send_sem=self.send.at[self.used],
            recv_sem=self.recv.at[self.used],
            device_id=target,
            device_id_type=MESH,
        )
        self.used += 1
        copy.start()
        self.open.append(copy)
        return copy

    def drain(self):
        for copy in self.open:
            copy.wait_send()


def greet(dsts, srcs):
    barrier = pltpu.get_barrier_semaphore()
    for other in dsts:
        pl.semaphore_signal(barrier, inc=1, device_id={"dst": other}, device_id_type=MESH)
    for other in srcs:
        pl.semaphore_signal(barrier, inc=1, device_id={"src": other}, device_id_type=MESH)
    return lambda: pl.semaphore_wait(barrier, len(dsts) + len(srcs))


def run_chains(chains):
    chains = list(chains)
    while chains:
        for chain in list(chains):
            try:
                next(chain)
            except StopIteration:
                chains.remove(chain)


def gather_body(x_ref, p_ref, att_ref, panel_ref, a_ref, send, recv, own_sem):
    d, y, x, k, z = place()
    sibling = node(y, x, 1 - k)
    wait_all = greet(
        [sibling, node(y + 1, x, k), node(y - 1, x, k), node(y, x + 1, k), node(y, x - 1, k)],
        [lax.rem(z + s, 8) for s in range(1, 8)],
    )
    own_copy = pltpu.make_async_copy(x_ref, panel_ref.at[d], own_sem)
    own_copy.start()
    rows = score_rows(att_ref[...], p_ref[...]) * LOG2E
    a_ref[z] = dot(rows, x_ref[...], NT, HIGHEST)
    wait_all()
    links = Links(send, recv)

    def chain(half):
        def at(u, v):
            return node(y + v, x + u, k) if half == 0 else node(y + u, x + v, k)

        def region(u, v, quarter=None):
            if quarter is None:
                return panel_ref.at[at(u, v), pl.ds(64 * half, 64)]
            return panel_ref.at[at(u, v), pl.ds(64 * half + 32 * quarter, 32)]

        def to(part, du, dv, src=None):
            return links.push(part if src is None else src, part, dst=at(du, dv))

        def twin(u, v, src=None):
            part = region(u, v)
            return links.push(part if src is None else src, part, dst=sibling)

        own = x_ref.at[pl.ds(64 * half, 64)]
        first = [to(region(0, 0), 1, 0, own), to(region(0, 0), -1, 0, own)]
        second = {0: [to(region(0, 0), 0, 1, own), to(region(0, 0), 0, -1, own)]}
        twins = [twin(0, 0, own)]
        last = {}

        def spread(u):
            second[u] = [to(region(u, 0), 0, 1), to(region(u, 0), 0, -1)]
            twins.append(twin(u, 0))

        def relay(u):
            pair = []
            for index, v in ((0, -1), (1, 1)):
                yield
                second[u][index].wait_recv()
                pair.append(to(region(u, v, index), 0, -v))
                twins.append(twin(u, v))
            last[u] = pair

        def finish(u):
            yield
            for copy in last[u]:
                copy.wait_recv()
            twins.append(twin(u, 2))

        far = []
        for index, u in ((0, -1), (1, 1)):
            yield
            first[index].wait_recv()
            far.append(to(region(u, 0, index), -u, 0))
            spread(u)
        yield from relay(0)
        yield
        for copy in far:
            copy.wait_recv()
        spread(2)
        yield from relay(-1)
        yield from relay(1)
        yield from finish(0)
        yield from relay(2)
        yield from finish(-1)
        yield from finish(1)
        yield from finish(2)
        yield
        for copy in twins:
            copy.wait_recv()

    scores = [
        links.push(a_ref.at[z], a_ref.at[z], src=lax.rem(z + s, 8)) for s in range(1, 8)
    ]
    run_chains([chain(0), chain(1)])
    for copy in scores:
        copy.wait_recv()
    own_copy.wait()
    links.drain()


def gather_inputs(x, proj, att_dst):
    count = 72 + 7
    return pl.pallas_call(
        gather_body,
        out_shape=(
            jax.ShapeDtypeStruct((32, 128, 256), F32),
            jax.ShapeDtypeStruct((8, 8, 128), F32),
        ),
        in_specs=[VMEM] * 3,
        out_specs=(ANY, VMEM),
        scratch_shapes=[
            pltpu.SemaphoreType.DMA((count,)),
            pltpu.SemaphoreType.DMA((count,)),
            pltpu.SemaphoreType.DMA,
        ],
        compiler_params=pltpu.CompilerParams(collective_id=0, has_side_effects=True),
    )(x, proj, att_dst)


def prepare_features(x_ref, p_ref, p_cat, hb, extra):
    high, low = split(p_ref[...])
    p_cat[0:256] = high
    p_cat[256:512] = low
    p_cat[512:768] = high
    even = (lanes((1, 128)) < 64).astype(BF16)
    odd = (lanes((1, 128)) >= 64).astype(BF16)

    def step(c, carry):
        xc = x_ref[c]
        x_high, x_low = split(xc)
        h = dot(jnp.concatenate([x_high, x_high, x_low], axis=1), p_cat[...])
        h_high, h_low = split(h)
        for pair in range(4):
            cols = slice(128 * pair, 128 * pair + 128)
            hb[c, pair, 0:128] = h_high[:, cols] * even
            hb[c, pair, 128:256] = h_high[:, cols] * odd
            hb[c, pair, 256:384] = h_low[:, cols] * even
            hb[c, pair, 384:512] = h_low[:, cols] * odd
        extra(c, xc)
        return carry

    lax.fori_loop(0, 32, step, 0)


def columns_of(rows):
    pad = jnp.zeros((128 - rows.shape[0], 128), F32)
    return jnp.concatenate([rows, pad], axis=0).T


def forward_body(
    blocks, counts, x_ref, p_ref, att_ref, a_ref, mask_ref, acc_out, b_out, p_cat, hb, top, abc, sums, acc
):
    rows = score_rows(att_ref[...], p_ref[...]) * LOG2E

    def extra(c, xc):
        b_out[c] = dot(rows, xc, NT, HIGHEST)

    prepare_features(x_ref, p_ref, p_cat, hb, extra)
    top[...] = jnp.full(top.shape, NEG, F32)
    sums[...] = jnp.zeros(sums.shape, F32)
    acc[...] = jnp.zeros(acc.shape, F32)
    live = counts[0]

    def find_top(k, carry):
        b, c = blocks[k, 0], blocks[k, 1]
        keep = mask_ref[k] > 0
        scores = b_out[c]
        for h in range(8):
            top[b * 8 + h] = jnp.maximum(top[b * 8 + h], jnp.where(keep, scores[h : h + 1], NEG))
        return carry

    lax.fori_loop(0, live, find_top, 0)

    def spread_top(b, carry):
        a_cols = columns_of(a_ref[b])
        for h in range(8):
            a_col = a_cols[:, h : h + 1]
            best = jnp.max(top[b * 8 + h], axis=1, keepdims=True)
            top[b * 8 + h] = jnp.broadcast_to(leaky(a_col + best), (128, 128))
            abc[b * 8 + h] = jnp.broadcast_to(a_col, (128, 128))
        return carry

    lax.fori_loop(0, 8, spread_top, 0)

    def accumulate(k, carry):
        b, c = blocks[k, 0], blocks[k, 1]
        keep = mask_ref[k] > 0
        scores = b_out[c]
        for pair in range(4):
            highs, lows = [], []
            for h in (2 * pair, 2 * pair + 1):
                raw = abc[b * 8 + h] + jnp.where(keep, scores[h : h + 1], NEG)
                w = jnp.exp2(leaky(raw) - top[b * 8 + h])
                sums[b * 8 + h] += w
                high, low = split(w)
                highs.append(high)
                lows.append(low)
            left = jnp.concatenate(highs + highs + lows, axis=1)
            right = jnp.concatenate([hb[c, pair], hb[c, pair, 0:256]], axis=0)
            acc[b * 4 + pair] += dot(left, right)
        return carry

    lax.fori_loop(0, live, accumulate, 0)

    def pack(b, carry):
        lane = lanes((128, 128))
        stats = [jnp.zeros((128, 128), F32)] * 2
        for h in range(8):
            way, h4 = h // 4, h % 4
            total = jnp.sum(sums[b * 8 + h], axis=1, keepdims=True)
            stats[way] = jnp.where(lane == h4, top[b * 8 + h], stats[way])
            stats[way] = jnp.where(lane == h4 + 4, total, stats[way])
        for way in range(2):
            packed = stats[way].T[0:8]
            for sub in range(2):
                span = slice(64 * sub, 64 * sub + 64)
                acc_out[b, way, sub, 0:64, 0:128] = acc[b * 4 + 2 * way][span]
                acc_out[b, way, sub, 0:64, 128:256] = acc[b * 4 + 2 * way + 1][span]
                acc_out[b, way, sub, 64:72, 0:128] = packed
                acc_out[b, way, sub, 64:72, 128:256] = jnp.zeros((8, 128), F32)
        return carry

    lax.fori_loop(0, 8, pack, 0)


def forward_local(blocks, counts, panel, proj, att_src, a, masks):
    return pl.pallas_call(
        forward_body,
        out_shape=(
            jax.ShapeDtypeStruct((8, 2, 2, 72, 256), F32),
            jax.ShapeDtypeStruct((32, 8, 128), F32),
        ),
        in_specs=[SMEM, SMEM] + [VMEM] * 5,
        out_specs=(VMEM, VMEM),
        scratch_shapes=[
            pltpu.VMEM((768, 512), BF16),
            pltpu.VMEM((32, 4, 512, 128), BF16),
            pltpu.VMEM((64, 128, 128), F32),
            pltpu.VMEM((64, 128, 128), F32),
            pltpu.VMEM((64, 128, 128), F32),
            pltpu.VMEM((32, 128, 128), F32),
        ],
        compiler_params=pltpu.CompilerParams(vmem_limit_bytes=BIG_VMEM),
    )(blocks, counts, panel, proj, att_src, a, masks)


def merge(arrived, mine, sub):
    one, two = arrived[64:72, 0:128], mine[64:72, 0:128]
    best = jnp.maximum(one[0:4], two[0:4])
    f_one, f_two = jnp.exp2(one[0:4] - best), jnp.exp2(two[0:4] - best)
    total = one[4:8] * f_one + two[4:8] * f_two
    cols = columns_of(jnp.concatenate([f_one, f_two], axis=0))[64 * sub : 64 * sub + 64]
    lane = lanes((64, 128))
    tiles = []
    for pair in range(2):
        span = slice(128 * pair, 128 * pair + 128)
        factor = [
            jnp.where(lane < 64, cols[:, s + 2 * pair : s + 2 * pair + 1], cols[:, s + 2 * pair + 1 : s + 2 * pair + 2])
            for s in (0, 4)
        ]
        tiles.append(arrived[0:64, span] * factor[0] + mine[0:64, span] * factor[1])
    return jnp.concatenate(tiles, axis=1), jnp.concatenate([best, total], axis=0)


def sum_body(acc_ref, out_ref, slots, send, recv):
    z = lax.axis_index("src")
    right, left = lax.rem(z + 1, 8), lax.rem(z + 7, 8)
    greet([], [right, left])()

    def copy(step, way, sub):
        if isinstance(step, int) and step == 0:
            src = acc_ref.at[left if way == 0 else right, way, sub]
        else:
            src = slots.at[step - 1, way, sub]
        return pltpu.make_async_remote_copy(
            src_ref=src,
            dst_ref=slots.at[step, way, sub],
            send_sem=send.at[step, way, sub],
            recv_sem=recv.at[step, way, sub],
            device_id={"src": right if way == 0 else left},
            device_id_type=MESH,
        )

    order = [(way, sub) for sub in range(2) for way in range(2)]
    for way, sub in order:
        copy(0, way, sub).start()

    def block_of(step, way):
        return lax.rem(z + 15 - step, 8) if way == 0 else lax.rem(z + 1 + step, 8)

    def hop(step, carry):
        for way, sub in order:
            pltpu.make_async_remote_copy(
                src_ref=slots.at[step - 1, way, sub],
                dst_ref=slots.at[step - 1, way, sub],
                send_sem=send.at[step - 1, way, sub],
                recv_sem=recv.at[step - 1, way, sub],
                device_id={"src": right if way == 0 else left},
                device_id_type=MESH,
            ).wait_recv()
            values, stats = merge(slots[step - 1, way, sub], acc_ref[block_of(step, way), way, sub], sub)
            slots[step - 1, way, sub, 0:64] = values
            slots[step - 1, way, sub, 64:72, 0:128] = stats
            copy(step, way, sub).start()
        return carry

    lax.fori_loop(1, 7, hop, 0)
    for way, sub in order:
        last = copy(6, way, sub)
        last.wait_recv()
        values, stats = merge(slots[6, way, sub], acc_ref[z, way, sub], sub)
        out_ref[way, sub, 0:64] = values
        out_ref[way, sub, 64:72, 0:128] = stats
        out_ref[way, sub, 64:72, 128:256] = jnp.zeros((8, 128), F32)
    for step in range(7):
        for way, sub in order:
            copy(step, way, sub).wait_send()


def sum_over_src(acc):
    return pl.pallas_call(
        sum_body,
        out_shape=jax.ShapeDtypeStruct((2, 2, 72, 256), F32),
        in_specs=[VMEM],
        out_specs=VMEM,
        scratch_shapes=[
            pltpu.VMEM((7, 2, 2, 72, 256), F32),
            pltpu.SemaphoreType.DMA((7, 2, 2)),
            pltpu.SemaphoreType.DMA((7, 2, 2)),
        ],
        compiler_params=pltpu.CompilerParams(collective_id=1, has_side_effects=True),
    )(acc)


def minus_one(power):
    series = power * (1 + power * (1 / 2 + power * (1 / 6 + power * (1 / 24 + power * (1 / 120)))))
    return jnp.where(power > -0.1, series, jnp.exp(power) - 1)


def owner_body(total_ref, x_ref, p_ref, att_ref, a_ref, cot_ref, out_ref, pay_ref, self_ref, dself_ref):
    proj = p_ref[...]
    h_own = dot(x_ref[...], proj, NN, HIGHEST)
    rows = score_rows(att_ref[...], proj) * LOG2E
    raw = a_ref[...] + dot(rows, x_ref[...], NT, HIGHEST)
    own = leaky(raw)
    parts = [total_ref[way, 0, 64:72, 0:128] for way in range(2)]
    tops = jnp.concatenate([part[0:4] for part in parts], axis=0)
    sums = jnp.concatenate([part[4:8] for part in parts], axis=0)
    best = jnp.maximum(tops, own)
    f_tot, f_own = jnp.exp2(tops - best), jnp.exp2(own - best)
    inverse = 1.0 / (sums * f_tot + f_own)
    slope = jnp.where(raw > 0, 1.0, 0.2)
    cols = columns_of(jnp.concatenate([f_tot * inverse, f_own * inverse, inverse, slope], axis=0))
    lane = lanes((128, 128))
    stats = jnp.zeros((128, 128), F32)
    for pair in range(4):
        way, inner = pair // 2, pair % 2
        span = slice(128 * pair, 128 * pair + 128)
        local = slice(128 * inner, 128 * inner + 128)
        acc = jnp.concatenate([total_ref[way, sub, 0:64, local] for sub in range(2)], axis=0)

        def wide(kind):
            s = 8 * kind + 2 * pair
            return jnp.where(lane < 64, cols[:, s : s + 1], cols[:, s + 1 : s + 2])

        alpha, h_pair = wide(1), h_own[:, span]
        agg = acc * wide(0) + h_pair * alpha
        low = jnp.minimum(agg, 0.0)
        out_ref[:, span] = jnp.where(agg > 0, agg, minus_one(low))
        grad = cot_ref[:, span] * jnp.where(agg > 0, 1.0, jnp.exp(low))
        pay_ref[0:128, span] = grad * wide(2)
        self_ref[span] = (grad * alpha).T
        for odd in range(2):
            h = 2 * pair + odd
            mine = lane >= 64 if odd else lane < 64
            row_dot = jnp.sum(jnp.where(mine, grad * agg, 0.0), axis=1, keepdims=True)
            d_alpha = jnp.sum(jnp.where(mine, grad * h_pair, 0.0), axis=1, keepdims=True)
            d_self = cols[:, 8 + h : 9 + h] * (d_alpha - row_dot) * cols[:, 24 + h : 25 + h]
            stats = jnp.where(lane == h, row_dot * cols[:, 16 + h : 17 + h], stats)
            stats = jnp.where(lane == 8 + h, d_self, stats)
    turned = stats.T
    pay_ref[128:136, 0:128] = best
    pay_ref[128:136, 128:256] = turned[0:8]
    pay_ref[128:136, 256:512] = jnp.zeros((8, 256), F32)
    dself_ref[...] = turned[8:16]


def owner_rows(total, x, proj, att_src, a_own, cotangent):
    return pl.pallas_call(
        owner_body,
        out_shape=(
            jax.ShapeDtypeStruct((128, 512), F32),
            jax.ShapeDtypeStruct((136, 512), F32),
            jax.ShapeDtypeStruct((512, 128), F32),
            jax.ShapeDtypeStruct((8, 128), F32),
        ),
        in_specs=[VMEM] * 6,
        out_specs=(VMEM,) * 4,
    )(total, x, proj, att_src, a_own, cotangent)


def grads_body(pay_ref, all_ref, send, recv, own_sem):
    z = lax.axis_index("src")
    right, left = lax.rem(z + 1, 8), lax.rem(z + 7, 8)
    wait_all = greet([], [right, left])
    own_copy = pltpu.make_async_copy(pay_ref, all_ref.at[z], own_sem)
    own_copy.start()
    wait_all()
    links = Links(send, recv)
    spans = (pl.ds(0, 64), pl.ds(64, 72))

    def push(step, way, sub):
        block = lax.rem(z + 8 - step, 8) if way == 0 else lax.rem(z + step, 8)
        part = all_ref.at[block, spans[sub]]
        src = pay_ref.at[spans[sub]] if step == 0 else part
        return links.push(src, part, src=right if way == 0 else left)

    order = [(way, sub) for sub in range(2) for way in range(2)]
    coming = {item: push(0, *item) for item in order}
    for step in range(1, 4):
        for item in order:
            coming[item].wait_recv()
            if step < 3 or item[0] == item[1]:
                coming[item] = push(step, *item)
            else:
                del coming[item]
    for copy in coming.values():
        copy.wait_recv()
    own_copy.wait()
    links.drain()


def gather_grads(pay):
    return pl.pallas_call(
        grads_body,
        out_shape=jax.ShapeDtypeStruct((8, 136, 512), F32),
        in_specs=[VMEM],
        out_specs=ANY,
        scratch_shapes=[
            pltpu.SemaphoreType.DMA((14,)),
            pltpu.SemaphoreType.DMA((14,)),
            pltpu.SemaphoreType.DMA,
        ],
        compiler_params=pltpu.CompilerParams(collective_id=2, has_side_effects=True),
    )(pay)


def backward_body(
    blocks, counts, spot, x_ref, p_ref, a_ref, b_ref, mask_ref, pay_ref, self_ref, dself_ref,
    dh_out, dsrc_out, ddst_out, p_cat, hb, gn, gt, top, abc, dots, ddst, dsrc,
):
    prepare_features(x_ref, p_ref, p_cat, hb, lambda c, xc: None)
    even = (lax.broadcasted_iota(jnp.int32, (128, 1), 0) < 64).astype(F32)
    odd = 1.0 - even

    def setup(b, carry):
        cols = columns_of(
            jnp.concatenate([a_ref[b], pay_ref[b, 128:136, 0:128], pay_ref[b, 128:136, 128:256]], axis=0)
        )
        dots[b] = cols
        for h in range(8):
            abc[b * 8 + h] = jnp.broadcast_to(cols[:, h : h + 1], (128, 128))
            top[b * 8 + h] = jnp.broadcast_to(cols[:, 8 + h : 9 + h], (128, 128))
        for pair in range(4):
            grad = pay_ref[b, 0:128, 128 * pair : 128 * pair + 128]
            high, low = split(grad)
            gn[b, pair, :, 0:128] = high
            gn[b, pair, :, 128:256] = low
            turned = grad.T
            e_high, e_low = split(turned * even)
            o_high, o_low = split(turned * odd)
            gt[b, pair, :, 0:128] = e_high
            gt[b, pair, :, 128:256] = o_high
            gt[b, pair, :, 256:384] = e_low
            gt[b, pair, :, 384:512] = o_low
        return carry

    lax.fori_loop(0, 8, setup, 0)
    ddst[...] = jnp.zeros(ddst.shape, F32)
    dsrc[...] = jnp.zeros(dsrc.shape, F32)
    dh_out[...] = jnp.zeros(dh_out.shape, F32)
    dh_out[spot[0]] = self_ref[...]

    def step(k, carry):
        b, c = blocks[k, 0], blocks[k, 1]
        keep = mask_ref[k] > 0
        scores = b_ref[c]
        cols = dots[b]
        for pair in range(4):
            g_high, g_low = gn[b, pair, :, 0:128], gn[b, pair, :, 128:256]
            h_high, h_low = hb[c, pair, 0:256], hb[c, pair, 256:512]
            d_alpha = dot(
                jnp.concatenate([g_high, g_high, g_low], axis=1),
                jnp.concatenate([h_high, h_low, h_high], axis=1),
                NT,
            )
            highs, lows = [], []
            for side in range(2):
                h = 2 * pair + side
                raw = abc[b * 8 + h] + jnp.where(keep, scores[h : h + 1], NEG)
                w = jnp.exp2(leaky(raw) - top[b * 8 + h])
                d_raw = w * (d_alpha[:, 128 * side : 128 * side + 128] - cols[:, 16 + h : 17 + h])
                d_raw = jnp.where(raw > 0, d_raw, 0.2 * d_raw)
                ddst[b * 8 + h] += d_raw
                dsrc[c * 8 + h] += jnp.sum(d_raw.reshape(16, 8, 128), axis=0)
                high, low = split(w)
                highs.append(high)
                lows.append(low)
            left = jnp.concatenate([gt[b, pair], gt[b, pair, :, 0:256]], axis=1)
            right = jnp.concatenate(highs + highs + lows, axis=0)
            dh_out[c, 128 * pair : 128 * pair + 128] += dot(left, right)
        return carry

    lax.fori_loop(0, counts[0], step, 0)

    def pack_dst(b, carry):
        lane = lanes((128, 128))
        packed = jnp.zeros((128, 128), F32)
        for h in range(8):
            packed = jnp.where(lane == h, jnp.sum(ddst[b * 8 + h], axis=1, keepdims=True), packed)
        ddst_out[b] = packed.T[0:8]
        return carry

    lax.fori_loop(0, 8, pack_dst, 0)
    ddst_out[spot[1]] += dself_ref[...]

    def pack_src(c, carry):
        dsrc_out[c] = jnp.concatenate(
            [jnp.sum(dsrc[c * 8 + h], axis=0, keepdims=True) for h in range(8)], axis=0
        )
        return carry

    lax.fori_loop(0, 32, pack_src, 0)
    dsrc_out[spot[0]] += dself_ref[...]


def backward_local(blocks, counts, spot, panel, proj, a, b, masks, pays, dh_self, d_self):
    return pl.pallas_call(
        backward_body,
        out_shape=(
            jax.ShapeDtypeStruct((32, 512, 128), F32),
            jax.ShapeDtypeStruct((32, 8, 128), F32),
            jax.ShapeDtypeStruct((8, 8, 128), F32),
        ),
        in_specs=[SMEM] * 3 + [VMEM] * 8,
        out_specs=(VMEM,) * 3,
        scratch_shapes=[
            pltpu.VMEM((768, 512), BF16),
            pltpu.VMEM((32, 4, 512, 128), BF16),
            pltpu.VMEM((8, 4, 128, 256), BF16),
            pltpu.VMEM((8, 4, 128, 512), BF16),
            pltpu.VMEM((64, 128, 128), F32),
            pltpu.VMEM((64, 128, 128), F32),
            pltpu.VMEM((8, 128, 128), F32),
            pltpu.VMEM((64, 128, 128), F32),
            pltpu.VMEM((256, 8, 128), F32),
        ],
        compiler_params=pltpu.CompilerParams(vmem_limit_bytes=BIG_VMEM),
    )(blocks, counts, spot, panel, proj, a, b, masks, pays, dh_self, d_self)


def project_body(dh_ref, dsrc_ref, x_ref, p_ref, att_ref, dx_ref, dp_ref, v_ref, p_cat, rows_t):
    @pl.when(pl.program_id(0) == 0)
    def _():
        proj = p_ref[...]
        high, low = split(proj)
        p_cat[:, 0:512] = high
        p_cat[:, 512:1024] = low
        p_cat[:, 1024:1536] = high
        rows = jnp.concatenate([score_rows(att_ref[...], proj), jnp.zeros((120, 256), F32)], axis=0)
        rows_t[...] = rows.T
        dp_ref[...] = jnp.zeros(dp_ref.shape, F32)
        v_ref[...] = jnp.zeros(v_ref.shape, F32)

    for s in range(dh_ref.shape[0]):
        x, d_src = x_ref[s], dsrc_ref[s]
        dh_high, dh_low = split(dh_ref[s])
        x_high, x_low = split(x)
        wide_src = jnp.concatenate([d_src, jnp.zeros((120, 128), F32)], axis=0)
        dx_ref[s] = dot(p_cat[...], jnp.concatenate([dh_high, dh_high, dh_low], axis=0)) + dot(
            rows_t[...], wide_src, NN, HIGHEST
        )
        dp_ref[...] += dot(
            jnp.concatenate([dh_high, dh_high, dh_low], axis=1), jnp.concatenate([x_high, x_low, x_high], axis=0)
        )
        v_ref[...] += dot(d_src, x, NN, HIGHEST)


def project_grads(dh, dsrc, panel, proj, att_src):
    n = 4
    return pl.pallas_call(
        project_body,
        grid=(32 // n,),
        out_shape=(
            jax.ShapeDtypeStruct((32, 256, 128), F32),
            jax.ShapeDtypeStruct((512, 256), F32),
            jax.ShapeDtypeStruct((8, 256), F32),
        ),
        in_specs=[
            pl.BlockSpec((n, 512, 128), lambda i: (i, 0, 0)),
            pl.BlockSpec((n, 8, 128), lambda i: (i, 0, 0)),
            pl.BlockSpec((n, 128, 256), lambda i: (i, 0, 0)),
            VMEM,
            VMEM,
        ],
        out_specs=(
            pl.BlockSpec((n, 256, 128), lambda i: (i, 0, 0)),
            pl.BlockSpec((512, 256), lambda i: (0, 0)),
            pl.BlockSpec((8, 256), lambda i: (0, 0)),
        ),
        scratch_shapes=[pltpu.VMEM((256, 1536), BF16), pltpu.VMEM((256, 128), F32)],
        compiler_params=pltpu.CompilerParams(vmem_limit_bytes=BIG_VMEM),
    )(dh, dsrc, panel, proj, att_src)


def reduce_body(
    dx_ref, dp_ref, v_ref, ddst_ref, x_ref, dx_out, dp_out, dst_out,
    send, recv, twin_dx, total, far, near, far2, near2, dst_all, pay, twin_pay, merged, plane, joined, tower,
):
    d, y, x, k, z = place()
    sibling = node(y, x, 1 - k)
    chip = y * 4 + x
    offsets = [(dy, dx) for dy in range(4) for dx in range(4) if (dy, dx) != (0, 0)]
    others = [lax.rem(z + s, 8) for s in range(1, 8)]
    wait_all = greet([sibling] + [node(y + dy, x + dx, k) for dy, dx in offsets], others)
    links = Links(send, recv)
    wait_all()

    dst_copies = [links.push(ddst_ref.at[t], dst_all.at[z], src=t) for t in others]

    def rank(offset):
        return 0 if 2 in offset else (2 if offset == (0, 0) else 1)

    cells = sorted([(0, 0)] + offsets, key=rank)
    twin_copies = {}
    for dy, dx in cells:
        yy, xx = lax.rem(y + dy, 4), lax.rem(x + dx, 4)
        twin_copies[dy, dx] = links.push(dx_ref.at[yy, xx, 1 - k], twin_dx.at[yy, xx], dst=sibling)

    def ring(region, plus, minus, far_buf, near_buf):
        c0 = links.push(region(2, 0), far_buf.at[0], dst=plus)
        c1 = links.push(region(2, 1), far_buf.at[1], dst=minus)
        c2 = links.push(region(1, 1), near_buf.at[0], dst=plus)
        c3 = links.push(region(-1, 0), near_buf.at[1], dst=minus)
        yield
        c0.wait_recv()
        part = region(1, 0)
        part[...] += far_buf[0]
        c4 = links.push(part, near_buf.at[2], dst=plus)
        yield
        c1.wait_recv()
        part = region(-1, 1)
        part[...] += far_buf[1]
        c5 = links.push(part, near_buf.at[3], dst=minus)
        for copy, index, piece in ((c2, 0, 1), (c3, 1, 0), (c4, 2, 0), (c5, 3, 1)):
            yield
            copy.wait_recv()
            part = region(0, piece)
            part[...] += near_buf[index]

    def grads(half):
        rows = pl.ds(128 * half, 128)

        def wide(v, piece):
            if half == 0:
                return total.at[lax.rem(y + v + 4, 4), pl.ds(2 * piece, 2), rows]
            return total.at[pl.ds(2 * piece, 2), lax.rem(x + v + 4, 4), rows]

        def narrow(u, piece):
            span = pl.ds(128 * half + 64 * piece, 64)
            if half == 0:
                return total.at[y, lax.rem(x + u + 4, 4), span]
            return total.at[lax.rem(y + u + 4, 4), x, span]

        along_y = (node(y + 1, x, k), node(y - 1, x, k))
        along_x = (node(y, x + 1, k), node(y, x - 1, k))
        first, then = (along_y, along_x) if half == 0 else (along_x, along_y)
        yield from ring(wide, *first, far.at[half], near.at[half])
        yield from ring(narrow, *then, far2.at[half], near2.at[half])

    def weights():
        for i in range(32):
            pay[i // 2, i % 2, 0:16] = dp_ref[16 * i : 16 * i + 16, 0:128]
            pay[i // 2, i % 2, 16:32] = dp_ref[16 * i : 16 * i + 16, 128:256]
            pay[i // 2, i % 2, 32:40] = jnp.zeros((8, 128), F32)
        for h in range(8):
            for side in range(2):
                i = 8 + h + 16 * side
                pay[i // 2, i % 2, 32:33] = v_ref[h : h + 1, 128 * side : 128 * side + 128]
        yield
        for copy in dst_copies:
            copy.wait_recv()
        dst_all[z] = ddst_ref[z]
        dst_total = dst_all[0]
        for t in range(1, 8):
            dst_total = dst_total + dst_all[t]
        dst_out[...] = dst_total
        u = dot(dst_total, x_ref[...], NN, HIGHEST)
        for h in range(8):
            for side in range(2):
                i = h + 16 * side
                pay[i // 2, i % 2, 32:33] = u[h : h + 1, 128 * side : 128 * side + 128]
        over = links.push(pay.at[:, 1 - k], twin_pay, dst=sibling)
        yield
        over.wait_recv()
        merged[...] = pay[:, k] + twin_pay[...]
        coming = []
        for dy, dx in offsets:
            target = lax.rem(y + dy, 4) * 4 + lax.rem(x + dx, 4)
            coming.append(links.push(merged.at[target], plane.at[chip], dst=node(y + dy, x + dx, k)))
        plane[chip] = merged[chip]
        yield
        for copy in coming:
            copy.wait_recv()
        value = plane[0]
        for i in range(1, 16):
            value = value + plane[i]
        joined[...] = value
        tower[z] = value
        coming = [links.push(joined, tower.at[z], src=t) for t in others]
        yield
        for copy in coming:
            copy.wait_recv()
        value = tower[0]
        for i in range(1, 8):
            value = value + tower[i]
        dp_out[chip, k] = value
        coming = [
            links.push(dp_out.at[chip, k], dp_out.at[chip, k], dst=node(y + dy, x + dx, k)) for dy, dx in offsets
        ]
        yield
        for copy in coming:
            copy.wait_recv()
        over = links.push(dp_out.at[:, k], dp_out.at[:, k], dst=sibling)
        yield
        over.wait_recv()

    small = weights()
    next(small)
    for dy, dx in cells:
        yy, xx = lax.rem(y + dy, 4), lax.rem(x + dx, 4)
        twin_copies[dy, dx].wait_recv()
        total[yy, xx] = dx_ref[yy, xx, k] + twin_dx[yy, xx]
    run_chains([grads(0), grads(1), small])
    dx_out[...] = total[y, x]
    links.drain()


def reduce_grads(dx, dp, v, ddst, x):
    count = 7 + 16 + 24 + 1 + 15 + 7 + 15 + 1
    return pl.pallas_call(
        reduce_body,
        out_shape=(
            jax.ShapeDtypeStruct((256, 128), F32),
            jax.ShapeDtypeStruct((16, 2, 40, 128), F32),
            jax.ShapeDtypeStruct((8, 128), F32),
        ),
        in_specs=[VMEM] * 5,
        out_specs=(VMEM,) * 3,
        scratch_shapes=[
            pltpu.SemaphoreType.DMA((count,)),
            pltpu.SemaphoreType.DMA((count,)),
            pltpu.VMEM((4, 4, 256, 128), F32),
            pltpu.VMEM((4, 4, 256, 128), F32),
            pltpu.VMEM((2, 2, 2, 128, 128), F32),
            pltpu.VMEM((2, 4, 2, 128, 128), F32),
            pltpu.VMEM((2, 2, 64, 128), F32),
            pltpu.VMEM((2, 4, 64, 128), F32),
            pltpu.VMEM((8, 8, 128), F32),
            pltpu.VMEM((16, 2, 40, 128), F32),
            pltpu.VMEM((16, 40, 128), F32),
            pltpu.VMEM((16, 40, 128), F32),
            pltpu.VMEM((16, 40, 128), F32),
            pltpu.VMEM((40, 128), F32),
            pltpu.VMEM((8, 40, 128), F32),
        ],
        compiler_params=pltpu.CompilerParams(
            collective_id=3, has_side_effects=True, vmem_limit_bytes=BIG_VMEM
        ),
    )(dx.reshape(4, 4, 2, 256, 128), dp, v, ddst, x)


def finish_body(dx_ref, w_ref, dst_ref, p_ref, src_att_ref, dst_att_ref, in_ref, proj_ref, src_ref, dst_out):
    proj = p_ref[...]
    a_rows = per_head_rows(dst_att_ref[...])
    s_rows = per_head_rows(src_att_ref[...])
    score = dot(a_rows, proj, NT, HIGHEST)
    pad = jnp.zeros((120, 256), F32)
    score_t = jnp.concatenate([score, pad], axis=0).T
    dst_wide = jnp.concatenate([dst_ref[...], jnp.zeros((120, 128), F32)], axis=0)
    in_ref[...] = (dx_ref[...] + dot(score_t, dst_wide, NN, HIGHEST)).T

    def row(i):
        return jnp.concatenate([w_ref[i, 32:33], w_ref[i + 16, 32:33]], axis=1)

    u = jnp.concatenate([row(h) for h in range(8)], axis=0)
    v = jnp.concatenate([row(8 + h) for h in range(8)], axis=0)
    uv = jnp.concatenate([u, v, jnp.zeros((112, 256), F32)], axis=0)
    att = jnp.concatenate([a_rows, s_rows, jnp.zeros((112, 512), F32)], axis=0)
    grad_t = jnp.concatenate(
        [jnp.concatenate([w_ref[i, 0:16], w_ref[i, 16:32]], axis=1) for i in range(32)], axis=0
    )
    proj_ref[...] = (grad_t + dot(att.T, uv, NN, HIGHEST)).T
    both = dot(jnp.concatenate([u, v], axis=0), proj, NN, HIGHEST)
    dst_out[...] = jnp.concatenate([both[h : h + 1, 64 * h : 64 * h + 64] for h in range(8)], axis=0)
    src_ref[...] = jnp.concatenate([both[8 + h : 9 + h, 64 * h : 64 * h + 64] for h in range(8)], axis=0)


def finish(dx, weights, dst_total, proj, att_src, att_dst):
    return pl.pallas_call(
        finish_body,
        out_shape=(
            jax.ShapeDtypeStruct((128, 256), F32),
            jax.ShapeDtypeStruct((256, 512), F32),
            jax.ShapeDtypeStruct((8, 64), F32),
            jax.ShapeDtypeStruct((8, 64), F32),
        ),
        in_specs=[VMEM] * 6,
        out_specs=(VMEM,) * 4,
    )(dx, weights.reshape(32, 40, 128), dst_total, proj, att_src, att_dst)


def shards(inputs, projection, att_src, att_dst, blocks, counts, tile_masks, cotangent):
    coords = blocks[0, 0]
    live = counts.reshape(1)
    masks = tile_masks[0, 0]
    z = lax.axis_index("src")
    spot = jnp.stack([lax.axis_index("dst"), z]).astype(jnp.int32)
    panel, a = gather_inputs(inputs, projection, att_dst)
    acc, b = forward_local(coords, live, panel, projection, att_src, a, masks)
    total = sum_over_src(acc)
    a_own = lax.dynamic_index_in_dim(a, z, 0, keepdims=False)
    output, pay, dh_self, d_self = owner_rows(total, inputs, projection, att_src, a_own, cotangent)
    pays = gather_grads(pay)
    dh, dsrc, ddst = backward_local(
        coords, live, spot, panel, projection, a, b, masks, pays, dh_self, d_self
    )
    dx, dp, v = project_grads(dh, dsrc, panel, projection, att_src)
    dx_own, weights, dst_total = reduce_grads(dx, dp, v, ddst, inputs)
    in_grad, proj_grad, src_grad, dst_grad = finish(
        dx_own, weights, dst_total, projection, att_src, att_dst
    )
    return (output, in_grad, proj_grad, src_grad, dst_grad)


def solution(mesh):
    in_specs = (
        P(("dst", "src"), None),
        P(),
        P(),
        P(),
        P("dst", "src", None, None),
        P("dst", "src"),
        P("dst", "src", None, None, None),
        P(("dst", "src"), None),
    )
    out_specs = (P(("dst", "src"), None), P(("dst", "src"), None), P(), P(), P())
    return jax.shard_map(shards, mesh=mesh, in_specs=in_specs, out_specs=out_specs, check_vma=False)
```

time: 1280 us -> 260 us (0.20)
  waiting for transfers between devices: 611 us -> 0 us
  Pallas kernels: 0 us -> 255 us
  blocking collectives: 220 us -> 0 us
  local copies, waits for them, and re-layouts: 118 us -> 2.63 us
  matrix products: 108 us -> 0 us
  other arithmetic: 107 us -> 0.56 us
  loops' own time: 95.1 us -> 0 us
  between operations: 14.4 us -> 1.32 us
    reduce_scatter x5 -> x0, waiting for transfers between devices: 386 us -> none  [the longest x1 169 us: shards(): lax.psum_scatter(d_src, 'dst', scatter_dimension=0, tiled=True)]
    pallas_call x0 -> x9, Pallas kernels: none -> 255 us  [the longest x1 57.1 us: reduce_grads(): pl.pallas_call(reduce_body, out_shape=(jax.ShapeDtypeStruct((256, 128), F...]
    psum x1 -> x0, waiting for transfers between devices: 177 us -> none  [shards(): lax.psum((grad_proj, grad_att_src, grad_att_dst), ('dst', 'src'))]
    dot_general x77 -> x0, matrix products: 108 us -> none  [the longest x23 42.3 us: backward_step(): d_alpha = jnp.einsum('dhc,shc->hds', grad_tile, h_src, precision=HIGHEST)]
    dynamic_slice x115 -> x0, local copies, waits for them, and re-layouts: 95.2 us -> none  [the longest x46 27.2 us: tile_inputs(): src_start = coords[slot, 1] * tile_size]
    another operation x2 -> x0, loops' own time: 95.1 us -> none  [the longest x1 47.7 us: shards(): lax.fori_loop(0, live_count, backward_step, start_grads)]
    pmax x1 -> x0, blocking collectives: 81.9 us -> none  [shards(): full_max = lax.pmax(row_max, 'src')]
    psum x1 -> x0, blocking collectives: 77.3 us -> none  [shards(): lax.psum((grad_proj, grad_att_src, grad_att_dst), ('dst', 'src'))]
  transfers between devices with their start and end apart: 8 -> 0, of which waited for: 8 -> 0; matrix products, arithmetic and copies ran while one was open for 1% -> 0% of each run, Pallas kernels for 0% -> 0%
where the time goes in v1:
time: 260 us
  Pallas kernels  255 us (98%)
  local copies, waits for them, and re-layouts  2.63 us (1%)
    pallas_call x1, Pallas kernels, reduce_grads(): pl.pallas_call(reduce_body, out_shape=(jax.ShapeDtypeStruct((256, 128), F...  57.1 us
    pallas_call x1, Pallas kernels, backward_local(): pl.pallas_call(backward_body, out_shape=(jax.ShapeDtypeStruct((32, 512, 1...  40.6 us
    pallas_call x1, Pallas kernels, forward_local(): pl.pallas_call(forward_body, out_shape=(jax.ShapeDtypeStruct((8, 2, 2, 72...  39.5 us
    pallas_call x1, Pallas kernels, gather_inputs(): pl.pallas_call(gather_body, out_shape=(jax.ShapeDtypeStruct((32, 128, 256...  32.9 us
    pallas_call x1, Pallas kernels, sum_over_src(): pl.pallas_call(sum_body, out_shape=jax.ShapeDtypeStruct((2, 2, 72, 256),...  32.7 us
    pallas_call x1, Pallas kernels, gather_grads(): pl.pallas_call(grads_body, out_shape=jax.ShapeDtypeStruct((8, 136, 512),...  23.3 us
    pallas_call x1, Pallas kernels, project_grads(): pl.pallas_call(project_body, grid=(32 // n,), out_shape=(jax.ShapeDtypeSt...  20.2 us

profile of v1, /device:TPU:1, one launch (start us, length us, event | category | flops | bytes accessed | tf_op | source)
XLA Modules:
  0.0 259.9 jit_solution(3776322706671843185)
XLA Ops:
  1.3 0.6 pad_add_fusion.spot
  1.8 1.4 copy.13.blocks
  3.2 32.9 %shard_map.119 = (f32[32,128,256]{2,1,0:T(8,128)}, f32[8,8,128]{2,1,0:T(8,128)}) custom-call(f32[128,256]{1,0:T(8,128)} %x_ref.5, f32[256,512]{1,0:T(8,128)} %p_ref.11, f32[8,64]{1,0:T(8,128)} %dst_att_ref.1), custom_call_target="tpu_custom_call" | custom-call | tf_op jit(solution)/shard_map/pallas_call | solution.py:193
  36.1 1.3 dynamic-slice_bitcast_fusion.a_ref
  37.4 39.5 %shard_map.120 = (f32[8,2,2,72,256]{4,3,2,1,0:T(8,128)}, f32[32,8,128]{2,1,0:T(8,128)}) custom-call(s32[32,2]{1,0:T(8,128)} %copy.13.blocks, s32[1]{0:T(128)} %bitcast.9.counts, f32[32,128,256]{2,1,0:T(8,128)} %get-tuple-element.26.x_ref, f32[256,512]{1,0:T(8,128)} %p_ref.11, f32[8,64]{1,0:T(8,128)} %src_att_ref.1, f32[8,8,128]{2,1,0:T(8,128)} %get-tuple-element.27.a_ref, ...), custom_call_target="tpu_custom_call" | custom-call | tf_op jit(solution)/shard_map/pallas_call | solution.py:317
  76.8 32.7 %shard_map.121.total_ref = f32[2,2,72,256]{3,2,1,0:T(8,128)} custom-call(f32[8,2,2,72,256]{4,3,2,1,0:T(8,128)} %get-tuple-element.28.acc_ref), custom_call_target="tpu_custom_call" | custom-call | tf_op jit(solution)/shard_map/pallas_call | solution.py:411
  109.6 5.0 %shard_map.122 = (f32[128,512]{1,0:T(8,128)}, f32[136,512]{1,0:T(8,128)}, f32[512,128]{1,0:T(8,128)}, f32[8,128]{1,0:T(8,128)}) custom-call(f32[2,2,72,256]{3,2,1,0:T(8,128)} %shard_map.121.total_ref, f32[128,256]{1,0:T(8,128)} %x_ref.5, f32[256,512]{1,0:T(8,128)} %p_ref.11, f32[8,64]{1,0:T(8,128)} %src_att_ref.1, f32[8,128]{1,0:T(8,128)} %dynamic-slice_bitcast_fusion.a_ref, ...), custom_call_target="tpu_custom_call" | custom-call | tf_op jit(solution)/shard_map/pallas_call | solution.py:479
  114.5 23.3 %shard_map.123.pay_ref = f32[8,136,512]{2,1,0:T(8,128)} custom-call(f32[136,512]{1,0:T(8,128)} %get-tuple-element.31.pay_ref), custom_call_target="tpu_custom_call" | custom-call | tf_op jit(solution)/shard_map/pallas_call | solution.py:524
  137.8 40.6 %shard_map.124 = (f32[32,512,128]{2,1,0:T(8,128)}, f32[32,8,128]{2,1,0:T(8,128)}, f32[8,8,128]{2,1,0:T(8,128)}) custom-call(s32[32,2]{1,0:T(8,128)} %copy.13.blocks, s32[1]{0:T(128)} %bitcast.10.counts, s32[2]{0:T(128)} %pad_add_fusion.spot, f32[32,128,256]{2,1,0:T(8,128)} %get-tuple-element.26.x_ref, f32[256,512]{1,0:T(8,128)} %p_ref.11, ...), custom_call_target="tpu_custom_call" | custom-call | tf_op jit(solution)/shard_map/pallas_call | solution.py:628
  178.4 20.2 %shard_map.125 = (f32[32,256,128]{2,1,0:T(8,128)}, f32[512,256]{1,0:T(8,128)}, f32[8,256]{1,0:T(8,128)}) custom-call(f32[32,512,128]{2,1,0:T(8,128)} %get-tuple-element.34.dh_ref, f32[32,8,128]{2,1,0:T(8,128)} %get-tuple-element.35.dsrc_ref, f32[32,128,256]{2,1,0:T(8,128)} %get-tuple-element.26.x_ref, f32[256,512]{1,0:T(8,128)} %p_ref.11, f32[8,64]{1,0:T(8,128)} %src_att_ref.1), custom_call_target="tpu_custom_call" | custom-call | tf_op jit(solution)/shard_map/pallas_call | solution.py:681
  198.6 57.1 %shard_map.126 = (f32[256,128]{1,0:T(8,128)}, f32[16,2,40,128]{3,2,1,0:T(8,128)}, f32[8,128]{1,0:T(8,128)}) custom-call(f32[4,4,2,256,128]{4,3,2,1,0:T(8,128)} %bitcast.13, f32[512,256]{1,0:T(8,128)} %get-tuple-element.37.dp_ref, f32[8,256]{1,0:T(8,128)} %get-tuple-element.38.v_ref, f32[8,8,128]{2,1,0:T(8,128)} %get-tuple-element.39.ddst_ref, f32[128,256]{1,0:T(8,128)} %x_ref.5), custom_call_target="tpu_custom_call" | custom-call | tf_op jit(solution)/shard_map/pallas_call | solution.py:841
  255.7 4.2 %shard_map.127 = (f32[128,256]{1,0:T(8,128)}, f32[256,512]{1,0:T(8,128)}, f32[8,64]{1,0:T(8,128)}, f32[8,64]{1,0:T(8,128)}) custom-call(f32[256,128]{1,0:T(8,128)} %get-tuple-element.40.dx_ref, f32[32,40,128]{2,1,0:T(8,128)} %bitcast.14, f32[8,128]{1,0:T(8,128)} %get-tuple-element.42.dst_ref, f32[256,512]{1,0:T(8,128)} %p_ref.11, f32[8,64]{1,0:T(8,128)} %src_att_ref.1, ...), custom_call_target="tpu_custom_call" | custom-call | tf_op jit(solution)/shard_map/pallas_call | solution.py:900

commit v2 on v1

--- a/solution.py
+++ b/solution.py
@@ -101,17 +101,21 @@
                 chains.remove(chain)
 
 
-def gather_body(x_ref, p_ref, att_ref, panel_ref, a_ref, send, recv, own_sem):
+def gather_body(x_ref, p_ref, src_ref, dst_ref, panel_ref, a_ref, pay, send, recv, own_sem):
     d, y, x, k, z = place()
     sibling = node(y, x, 1 - k)
     wait_all = greet(
         [sibling, node(y + 1, x, k), node(y - 1, x, k), node(y, x + 1, k), node(y, x - 1, k)],
         [lax.rem(z + s, 8) for s in range(1, 8)],
     )
-    own_copy = pltpu.make_async_copy(x_ref, panel_ref.at[d], own_sem)
+    rows = jnp.concatenate([score_rows(r[...], p_ref[...]) for r in (src_ref, dst_ref)], axis=0) * LOG2E
+    scores = dot(rows, x_ref[...], NT, HIGHEST)
+    pay[0:128] = x_ref[...]
+    pay[128:136, 0:128] = scores[0:8]
+    pay[128:136, 128:256] = scores[8:16]
+    a_ref[z] = scores[8:16]
+    own_copy = pltpu.make_async_copy(pay, panel_ref.at[d], own_sem)
     own_copy.start()
-    rows = score_rows(att_ref[...], p_ref[...]) * LOG2E
-    a_ref[z] = dot(rows, x_ref[...], NT, HIGHEST)
     wait_all()
     links = Links(send, recv)
 
@@ -120,9 +124,10 @@
             return node(y + v, x + u, k) if half == 0 else node(y + u, x + v, k)
 
         def region(u, v, quarter=None):
-            if quarter is None:
-                return panel_ref.at[at(u, v), pl.ds(64 * half, 64)]
-            return panel_ref.at[at(u, v), pl.ds(64 * half + 32 * quarter, 32)]
+            start, size = 64 * half, 64 + 8 * half
+            if quarter is not None:
+                start, size = start + 32 * quarter, 32 + 8 * half * quarter
+            return panel_ref.at[at(u, v), pl.ds(start, size)]
 
         def to(part, du, dv, src=None):
             return links.push(part if src is None else src, part, dst=at(du, dv))
@@ -131,7 +136,7 @@
             part = region(u, v)
             return links.push(part if src is None else src, part, dst=sibling)
 
-        own = x_ref.at[pl.ds(64 * half, 64)]
+        own = pay.at[pl.ds(64 * half, 64 + 8 * half)]
         first = [to(region(0, 0), 1, 0, own), to(region(0, 0), -1, 0, own)]
         second = {0: [to(region(0, 0), 0, 1, own), to(region(0, 0), 0, -1, own)]}
         twins = [twin(0, 0, own)]
@@ -188,48 +193,66 @@
     links.drain()
 
 
-def gather_inputs(x, proj, att_dst):
+def gather_inputs(x, proj, att_src, att_dst):
     count = 72 + 7
     return pl.pallas_call(
         gather_body,
         out_shape=(
-            jax.ShapeDtypeStruct((32, 128, 256), F32),
+            jax.ShapeDtypeStruct((32, 136, 256), F32),
             jax.ShapeDtypeStruct((8, 8, 128), F32),
         ),
-        in_specs=[VMEM] * 3,
+        in_specs=[VMEM] * 4,
         out_specs=(ANY, VMEM),
         scratch_shapes=[
+            pltpu.VMEM((136, 256), F32),
             pltpu.SemaphoreType.DMA((count,)),
             pltpu.SemaphoreType.DMA((count,)),
             pltpu.SemaphoreType.DMA,
         ],
         compiler_params=pltpu.CompilerParams(collective_id=0, has_side_effects=True),
-    )(x, proj, att_dst)
-
-
-def prepare_features(x_ref, p_ref, p_cat, hb, extra):
+    )(x, proj, att_src, att_dst)
+
+
+def split_weights(p_ref, p_cat):
     high, low = split(p_ref[...])
     p_cat[0:256] = high
     p_cat[256:512] = low
     p_cat[512:768] = high
+
+
+def stream_in(panel, x_ref, masks, mask_ref, sems):
+    def part(group):
+        span = pl.ds(4 * group, 4)
+        return pltpu.make_async_copy(panel.at[span], x_ref.at[span], sems.at[group])
+
+    for group in range(8):
+        part(group).start()
+    pltpu.make_async_copy(masks, mask_ref, sems.at[8]).start()
+    return part
+
+
+def prepare_features(x_ref, p_cat, hb, arrive):
     even = (lanes((1, 128)) < 64).astype(BF16)
     odd = (lanes((1, 128)) >= 64).astype(BF16)
-
-    def step(c, carry):
-        xc = x_ref[c]
-        x_high, x_low = split(xc)
-        h = dot(jnp.concatenate([x_high, x_high, x_low], axis=1), p_cat[...])
-        h_high, h_low = split(h)
-        for pair in range(4):
-            cols = slice(128 * pair, 128 * pair + 128)
-            hb[c, pair, 0:128] = h_high[:, cols] * even
-            hb[c, pair, 128:256] = h_high[:, cols] * odd
-            hb[c, pair, 256:384] = h_low[:, cols] * even
-            hb[c, pair, 384:512] = h_low[:, cols] * odd
-        extra(c, xc)
+    n = 4
+
+    def step(group, carry):
+        arrive(group).wait()
+        x_high, x_low = split(jnp.concatenate([x_ref[group * n + s, 0:128] for s in range(n)], axis=0))
+        left = jnp.concatenate([x_high, x_high, x_low], axis=1)
+        for wide in range(2):
+            h_high, h_low = split(dot(left, p_cat[:, 256 * wide : 256 * wide + 256]))
+            for s in range(n):
+                for side in range(2):
+                    part = (slice(128 * s, 128 * s + 128), slice(128 * side, 128 * side + 128))
+                    pair = 2 * wide + side
+                    hb[group * n + s, pair, 0:128] = h_high[part] * even
+                    hb[group * n + s, pair, 128:256] = h_high[part] * odd
+                    hb[group * n + s, pair, 256:384] = h_low[part] * even
+                    hb[group * n + s, pair, 384:512] = h_low[part] * odd
         return carry
 
-    lax.fori_loop(0, 32, step, 0)
+    lax.fori_loop(0, 32 // n, step, 0)
 
 
 def columns_of(rows):
@@ -237,15 +260,35 @@
     return jnp.concatenate([rows, pad], axis=0).T
 
 
+def spread_rows(rows_of, put):
+    parts = []
+    for b in range(8):
+        kinds = rows_of(b)
+        pieces = []
+        for rows in kinds:
+            high = rows.astype(BF16).astype(F32)
+            middle = (rows - high).astype(BF16).astype(F32)
+            pieces += [high, middle, rows - high - middle]
+        parts.append(columns_of(jnp.concatenate(pieces, axis=0)).astype(BF16))
+    left = jnp.concatenate(parts, axis=0)
+    count = len(kinds)
+    row = lax.broadcasted_iota(jnp.int32, (128, 128 * count), 0)
+    kind = lax.broadcasted_iota(jnp.int32, (128, 128 * count), 1) // 128
+    for h in range(8):
+        pick = jnp.logical_and(row // 24 == kind, lax.rem(row, 8) == h)
+        out = dot(left, jnp.where(pick, 1.0, 0.0).astype(BF16))
+        for k in range(count):
+            for b in range(8):
+                put(k, b, h, out[128 * b : 128 * b + 128, 128 * k : 128 * k + 128])
+
+
 def forward_body(
-    blocks, counts, x_ref, p_ref, att_ref, a_ref, mask_ref, acc_out, b_out, p_cat, hb, top, abc, sums, acc
+    blocks, counts, panel, p_ref, a_ref, masks, acc_out, p_cat, hb, top, abc, sums, acc, top_rows, x_ref, mask_ref, sems
 ):
-    rows = score_rows(att_ref[...], p_ref[...]) * LOG2E
-
-    def extra(c, xc):
-        b_out[c] = dot(rows, xc, NT, HIGHEST)
-
-    prepare_features(x_ref, p_ref, p_cat, hb, extra)
+    arrive = stream_in(panel, x_ref, masks, mask_ref, sems)
+    split_weights(p_ref, p_cat)
+    prepare_features(x_ref, p_cat, hb, arrive)
+    pltpu.make_async_copy(masks, mask_ref, sems.at[8]).wait()
     top[...] = jnp.full(top.shape, NEG, F32)
     sums[...] = jnp.zeros(sums.shape, F32)
     acc[...] = jnp.zeros(acc.shape, F32)
@@ -254,28 +297,29 @@
     def find_top(k, carry):
         b, c = blocks[k, 0], blocks[k, 1]
         keep = mask_ref[k] > 0
-        scores = b_out[c]
+        scores = x_ref[c, 128:136, 0:128]
         for h in range(8):
             top[b * 8 + h] = jnp.maximum(top[b * 8 + h], jnp.where(keep, scores[h : h + 1], NEG))
         return carry
 
     lax.fori_loop(0, live, find_top, 0)
 
-    def spread_top(b, carry):
-        a_cols = columns_of(a_ref[b])
-        for h in range(8):
-            a_col = a_cols[:, h : h + 1]
-            best = jnp.max(top[b * 8 + h], axis=1, keepdims=True)
-            top[b * 8 + h] = jnp.broadcast_to(leaky(a_col + best), (128, 128))
-            abc[b * 8 + h] = jnp.broadcast_to(a_col, (128, 128))
+    def find_rows(b, carry):
+        best = jnp.concatenate([jnp.max(top[b * 8 + h].T, axis=0, keepdims=True) for h in range(8)], axis=0)
+        top_rows[b] = leaky(a_ref[b] + best)
         return carry
 
-    lax.fori_loop(0, 8, spread_top, 0)
+    lax.fori_loop(0, 8, find_rows, 0)
+
+    def put(kind, b, h, tile):
+        (abc, top)[kind][b * 8 + h] = tile
+
+    spread_rows(lambda b: [a_ref[b], top_rows[b]], put)
 
     def accumulate(k, carry):
         b, c = blocks[k, 0], blocks[k, 1]
         keep = mask_ref[k] > 0
-        scores = b_out[c]
+        scores = x_ref[c, 128:136, 0:128]
         for pair in range(4):
             highs, lows = [], []
             for h in (2 * pair, 2 * pair + 1):
@@ -293,15 +337,9 @@
     lax.fori_loop(0, live, accumulate, 0)
 
     def pack(b, carry):
-        lane = lanes((128, 128))
-        stats = [jnp.zeros((128, 128), F32)] * 2
-        for h in range(8):
-            way, h4 = h // 4, h % 4
-            total = jnp.sum(sums[b * 8 + h], axis=1, keepdims=True)
-            stats[way] = jnp.where(lane == h4, top[b * 8 + h], stats[way])
-            stats[way] = jnp.where(lane == h4 + 4, total, stats[way])
+        totals = [jnp.sum(sums[b * 8 + h].T, axis=0, keepdims=True) for h in range(8)]
         for way in range(2):
-            packed = stats[way].T[0:8]
+            packed = jnp.concatenate([top_rows[b, 4 * way : 4 * way + 4]] + totals[4 * way : 4 * way + 4], axis=0)
             for sub in range(2):
                 span = slice(64 * sub, 64 * sub + 64)
                 acc_out[b, way, sub, 0:64, 0:128] = acc[b * 4 + 2 * way][span]
@@ -313,15 +351,12 @@
     lax.fori_loop(0, 8, pack, 0)
 
 
-def forward_local(blocks, counts, panel, proj, att_src, a, masks):
+def forward_local(blocks, counts, panel, proj, a, masks):
     return pl.pallas_call(
         forward_body,
-        out_shape=(
-            jax.ShapeDtypeStruct((8, 2, 2, 72, 256), F32),
-            jax.ShapeDtypeStruct((32, 8, 128), F32),
-        ),
-        in_specs=[SMEM, SMEM] + [VMEM] * 5,
-        out_specs=(VMEM, VMEM),
+        out_shape=jax.ShapeDtypeStruct((8, 2, 2, 72, 256), F32),
+        in_specs=[SMEM, SMEM, ANY, VMEM, VMEM, ANY],
+        out_specs=VMEM,
         scratch_shapes=[
             pltpu.VMEM((768, 512), BF16),
             pltpu.VMEM((32, 4, 512, 128), BF16),
@@ -329,9 +364,13 @@
             pltpu.VMEM((64, 128, 128), F32),
             pltpu.VMEM((64, 128, 128), F32),
             pltpu.VMEM((32, 128, 128), F32),
+            pltpu.VMEM((8, 8, 128), F32),
+            pltpu.VMEM((32, 136, 256), F32),
+            pltpu.VMEM((32, 128, 128), jnp.int32),
+            pltpu.SemaphoreType.DMA((9,)),
         ],
         compiler_params=pltpu.CompilerParams(vmem_limit_bytes=BIG_VMEM),
-    )(blocks, counts, panel, proj, att_src, a, masks)
+    )(blocks, counts, panel, proj, a, masks)
 
 
 def merge(arrived, mine, sub):
@@ -536,21 +575,19 @@
 
 
 def backward_body(
-    blocks, counts, spot, x_ref, p_ref, a_ref, b_ref, mask_ref, pay_ref, self_ref, dself_ref,
-    dh_out, dsrc_out, ddst_out, p_cat, hb, gn, gt, top, abc, dots, ddst, dsrc,
+    blocks, counts, spot, panel, p_ref, att_ref, a_ref, masks, pay_ref, self_ref, dself_ref,
+    dx_out, dp_out, ddst_out, p_cat, hb, gn, gt, top, abc, dots, ddst, dsrc, dh, p_wide, att_wide,
+    dx_slots, dx_sems, x_ref, mask_ref, sems,
 ):
-    prepare_features(x_ref, p_ref, p_cat, hb, lambda c, xc: None)
+    arrive = stream_in(panel, x_ref, masks, mask_ref, sems)
+    split_weights(p_ref, p_cat)
+    prepare_features(x_ref, p_cat, hb, arrive)
+    pltpu.make_async_copy(masks, mask_ref, sems.at[8]).wait()
     even = (lax.broadcasted_iota(jnp.int32, (128, 1), 0) < 64).astype(F32)
     odd = 1.0 - even
 
     def setup(b, carry):
-        cols = columns_of(
-            jnp.concatenate([a_ref[b], pay_ref[b, 128:136, 0:128], pay_ref[b, 128:136, 128:256]], axis=0)
-        )
-        dots[b] = cols
-        for h in range(8):
-            abc[b * 8 + h] = jnp.broadcast_to(cols[:, h : h + 1], (128, 128))
-            top[b * 8 + h] = jnp.broadcast_to(cols[:, 8 + h : 9 + h], (128, 128))
+        dots[b] = columns_of(pay_ref[b, 128:136, 128:256])
         for pair in range(4):
             grad = pay_ref[b, 0:128, 128 * pair : 128 * pair + 128]
             high, low = split(grad)
@@ -566,15 +603,20 @@
         return carry
 
     lax.fori_loop(0, 8, setup, 0)
+
+    def put(kind, b, h, tile):
+        (abc, top)[kind][b * 8 + h] = tile
+
+    spread_rows(lambda b: [a_ref[b], pay_ref[b, 128:136, 0:128]], put)
     ddst[...] = jnp.zeros(ddst.shape, F32)
     dsrc[...] = jnp.zeros(dsrc.shape, F32)
-    dh_out[...] = jnp.zeros(dh_out.shape, F32)
-    dh_out[spot[0]] = self_ref[...]
+    dh[...] = jnp.zeros(dh.shape, F32)
+    dh[spot[0]] = self_ref[...]
 
     def step(k, carry):
         b, c = blocks[k, 0], blocks[k, 1]
         keep = mask_ref[k] > 0
-        scores = b_ref[c]
+        scores = x_ref[c, 128:136, 0:128]
         cols = dots[b]
         for pair in range(4):
             g_high, g_low = gn[b, pair, :, 0:128], gn[b, pair, :, 128:256]
@@ -589,7 +631,7 @@
                 h = 2 * pair + side
                 raw = abc[b * 8 + h] + jnp.where(keep, scores[h : h + 1], NEG)
                 w = jnp.exp2(leaky(raw) - top[b * 8 + h])
-                d_raw = w * (d_alpha[:, 128 * side : 128 * side + 128] - cols[:, 16 + h : 17 + h])
+                d_raw = w * (d_alpha[:, 128 * side : 128 * side + 128] - cols[:, h : h + 1])
                 d_raw = jnp.where(raw > 0, d_raw, 0.2 * d_raw)
                 ddst[b * 8 + h] += d_raw
                 dsrc[c * 8 + h] += jnp.sum(d_raw.reshape(16, 8, 128), axis=0)
@@ -598,42 +640,82 @@
                 lows.append(low)
             left = jnp.concatenate([gt[b, pair], gt[b, pair, :, 0:256]], axis=1)
             right = jnp.concatenate(highs + highs + lows, axis=0)
-            dh_out[c, 128 * pair : 128 * pair + 128] += dot(left, right)
+            dh[c, 128 * pair : 128 * pair + 128] += dot(left, right)
         return carry
 
     lax.fori_loop(0, counts[0], step, 0)
 
     def pack_dst(b, carry):
-        lane = lanes((128, 128))
-        packed = jnp.zeros((128, 128), F32)
-        for h in range(8):
-            packed = jnp.where(lane == h, jnp.sum(ddst[b * 8 + h], axis=1, keepdims=True), packed)
-        ddst_out[b] = packed.T[0:8]
+        ddst_out[b] = jnp.concatenate(
+            [jnp.sum(ddst[b * 8 + h].T, axis=0, keepdims=True) for h in range(8)], axis=0
+        )
         return carry
 
     lax.fori_loop(0, 8, pack_dst, 0)
     ddst_out[spot[1]] += dself_ref[...]
 
-    def pack_src(c, carry):
-        dsrc_out[c] = jnp.concatenate(
-            [jnp.sum(dsrc[c * 8 + h], axis=0, keepdims=True) for h in range(8)], axis=0
+    high, low = split(p_ref[...])
+    p_wide[:, 0:512] = high
+    p_wide[:, 512:1024] = low
+    p_wide[:, 1024:1536] = high
+    att_cols = columns_of(jnp.concatenate([att_ref[...], jnp.zeros((8, 64), F32)], axis=1))
+    for h in range(8):
+        att_wide[64 * h : 64 * h + 64] = jnp.broadcast_to(att_cols[0:64, h : h + 1], (64, 128))
+    dp_out[...] = jnp.zeros(dp_out.shape, F32)
+    own = spot[0]
+
+    def leave(four, slot):
+        return pltpu.make_async_copy(dx_slots.at[slot], dx_out.at[pl.ds(4 * four, 4)], dx_sems.at[slot])
+
+    def project(four, carry):
+        wide_dh, wide_src = [], []
+        for s in range(4):
+            c = 4 * four + s
+            d_src = jnp.concatenate(
+                [jnp.sum(dsrc[c * 8 + h], axis=0, keepdims=True) for h in range(8)], axis=0
+            )
+            d_src = d_src + jnp.where(c == own, dself_ref[...], 0.0)
+            spread = jnp.concatenate(
+                [att_wide[64 * h : 64 * h + 64] * d_src[h : h + 1] for h in range(8)], axis=0
+            )
+            wide_dh.append(dh[c] + spread)
+            wide_src.append(jnp.concatenate([d_src, jnp.zeros((8, 128), F32)], axis=0))
+        high, low = split(jnp.concatenate(wide_dh, axis=1))
+        s_high, s_low = split(jnp.concatenate(wide_src, axis=1))
+        x_high, x_low = split(jnp.concatenate([x_ref[4 * four + s, 0:128] for s in range(4)], axis=0))
+        dx = dot(p_wide[...], jnp.concatenate([high, high, low], axis=0))
+        slot = lax.rem(four, 2)
+
+        @pl.when(four >= 2)
+        def _():
+            leave(four - 2, slot).wait()
+
+        for s in range(4):
+            dx_slots[slot, s] = dx[:, 128 * s : 128 * s + 128]
+        leave(four, slot).start()
+        tall_high = jnp.concatenate([high, s_high], axis=0)
+        tall_low = jnp.concatenate([low, s_low], axis=0)
+        dp_out[...] += dot(
+            jnp.concatenate([tall_high, tall_high, tall_low], axis=1),
+            jnp.concatenate([x_high, x_low, x_high], axis=0),
         )
         return carry
 
-    lax.fori_loop(0, 32, pack_src, 0)
-    dsrc_out[spot[0]] += dself_ref[...]
-
-
-def backward_local(blocks, counts, spot, panel, proj, a, b, masks, pays, dh_self, d_self):
+    lax.fori_loop(0, 8, project, 0)
+    leave(6, 0).wait()
+    leave(7, 1).wait()
+
+
+def backward_local(blocks, counts, spot, panel, proj, att_src, a, masks, pays, dh_self, d_self):
     return pl.pallas_call(
         backward_body,
         out_shape=(
-            jax.ShapeDtypeStruct((32, 512, 128), F32),
-            jax.ShapeDtypeStruct((32, 8, 128), F32),
+            jax.ShapeDtypeStruct((32, 256, 128), F32),
+            jax.ShapeDtypeStruct((528, 256), F32),
             jax.ShapeDtypeStruct((8, 8, 128), F32),
         ),
-        in_specs=[SMEM] * 3 + [VMEM] * 8,
-        out_specs=(VMEM,) * 3,
+        in_specs=[SMEM] * 3 + [ANY, VMEM, VMEM, VMEM, ANY, VMEM, VMEM, VMEM],
+        out_specs=(ANY, VMEM, VMEM),
         scratch_shapes=[
             pltpu.VMEM((768, 512), BF16),
             pltpu.VMEM((32, 4, 512, 128), BF16),
@@ -644,67 +726,21 @@
             pltpu.VMEM((8, 128, 128), F32),
             pltpu.VMEM((64, 128, 128), F32),
             pltpu.VMEM((256, 8, 128), F32),
+            pltpu.VMEM((32, 512, 128), F32),
+            pltpu.VMEM((256, 1536), BF16),
+            pltpu.VMEM((512, 128), F32),
+            pltpu.VMEM((2, 4, 256, 128), F32),
+            pltpu.SemaphoreType.DMA((2,)),
+            pltpu.VMEM((32, 136, 256), F32),
+            pltpu.VMEM((32, 128, 128), jnp.int32),
+            pltpu.SemaphoreType.DMA((9,)),
         ],
         compiler_params=pltpu.CompilerParams(vmem_limit_bytes=BIG_VMEM),
-    )(blocks, counts, spot, panel, proj, a, b, masks, pays, dh_self, d_self)
-
-
-def project_body(dh_ref, dsrc_ref, x_ref, p_ref, att_ref, dx_ref, dp_ref, v_ref, p_cat, rows_t):
-    @pl.when(pl.program_id(0) == 0)
-    def _():
-        proj = p_ref[...]
-        high, low = split(proj)
-        p_cat[:, 0:512] = high
-        p_cat[:, 512:1024] = low
-        p_cat[:, 1024:1536] = high
-        rows = jnp.concatenate([score_rows(att_ref[...], proj), jnp.zeros((120, 256), F32)], axis=0)
-        rows_t[...] = rows.T
-        dp_ref[...] = jnp.zeros(dp_ref.shape, F32)
-        v_ref[...] = jnp.zeros(v_ref.shape, F32)
-
-    for s in range(dh_ref.shape[0]):
-        x, d_src = x_ref[s], dsrc_ref[s]
-        dh_high, dh_low = split(dh_ref[s])
-        x_high, x_low = split(x)
-        wide_src = jnp.concatenate([d_src, jnp.zeros((120, 128), F32)], axis=0)
-        dx_ref[s] = dot(p_cat[...], jnp.concatenate([dh_high, dh_high, dh_low], axis=0)) + dot(
-            rows_t[...], wide_src, NN, HIGHEST
-        )
-        dp_ref[...] += dot(
-            jnp.concatenate([dh_high, dh_high, dh_low], axis=1), jnp.concatenate([x_high, x_low, x_high], axis=0)
-        )
-        v_ref[...] += dot(d_src, x, NN, HIGHEST)
-
-
-def project_grads(dh, dsrc, panel, proj, att_src):
-    n = 4
-    return pl.pallas_call(
-        project_body,
-        grid=(32 // n,),
-        out_shape=(
-            jax.ShapeDtypeStruct((32, 256, 128), F32),
-            jax.ShapeDtypeStruct((512, 256), F32),
-            jax.ShapeDtypeStruct((8, 256), F32),
-        ),
-        in_specs=[
-            pl.BlockSpec((n, 512, 128), lambda i: (i, 0, 0)),
-            pl.BlockSpec((n, 8, 128), lambda i: (i, 0, 0)),
-            pl.BlockSpec((n, 128, 256), lambda i: (i, 0, 0)),
-            VMEM,
-            VMEM,
-        ],
-        out_specs=(
-            pl.BlockSpec((n, 256, 128), lambda i: (i, 0, 0)),
-            pl.BlockSpec((512, 256), lambda i: (0, 0)),
-            pl.BlockSpec((8, 256), lambda i: (0, 0)),
-        ),
-        scratch_shapes=[pltpu.VMEM((256, 1536), BF16), pltpu.VMEM((256, 128), F32)],
-        compiler_params=pltpu.CompilerParams(vmem_limit_bytes=BIG_VMEM),
-    )(dh, dsrc, panel, proj, att_src)
+    )(blocks, counts, spot, panel, proj, att_src, a, masks, pays, dh_self, d_self)
 
 
 def reduce_body(
-    dx_ref, dp_ref, v_ref, ddst_ref, x_ref, dx_out, dp_out, dst_out,
+    dx_ref, dp_ref, ddst_ref, x_ref, dx_out, dp_out, dst_out,
     send, recv, twin_dx, total, far, near, far2, near2, dst_all, pay, twin_pay, merged, plane, joined, tower,
 ):
     d, y, x, k, z = place()
@@ -776,7 +812,7 @@
         for h in range(8):
             for side in range(2):
                 i = 8 + h + 16 * side
-                pay[i // 2, i % 2, 32:33] = v_ref[h : h + 1, 128 * side : 128 * side + 128]
+                pay[i // 2, i % 2, 32:33] = dp_ref[512 + h : 513 + h, 128 * side : 128 * side + 128]
         yield
         for copy in dst_copies:
             copy.wait_recv()
@@ -836,7 +872,7 @@
     links.drain()
 
 
-def reduce_grads(dx, dp, v, ddst, x):
+def reduce_grads(dx, dp, ddst, x):
     count = 7 + 16 + 24 + 1 + 15 + 7 + 15 + 1
     return pl.pallas_call(
         reduce_body,
@@ -845,7 +881,7 @@
             jax.ShapeDtypeStruct((16, 2, 40, 128), F32),
             jax.ShapeDtypeStruct((8, 128), F32),
         ),
-        in_specs=[VMEM] * 5,
+        in_specs=[VMEM] * 4,
         out_specs=(VMEM,) * 3,
         scratch_shapes=[
             pltpu.SemaphoreType.DMA((count,)),
@@ -867,13 +903,12 @@
         compiler_params=pltpu.CompilerParams(
             collective_id=3, has_side_effects=True, vmem_limit_bytes=BIG_VMEM
         ),
-    )(dx.reshape(4, 4, 2, 256, 128), dp, v, ddst, x)
-
-
-def finish_body(dx_ref, w_ref, dst_ref, p_ref, src_att_ref, dst_att_ref, in_ref, proj_ref, src_ref, dst_out):
+    )(dx.reshape(4, 4, 2, 256, 128), dp, ddst, x)
+
+
+def finish_body(dx_ref, w_ref, dst_ref, p_ref, dst_att_ref, in_ref, proj_ref, src_ref, dst_out):
     proj = p_ref[...]
     a_rows = per_head_rows(dst_att_ref[...])
-    s_rows = per_head_rows(src_att_ref[...])
     score = dot(a_rows, proj, NT, HIGHEST)
     pad = jnp.zeros((120, 256), F32)
     score_t = jnp.concatenate([score, pad], axis=0).T
@@ -885,18 +920,18 @@
 
     u = jnp.concatenate([row(h) for h in range(8)], axis=0)
     v = jnp.concatenate([row(8 + h) for h in range(8)], axis=0)
-    uv = jnp.concatenate([u, v, jnp.zeros((112, 256), F32)], axis=0)
-    att = jnp.concatenate([a_rows, s_rows, jnp.zeros((112, 512), F32)], axis=0)
+    wide_u = jnp.concatenate([u, jnp.zeros((120, 256), F32)], axis=0)
+    att = jnp.concatenate([a_rows, jnp.zeros((120, 512), F32)], axis=0)
     grad_t = jnp.concatenate(
         [jnp.concatenate([w_ref[i, 0:16], w_ref[i, 16:32]], axis=1) for i in range(32)], axis=0
     )
-    proj_ref[...] = (grad_t + dot(att.T, uv, NN, HIGHEST)).T
+    proj_ref[...] = (grad_t + dot(att.T, wide_u, NN, HIGHEST)).T
     both = dot(jnp.concatenate([u, v], axis=0), proj, NN, HIGHEST)
     dst_out[...] = jnp.concatenate([both[h : h + 1, 64 * h : 64 * h + 64] for h in range(8)], axis=0)
     src_ref[...] = jnp.concatenate([both[8 + h : 9 + h, 64 * h : 64 * h + 64] for h in range(8)], axis=0)
 
 
-def finish(dx, weights, dst_total, proj, att_src, att_dst):
+def finish(dx, weights, dst_total, proj, att_dst):
     return pl.pallas_call(
         finish_body,
         out_shape=(
@@ -905,9 +940,9 @@
             jax.ShapeDtypeStruct((8, 64), F32),
             jax.ShapeDtypeStruct((8, 64), F32),
         ),
-        in_specs=[VMEM] * 6,
+        in_specs=[VMEM] * 5,
         out_specs=(VMEM,) * 4,
-    )(dx, weights.reshape(32, 40, 128), dst_total, proj, att_src, att_dst)
+    )(dx, weights.reshape(32, 40, 128), dst_total, proj, att_dst)
 
 
 def shards(inputs, projection, att_src, att_dst, blocks, counts, tile_masks, cotangent):
@@ -916,20 +951,17 @@
     masks = tile_masks[0, 0]
     z = lax.axis_index("src")
     spot = jnp.stack([lax.axis_index("dst"), z]).astype(jnp.int32)
-    panel, a = gather_inputs(inputs, projection, att_dst)
-    acc, b = forward_local(coords, live, panel, projection, att_src, a, masks)
+    panel, a = gather_inputs(inputs, projection, att_src, att_dst)
+    acc = forward_local(coords, live, panel, projection, a, masks)
     total = sum_over_src(acc)
     a_own = lax.dynamic_index_in_dim(a, z, 0, keepdims=False)
     output, pay, dh_self, d_self = owner_rows(total, inputs, projection, att_src, a_own, cotangent)
     pays = gather_grads(pay)
-    dh, dsrc, ddst = backward_local(
-        coords, live, spot, panel, projection, a, b, masks, pays, dh_self, d_self
+    dx, dp, ddst = backward_local(
+        coords, live, spot, panel, projection, att_src, a, masks, pays, dh_self, d_self
     )
-    dx, dp, v = project_grads(dh, dsrc, panel, projection, att_src)
-    dx_own, weights, dst_total = reduce_grads(dx, dp, v, ddst, inputs)
-    in_grad, proj_grad, src_grad, dst_grad = finish(
-        dx_own, weights, dst_total, projection, att_src, att_dst
-    )
+    dx_own, weights, dst_total = reduce_grads(dx, dp, ddst, inputs)
+    in_grad, proj_grad, src_grad, dst_grad = finish(dx_own, weights, dst_total, projection, att_dst)
     return (output, in_grad, proj_grad, src_grad, dst_grad)
 
 

time: 260 us -> 230 us (0.88)
  Pallas kernels: 255 us -> 225 us
    pallas_call x4 -> x3, Pallas kernels: 133 us -> 106 us  [the longest x1 44.5 us: backward_local(): pl.pallas_call(backward_body, out_shape=(jax.ShapeDtypeStruct((32, 256, 1...]
    pallas_call x1, Pallas kernels: 57.1 us -> 53.9 us  [reduce_grads(): pl.pallas_call(reduce_body, out_shape=(jax.ShapeDtypeStruct((256, 128), F...]
where the time goes in v2:
time: 230 us
  Pallas kernels  225 us (98%)
  local copies, waits for them, and re-layouts  2.63 us (1%)
    pallas_call x1, Pallas kernels, reduce_grads(): pl.pallas_call(reduce_body, out_shape=(jax.ShapeDtypeStruct((256, 128), F...  53.9 us
    pallas_call x1, Pallas kernels, backward_local(): pl.pallas_call(backward_body, out_shape=(jax.ShapeDtypeStruct((32, 256, 1...  44.5 us
    pallas_call x1, Pallas kernels, gather_inputs(): pl.pallas_call(gather_body, out_shape=(jax.ShapeDtypeStruct((32, 136, 256...  33.5 us
    pallas_call x1, Pallas kernels, sum_over_src(): pl.pallas_call(sum_body, out_shape=jax.ShapeDtypeStruct((2, 2, 72, 256),...  31.2 us
    pallas_call x1, Pallas kernels, forward_local(): pl.pallas_call(forward_body, out_shape=jax.ShapeDtypeStruct((8, 2, 2, 72,...  28 us
    pallas_call x1, Pallas kernels, gather_grads(): pl.pallas_call(grads_body, out_shape=jax.ShapeDtypeStruct((8, 136, 512),...  24.6 us
    pallas_call x1, Pallas kernels, owner_rows(): pl.pallas_call(owner_body, out_shape=(jax.ShapeDtypeStruct((128, 512), F3...  4.93 us

profile of v2, /device:TPU:1, one launch (start us, length us, event | category | flops | bytes accessed | tf_op | source)
XLA Modules:
  0.0 229.5 jit_solution(16540958975103753865)
XLA Ops:
  1.3 0.6 pad_add_fusion.spot
  1.9 1.4 copy.13.blocks
  3.3 33.5 %shard_map.119 = (f32[32,136,256]{2,1,0:T(8,128)}, f32[8,8,128]{2,1,0:T(8,128)}) custom-call(f32[128,256]{1,0:T(8,128)} %x_ref.5, f32[256,512]{1,0:T(8,128)} %p_ref.9, f32[8,64]{1,0:T(8,128)} %att_ref.3, f32[8,64]{1,0:T(8,128)} %dst_att_ref.1), custom_call_target="tpu_custom_call" | custom-call | tf_op jit(solution)/shard_map/pallas_call | solution.py:198
  36.8 1.3 dynamic-slice_bitcast_fusion.a_ref
  38.0 28.0 %shard_map.120.acc_ref = f32[8,2,2,72,256]{4,3,2,1,0:T(8,128)} custom-call(s32[32,2]{1,0:T(8,128)} %copy.13.blocks, s32[1]{0:T(128)} %bitcast.9.counts, f32[32,136,256]{2,1,0:T(8,128)} %get-tuple-element.21.panel, f32[256,512]{1,0:T(8,128)} %p_ref.9, f32[8,8,128]{2,1,0:T(8,128)} %get-tuple-element.22.a_ref, s32[32,128,128]{2,1,0:T(8,128)} %bitcast.11), custom_call_target="tpu_custom_call" | custom-call | tf_op jit(solution)/shard_map/pallas_call | solution.py:355
  66.1 31.2 %shard_map.121.total_ref = f32[2,2,72,256]{3,2,1,0:T(8,128)} custom-call(f32[8,2,2,72,256]{4,3,2,1,0:T(8,128)} %shard_map.120.acc_ref), custom_call_target="tpu_custom_call" | custom-call | tf_op jit(solution)/shard_map/pallas_call | solution.py:450
  97.3 4.9 %shard_map.122 = (f32[128,512]{1,0:T(8,128)}, f32[136,512]{1,0:T(8,128)}, f32[512,128]{1,0:T(8,128)}, f32[8,128]{1,0:T(8,128)}) custom-call(f32[2,2,72,256]{3,2,1,0:T(8,128)} %shard_map.121.total_ref, f32[128,256]{1,0:T(8,128)} %x_ref.5, f32[256,512]{1,0:T(8,128)} %p_ref.9, f32[8,64]{1,0:T(8,128)} %att_ref.3, f32[8,128]{1,0:T(8,128)} %dynamic-slice_bitcast_fusion.a_ref, ...), custom_call_target="tpu_custom_call" | custom-call | tf_op jit(solution)/shard_map/pallas_call | solution.py:518
  102.2 24.6 %shard_map.123.pay_ref = f32[8,136,512]{2,1,0:T(8,128)} custom-call(f32[136,512]{1,0:T(8,128)} %get-tuple-element.24.pay_ref), custom_call_target="tpu_custom_call" | custom-call | tf_op jit(solution)/shard_map/pallas_call | solution.py:563
  126.8 44.5 %shard_map.124 = (f32[32,256,128]{2,1,0:T(8,128)}, f32[528,256]{1,0:T(8,128)}, f32[8,8,128]{2,1,0:T(8,128)}) custom-call(s32[32,2]{1,0:T(8,128)} %copy.13.blocks, s32[1]{0:T(128)} %bitcast.10.counts, s32[2]{0:T(128)} %pad_add_fusion.spot, f32[32,136,256]{2,1,0:T(8,128)} %get-tuple-element.21.panel, f32[256,512]{1,0:T(8,128)} %p_ref.9, f32[8,64]{1,0:T(8,128)} %att_ref.3, ...), custom_call_target="tpu_custom_call" | custom-call | tf_op jit(solution)/shard_map/pallas_call | solution.py:710
  171.2 53.9 %shard_map.125 = (f32[256,128]{1,0:T(8,128)}, f32[16,2,40,128]{3,2,1,0:T(8,128)}, f32[8,128]{1,0:T(8,128)}) custom-call(f32[4,4,2,256,128]{4,3,2,1,0:T(8,128)} %bitcast.13, f32[528,256]{1,0:T(8,128)} %get-tuple-element.28.dp_ref, f32[8,8,128]{2,1,0:T(8,128)} %get-tuple-element.29.ddst_ref, f32[128,256]{1,0:T(8,128)} %x_ref.5), custom_call_target="tpu_custom_call" | custom-call | tf_op jit(solution)/shard_map/pallas_call | solution.py:877
  225.1 4.4 %shard_map.126 = (f32[128,256]{1,0:T(8,128)}, f32[256,512]{1,0:T(8,128)}, f32[8,64]{1,0:T(8,128)}, f32[8,64]{1,0:T(8,128)}) custom-call(f32[256,128]{1,0:T(8,128)} %get-tuple-element.30.dx_ref, f32[32,40,128]{2,1,0:T(8,128)} %bitcast.14, f32[8,128]{1,0:T(8,128)} %get-tuple-element.32.dst_ref, f32[256,512]{1,0:T(8,128)} %p_ref.9, f32[8,64]{1,0:T(8,128)} %dst_att_ref.1), custom_call_target="tpu_custom_call" | custom-call | tf_op jit(solution)/shard_map/pallas_call | solution.py:935

commit v3 on v2

--- a/solution.py
+++ b/solution.py
@@ -101,21 +101,50 @@
                 chains.remove(chain)
 
 
-def gather_body(x_ref, p_ref, src_ref, dst_ref, panel_ref, a_ref, pay, send, recv, own_sem):
+def around(links, own_ref, all_ref, z):
+    spans = (pl.ds(0, 64), pl.ds(64, 72))
+    right, left = lax.rem(z + 1, 8), lax.rem(z + 7, 8)
+
+    def push(step, way, sub):
+        block = lax.rem(z + 8 - step, 8) if way == 0 else lax.rem(z + step, 8)
+        part = all_ref.at[block, spans[sub]]
+        source = own_ref.at[spans[sub]] if step == 0 else part
+        return links.push(source, part, src=right if way == 0 else left)
+
+    order = [(way, sub) for sub in range(2) for way in range(2)]
+    coming = {item: push(0, *item) for item in order}
+    for step in range(1, 4):
+        for item in order:
+            yield
+            coming[item].wait_recv()
+            if step < 3 or item[0] == item[1]:
+                coming[item] = push(step, *item)
+            else:
+                del coming[item]
+    for copy in list(coming.values()):
+        yield
+        copy.wait_recv()
+
+
+def gather_body(x_ref, p_ref, src_ref, dst_ref, panel_ref, group_ref, own_ref, pay, send, recv, own_sem):
     d, y, x, k, z = place()
     sibling = node(y, x, 1 - k)
     wait_all = greet(
         [sibling, node(y + 1, x, k), node(y - 1, x, k), node(y, x + 1, k), node(y, x - 1, k)],
-        [lax.rem(z + s, 8) for s in range(1, 8)],
+        [lax.rem(z + 1, 8), lax.rem(z + 7, 8)],
     )
     rows = jnp.concatenate([score_rows(r[...], p_ref[...]) for r in (src_ref, dst_ref)], axis=0) * LOG2E
     scores = dot(rows, x_ref[...], NT, HIGHEST)
     pay[0:128] = x_ref[...]
     pay[128:136, 0:128] = scores[0:8]
     pay[128:136, 128:256] = scores[8:16]
-    a_ref[z] = scores[8:16]
-    own_copy = pltpu.make_async_copy(pay, panel_ref.at[d], own_sem)
-    own_copy.start()
+    own_ref[...] = scores
+    own_copies = [
+        pltpu.make_async_copy(pay, panel_ref.at[d], own_sem.at[0]),
+        pltpu.make_async_copy(pay, group_ref.at[z], own_sem.at[1]),
+    ]
+    for copy in own_copies:
+        copy.start()
     wait_all()
     links = Links(send, recv)
 
@@ -183,31 +212,28 @@
         for copy in twins:
             copy.wait_recv()
 
-    scores = [
-        links.push(a_ref.at[z], a_ref.at[z], src=lax.rem(z + s, 8)) for s in range(1, 8)
-    ]
-    run_chains([chain(0), chain(1)])
-    for copy in scores:
-        copy.wait_recv()
-    own_copy.wait()
+    run_chains([chain(0), chain(1), around(links, pay, group_ref, z)])
+    for copy in own_copies:
+        copy.wait()
     links.drain()
 
 
 def gather_inputs(x, proj, att_src, att_dst):
-    count = 72 + 7
+    count = 72 + 14
     return pl.pallas_call(
         gather_body,
         out_shape=(
             jax.ShapeDtypeStruct((32, 136, 256), F32),
-            jax.ShapeDtypeStruct((8, 8, 128), F32),
+            jax.ShapeDtypeStruct((8, 136, 256), F32),
+            jax.ShapeDtypeStruct((16, 128), F32),
         ),
         in_specs=[VMEM] * 4,
-        out_specs=(ANY, VMEM),
+        out_specs=(ANY, ANY, VMEM),
         scratch_shapes=[
             pltpu.VMEM((136, 256), F32),
             pltpu.SemaphoreType.DMA((count,)),
             pltpu.SemaphoreType.DMA((count,)),
-            pltpu.SemaphoreType.DMA,
+            pltpu.SemaphoreType.DMA((2,)),
         ],
         compiler_params=pltpu.CompilerParams(collective_id=0, has_side_effects=True),
     )(x, proj, att_src, att_dst)
@@ -220,14 +246,15 @@
     p_cat[512:768] = high
 
 
-def stream_in(panel, x_ref, masks, mask_ref, sems):
-    def part(group):
-        span = pl.ds(4 * group, 4)
-        return pltpu.make_async_copy(panel.at[span], x_ref.at[span], sems.at[group])
-
-    for group in range(8):
-        part(group).start()
+def stream_in(panel, x_ref, masks, mask_ref, group, a_ref, sems):
+    def part(i):
+        span = pl.ds(4 * i, 4)
+        return pltpu.make_async_copy(panel.at[span], x_ref.at[span], sems.at[i])
+
+    for i in range(8):
+        part(i).start()
     pltpu.make_async_copy(masks, mask_ref, sems.at[8]).start()
+    pltpu.make_async_copy(group.at[:, pl.ds(128, 8), pl.ds(128, 128)], a_ref, sems.at[9]).start()
     return part
 
 
@@ -283,19 +310,20 @@
 
 
 def forward_body(
-    blocks, counts, panel, p_ref, a_ref, masks, acc_out, p_cat, hb, top, abc, sums, acc, top_rows, x_ref, mask_ref, sems
+    blocks, counts, panel, p_ref, group, masks, acc_out, p_cat, hb, top, abc, sums, acc, top_rows, a_ref, x_ref, mask_ref, sems
 ):
-    arrive = stream_in(panel, x_ref, masks, mask_ref, sems)
+    arrive = stream_in(panel, x_ref, masks, mask_ref, group, a_ref, sems)
     split_weights(p_ref, p_cat)
     prepare_features(x_ref, p_cat, hb, arrive)
     pltpu.make_async_copy(masks, mask_ref, sems.at[8]).wait()
+    pltpu.make_async_copy(group.at[:, pl.ds(128, 8), pl.ds(128, 128)], a_ref, sems.at[9]).wait()
     top[...] = jnp.full(top.shape, NEG, F32)
     sums[...] = jnp.zeros(sums.shape, F32)
     acc[...] = jnp.zeros(acc.shape, F32)
     live = counts[0]
 
     def find_top(k, carry):
-        b, c = blocks[k, 0], blocks[k, 1]
+        b, c = blocks[2 * k], blocks[2 * k + 1]
         keep = mask_ref[k] > 0
         scores = x_ref[c, 128:136, 0:128]
         for h in range(8):
@@ -317,7 +345,7 @@
     spread_rows(lambda b: [a_ref[b], top_rows[b]], put)
 
     def accumulate(k, carry):
-        b, c = blocks[k, 0], blocks[k, 1]
+        b, c = blocks[2 * k], blocks[2 * k + 1]
         keep = mask_ref[k] > 0
         scores = x_ref[c, 128:136, 0:128]
         for pair in range(4):
@@ -339,23 +367,25 @@
     def pack(b, carry):
         totals = [jnp.sum(sums[b * 8 + h].T, axis=0, keepdims=True) for h in range(8)]
         for way in range(2):
-            packed = jnp.concatenate([top_rows[b, 4 * way : 4 * way + 4]] + totals[4 * way : 4 * way + 4], axis=0)
-            for sub in range(2):
-                span = slice(64 * sub, 64 * sub + 64)
-                acc_out[b, way, sub, 0:64, 0:128] = acc[b * 4 + 2 * way][span]
-                acc_out[b, way, sub, 0:64, 128:256] = acc[b * 4 + 2 * way + 1][span]
-                acc_out[b, way, sub, 64:72, 0:128] = packed
-                acc_out[b, way, sub, 64:72, 128:256] = jnp.zeros((8, 128), F32)
+            for inner in range(2):
+                h = 4 * way + 2 * inner
+                packed = jnp.concatenate(
+                    [top_rows[b, h : h + 2]] + totals[h : h + 2] + [jnp.zeros((4, 128), F32)], axis=0
+                )
+                for half in range(2):
+                    sub = 2 * inner + half
+                    acc_out[b, way, sub, 0:64] = acc[b * 4 + 2 * way + inner][64 * half : 64 * half + 64]
+                    acc_out[b, way, sub, 64:72] = packed
         return carry
 
     lax.fori_loop(0, 8, pack, 0)
 
 
-def forward_local(blocks, counts, panel, proj, a, masks):
+def forward_local(blocks, counts, panel, proj, group, masks):
     return pl.pallas_call(
         forward_body,
-        out_shape=jax.ShapeDtypeStruct((8, 2, 2, 72, 256), F32),
-        in_specs=[SMEM, SMEM, ANY, VMEM, VMEM, ANY],
+        out_shape=jax.ShapeDtypeStruct((8, 2, 4, 72, 128), F32),
+        in_specs=[SMEM, SMEM, ANY, VMEM, ANY, ANY],
         out_specs=VMEM,
         scratch_shapes=[
             pltpu.VMEM((768, 512), BF16),
@@ -365,36 +395,35 @@
             pltpu.VMEM((64, 128, 128), F32),
             pltpu.VMEM((32, 128, 128), F32),
             pltpu.VMEM((8, 8, 128), F32),
+            pltpu.VMEM((8, 8, 128), F32),
             pltpu.VMEM((32, 136, 256), F32),
             pltpu.VMEM((32, 128, 128), jnp.int32),
-            pltpu.SemaphoreType.DMA((9,)),
+            pltpu.SemaphoreType.DMA((10,)),
         ],
         compiler_params=pltpu.CompilerParams(vmem_limit_bytes=BIG_VMEM),
-    )(blocks, counts, panel, proj, a, masks)
-
-
-def merge(arrived, mine, sub):
-    one, two = arrived[64:72, 0:128], mine[64:72, 0:128]
-    best = jnp.maximum(one[0:4], two[0:4])
-    f_one, f_two = jnp.exp2(one[0:4] - best), jnp.exp2(two[0:4] - best)
-    total = one[4:8] * f_one + two[4:8] * f_two
-    cols = columns_of(jnp.concatenate([f_one, f_two], axis=0))[64 * sub : 64 * sub + 64]
+    )(blocks, counts, panel, proj, group, masks)
+
+
+def merge(arrived, mine, half):
+    one, two = arrived[64:72], mine[64:72]
+    best = jnp.maximum(one[0:2], two[0:2])
+    f_one, f_two = jnp.exp2(one[0:2] - best), jnp.exp2(two[0:2] - best)
+    total = one[2:4] * f_one + two[2:4] * f_two
+    cols = columns_of(jnp.concatenate([f_one, f_two, best, total], axis=0))[64 * half : 64 * half + 64]
     lane = lanes((64, 128))
-    tiles = []
-    for pair in range(2):
-        span = slice(128 * pair, 128 * pair + 128)
-        factor = [
-            jnp.where(lane < 64, cols[:, s + 2 * pair : s + 2 * pair + 1], cols[:, s + 2 * pair + 1 : s + 2 * pair + 2])
-            for s in (0, 4)
-        ]
-        tiles.append(arrived[0:64, span] * factor[0] + mine[0:64, span] * factor[1])
-    return jnp.concatenate(tiles, axis=1), jnp.concatenate([best, total], axis=0)
-
-
-def sum_body(acc_ref, out_ref, slots, send, recv):
+    factor = [jnp.where(lane < 64, cols[:, s : s + 1], cols[:, s + 1 : s + 2]) for s in (0, 2)]
+    values = arrived[0:64] * factor[0] + mine[0:64] * factor[1]
+    return values, jnp.concatenate([best, total, one[4:8]], axis=0)
+
+
+def exchange_body(
+    acc_ref, x_ref, p_ref, own_ref, cot_ref, out_ref, all_ref, self_ref, dself_ref,
+    slots, total, pay, h_own, send, recv, grad_send, grad_recv, own_sem,
+):
     z = lax.axis_index("src")
     right, left = lax.rem(z + 1, 8), lax.rem(z + 7, 8)
-    greet([], [right, left])()
+    wait_all = greet([], [right, left])
+    wait_all()
 
     def copy(step, way, sub):
         if isinstance(step, int) and step == 0:
@@ -410,9 +439,10 @@
             device_id_type=MESH,
         )
 
-    order = [(way, sub) for sub in range(2) for way in range(2)]
+    order = [(way, sub) for sub in range(4) for way in range(2)]
     for way, sub in order:
         copy(0, way, sub).start()
+    h_own[...] = dot(x_ref[...], p_ref[...], NN, HIGHEST)
 
     def block_of(step, way):
         return lax.rem(z + 15 - step, 8) if way == 0 else lax.rem(z + 1 + step, 8)
@@ -427,9 +457,9 @@
                 device_id={"src": right if way == 0 else left},
                 device_id_type=MESH,
             ).wait_recv()
-            values, stats = merge(slots[step - 1, way, sub], acc_ref[block_of(step, way), way, sub], sub)
+            values, stats = merge(slots[step - 1, way, sub], acc_ref[block_of(step, way), way, sub], sub % 2)
             slots[step - 1, way, sub, 0:64] = values
-            slots[step - 1, way, sub, 64:72, 0:128] = stats
+            slots[step - 1, way, sub, 64:72] = stats
             copy(step, way, sub).start()
         return carry
 
@@ -437,28 +467,45 @@
     for way, sub in order:
         last = copy(6, way, sub)
         last.wait_recv()
-        values, stats = merge(slots[6, way, sub], acc_ref[z, way, sub], sub)
-        out_ref[way, sub, 0:64] = values
-        out_ref[way, sub, 64:72, 0:128] = stats
-        out_ref[way, sub, 64:72, 128:256] = jnp.zeros((8, 128), F32)
+        values, stats = merge(slots[6, way, sub], acc_ref[z, way, sub], sub % 2)
+        total[way, sub, 0:64] = values
+        total[way, sub, 64:72] = stats
+    owner_rows(total, own_ref, h_own, cot_ref, out_ref, pay, self_ref, dself_ref)
+    own_copy = pltpu.make_async_copy(pay, all_ref.at[z], own_sem)
+    own_copy.start()
+    links = Links(grad_send, grad_recv)
+    run_chains([around(links, pay, all_ref, z)])
     for step in range(7):
         for way, sub in order:
             copy(step, way, sub).wait_send()
-
-
-def sum_over_src(acc):
+    own_copy.wait()
+    links.drain()
+
+
+def exchange(acc, x, proj, own, cotangent):
     return pl.pallas_call(
-        sum_body,
-        out_shape=jax.ShapeDtypeStruct((2, 2, 72, 256), F32),
-        in_specs=[VMEM],
-        out_specs=VMEM,
+        exchange_body,
+        out_shape=(
+            jax.ShapeDtypeStruct((128, 512), F32),
+            jax.ShapeDtypeStruct((8, 136, 512), F32),
+            jax.ShapeDtypeStruct((512, 128), F32),
+            jax.ShapeDtypeStruct((8, 128), F32),
+        ),
+        in_specs=[VMEM] * 5,
+        out_specs=(VMEM, ANY, VMEM, VMEM),
         scratch_shapes=[
-            pltpu.VMEM((7, 2, 2, 72, 256), F32),
-            pltpu.SemaphoreType.DMA((7, 2, 2)),
-            pltpu.SemaphoreType.DMA((7, 2, 2)),
+            pltpu.VMEM((7, 2, 4, 72, 128), F32),
+            pltpu.VMEM((2, 4, 72, 128), F32),
+            pltpu.VMEM((136, 512), F32),
+            pltpu.VMEM((128, 512), F32),
+            pltpu.SemaphoreType.DMA((7, 2, 4)),
+            pltpu.SemaphoreType.DMA((7, 2, 4)),
+            pltpu.SemaphoreType.DMA((14,)),
+            pltpu.SemaphoreType.DMA((14,)),
+            pltpu.SemaphoreType.DMA,
         ],
         compiler_params=pltpu.CompilerParams(collective_id=1, has_side_effects=True),
-    )(acc)
+    )(acc, x, proj, own, cotangent)
 
 
 def minus_one(power):
@@ -466,15 +513,12 @@
     return jnp.where(power > -0.1, series, jnp.exp(power) - 1)
 
 
-def owner_body(total_ref, x_ref, p_ref, att_ref, a_ref, cot_ref, out_ref, pay_ref, self_ref, dself_ref):
-    proj = p_ref[...]
-    h_own = dot(x_ref[...], proj, NN, HIGHEST)
-    rows = score_rows(att_ref[...], proj) * LOG2E
-    raw = a_ref[...] + dot(rows, x_ref[...], NT, HIGHEST)
+def owner_rows(total_ref, own_ref, h_own, cot_ref, out_ref, pay_ref, self_ref, dself_ref):
+    raw = own_ref[0:8] + own_ref[8:16]
     own = leaky(raw)
-    parts = [total_ref[way, 0, 64:72, 0:128] for way in range(2)]
-    tops = jnp.concatenate([part[0:4] for part in parts], axis=0)
-    sums = jnp.concatenate([part[4:8] for part in parts], axis=0)
+    parts = [total_ref[pair // 2, 2 * (pair % 2), 64:72] for pair in range(4)]
+    tops = jnp.concatenate([part[0:2] for part in parts], axis=0)
+    sums = jnp.concatenate([part[2:4] for part in parts], axis=0)
     best = jnp.maximum(tops, own)
     f_tot, f_own = jnp.exp2(tops - best), jnp.exp2(own - best)
     inverse = 1.0 / (sums * f_tot + f_own)
@@ -485,8 +529,7 @@
     for pair in range(4):
         way, inner = pair // 2, pair % 2
         span = slice(128 * pair, 128 * pair + 128)
-        local = slice(128 * inner, 128 * inner + 128)
-        acc = jnp.concatenate([total_ref[way, sub, 0:64, local] for sub in range(2)], axis=0)
+        acc = jnp.concatenate([total_ref[way, 2 * inner + half, 0:64] for half in range(2)], axis=0)
 
         def wide(kind):
             s = 8 * kind + 2 * pair
@@ -514,75 +557,16 @@
     dself_ref[...] = turned[8:16]
 
 
-def owner_rows(total, x, proj, att_src, a_own, cotangent):
-    return pl.pallas_call(
-        owner_body,
-        out_shape=(
-            jax.ShapeDtypeStruct((128, 512), F32),
-            jax.ShapeDtypeStruct((136, 512), F32),
-            jax.ShapeDtypeStruct((512, 128), F32),
-            jax.ShapeDtypeStruct((8, 128), F32),
-        ),
-        in_specs=[VMEM] * 6,
-        out_specs=(VMEM,) * 4,
-    )(total, x, proj, att_src, a_own, cotangent)
-
-
-def grads_body(pay_ref, all_ref, send, recv, own_sem):
-    z = lax.axis_index("src")
-    right, left = lax.rem(z + 1, 8), lax.rem(z + 7, 8)
-    wait_all = greet([], [right, left])
-    own_copy = pltpu.make_async_copy(pay_ref, all_ref.at[z], own_sem)
-    own_copy.start()
-    wait_all()
-    links = Links(send, recv)
-    spans = (pl.ds(0, 64), pl.ds(64, 72))
-
-    def push(step, way, sub):
-        block = lax.rem(z + 8 - step, 8) if way == 0 else lax.rem(z + step, 8)
-        part = all_ref.at[block, spans[sub]]
-        src = pay_ref.at[spans[sub]] if step == 0 else part
-        return links.push(src, part, src=right if way == 0 else left)
-
-    order = [(way, sub) for sub in range(2) for way in range(2)]
-    coming = {item: push(0, *item) for item in order}
-    for step in range(1, 4):
-        for item in order:
-            coming[item].wait_recv()
-            if step < 3 or item[0] == item[1]:
-                coming[item] = push(step, *item)
-            else:
-                del coming[item]
-    for copy in coming.values():
-        copy.wait_recv()
-    own_copy.wait()
-    links.drain()
-
-
-def gather_grads(pay):
-    return pl.pallas_call(
-        grads_body,
-        out_shape=jax.ShapeDtypeStruct((8, 136, 512), F32),
-        in_specs=[VMEM],
-        out_specs=ANY,
-        scratch_shapes=[
-            pltpu.SemaphoreType.DMA((14,)),
-            pltpu.SemaphoreType.DMA((14,)),
-            pltpu.SemaphoreType.DMA,
-        ],
-        compiler_params=pltpu.CompilerParams(collective_id=2, has_side_effects=True),
-    )(pay)
-
-
 def backward_body(
-    blocks, counts, spot, panel, p_ref, att_ref, a_ref, masks, pay_ref, self_ref, dself_ref,
-    dx_out, dp_out, ddst_out, p_cat, hb, gn, gt, top, abc, dots, ddst, dsrc, dh, p_wide, att_wide,
-    dx_slots, dx_sems, x_ref, mask_ref, sems,
+    blocks, counts, spot, panel, p_ref, att_ref, group, masks, pay_ref, self_ref, dself_ref,
+    dx_out, w_out, ddst_out, p_cat, hb, gn, gt, top, abc, dots, ddst, dsrc, dh, p_wide, att_wide,
+    dx_slots, dx_sems, dp_out, group_sems, a_ref, x_ref, mask_ref, sems,
 ):
-    arrive = stream_in(panel, x_ref, masks, mask_ref, sems)
+    arrive = stream_in(panel, x_ref, masks, mask_ref, group, a_ref, sems)
     split_weights(p_ref, p_cat)
     prepare_features(x_ref, p_cat, hb, arrive)
     pltpu.make_async_copy(masks, mask_ref, sems.at[8]).wait()
+    pltpu.make_async_copy(group.at[:, pl.ds(128, 8), pl.ds(128, 128)], a_ref, sems.at[9]).wait()
     even = (lax.broadcasted_iota(jnp.int32, (128, 1), 0) < 64).astype(F32)
     odd = 1.0 - even
 
@@ -614,7 +598,7 @@
     dh[spot[0]] = self_ref[...]
 
     def step(k, carry):
-        b, c = blocks[k, 0], blocks[k, 1]
+        b, c = blocks[2 * k], blocks[2 * k + 1]
         keep = mask_ref[k] > 0
         scores = x_ref[c, 128:136, 0:128]
         cols = dots[b]
@@ -645,6 +629,14 @@
 
     lax.fori_loop(0, counts[0], step, 0)
 
+    def group_half(b, side):
+        part = group.at[b, pl.ds(0, 128), pl.ds(128 * side, 128)]
+        return pltpu.make_async_copy(part, abc.at[2 * b + side], group_sems.at[2 * b + side])
+
+    for b in range(8):
+        for side in range(2):
+            group_half(b, side).start()
+
     def pack_dst(b, carry):
         ddst_out[b] = jnp.concatenate(
             [jnp.sum(ddst[b * 8 + h].T, axis=0, keepdims=True) for h in range(8)], axis=0
@@ -702,19 +694,33 @@
         return carry
 
     lax.fori_loop(0, 8, project, 0)
+    u = jnp.zeros((8, 256), F32)
+    for b in range(8):
+        for side in range(2):
+            group_half(b, side).wait()
+        u += dot(ddst_out[b], jnp.concatenate([abc[2 * b], abc[2 * b + 1]], axis=1), NN, HIGHEST)
+    for i in range(32):
+        w_out[i, 0:16] = dp_out[16 * i : 16 * i + 16, 0:128]
+        w_out[i, 16:32] = dp_out[16 * i : 16 * i + 16, 128:256]
+        w_out[i, 32:48] = jnp.zeros((16, 128), F32)
+    for h in range(8):
+        for side in range(2):
+            span = slice(128 * side, 128 * side + 128)
+            w_out[h + 16 * side, 32:33] = u[h : h + 1, span]
+            w_out[8 + h + 16 * side, 32:33] = dp_out[512 + h : 513 + h, span]
     leave(6, 0).wait()
     leave(7, 1).wait()
 
 
-def backward_local(blocks, counts, spot, panel, proj, att_src, a, masks, pays, dh_self, d_self):
+def backward_local(blocks, counts, spot, panel, proj, att_src, group, masks, pays, dh_self, d_self):
     return pl.pallas_call(
         backward_body,
         out_shape=(
             jax.ShapeDtypeStruct((32, 256, 128), F32),
-            jax.ShapeDtypeStruct((528, 256), F32),
+            jax.ShapeDtypeStruct((32, 48, 128), F32),
             jax.ShapeDtypeStruct((8, 8, 128), F32),
         ),
-        in_specs=[SMEM] * 3 + [ANY, VMEM, VMEM, VMEM, ANY, VMEM, VMEM, VMEM],
+        in_specs=[SMEM] * 3 + [ANY, VMEM, VMEM, ANY, ANY, VMEM, VMEM, VMEM],
         out_specs=(ANY, VMEM, VMEM),
         scratch_shapes=[
             pltpu.VMEM((768, 512), BF16),
@@ -731,17 +737,20 @@
             pltpu.VMEM((512, 128), F32),
             pltpu.VMEM((2, 4, 256, 128), F32),
             pltpu.SemaphoreType.DMA((2,)),
+            pltpu.VMEM((528, 256), F32),
+            pltpu.SemaphoreType.DMA((16,)),
+            pltpu.VMEM((8, 8, 128), F32),
             pltpu.VMEM((32, 136, 256), F32),
             pltpu.VMEM((32, 128, 128), jnp.int32),
-            pltpu.SemaphoreType.DMA((9,)),
+            pltpu.SemaphoreType.DMA((10,)),
         ],
         compiler_params=pltpu.CompilerParams(vmem_limit_bytes=BIG_VMEM),
-    )(blocks, counts, spot, panel, proj, att_src, a, masks, pays, dh_self, d_self)
+    )(blocks, counts, spot, panel, proj, att_src, group, masks, pays, dh_self, d_self)
 
 
 def reduce_body(
-    dx_ref, dp_ref, ddst_ref, x_ref, dx_out, dp_out, dst_out,
-    send, recv, twin_dx, total, far, near, far2, near2, dst_all, pay, twin_pay, merged, plane, joined, tower,
+    dx_ref, w_ref, ddst_ref, dx_out, dp_out, dst_out,
+    send, recv, twin_dx, twin_w, total, far, near, far2, near2, dst_all, joined, tower,
 ):
     d, y, x, k, z = place()
     sibling = node(y, x, 1 - k)
@@ -752,40 +761,54 @@
     links = Links(send, recv)
     wait_all()
 
-    dst_copies = [links.push(ddst_ref.at[t], dst_all.at[z], src=t) for t in others]
-
     def rank(offset):
         return 0 if 2 in offset else (2 if offset == (0, 0) else 1)
 
     cells = sorted([(0, 0)] + offsets, key=rank)
+    twin_weights = links.push(w_ref.at[:, :, 1 - k], twin_w, dst=sibling)
     twin_copies = {}
     for dy, dx in cells:
         yy, xx = lax.rem(y + dy, 4), lax.rem(x + dx, 4)
         twin_copies[dy, dx] = links.push(dx_ref.at[yy, xx, 1 - k], twin_dx.at[yy, xx], dst=sibling)
+    dst_copies = [links.push(ddst_ref.at[t], dst_all.at[z], src=t) for t in others]
+    twin_weights.wait_recv()
+
+    def add_cells(wanted):
+        for dy, dx in cells:
+            if rank((dy, dx)) != wanted:
+                continue
+            yy, xx = lax.rem(y + dy, 4), lax.rem(x + dx, 4)
+            twin_copies[dy, dx].wait_recv()
+            total[yy, xx, 0:128] = dx_ref[yy, xx, k, 0:128] + twin_dx[yy, xx, 0:128]
+            total[yy, xx, 128:152] = w_ref[yy, xx, k, 0:24] + twin_w[yy, xx, 0:24]
+            total[yy, xx, 152:280] = dx_ref[yy, xx, k, 128:256] + twin_dx[yy, xx, 128:256]
+            total[yy, xx, 280:304] = w_ref[yy, xx, k, 24:48] + twin_w[yy, xx, 24:48]
 
     def ring(region, plus, minus, far_buf, near_buf):
-        c0 = links.push(region(2, 0), far_buf.at[0], dst=plus)
-        c1 = links.push(region(2, 1), far_buf.at[1], dst=minus)
-        c2 = links.push(region(1, 1), near_buf.at[0], dst=plus)
-        c3 = links.push(region(-1, 0), near_buf.at[1], dst=minus)
+        c0 = links.push(region(2, 0), far_buf(0, 0), dst=plus)
+        c1 = links.push(region(2, 1), far_buf(1, 1), dst=minus)
+        yield
+        c2 = links.push(region(1, 1), near_buf(0, 1), dst=plus)
+        c3 = links.push(region(-1, 0), near_buf(1, 0), dst=minus)
         yield
         c0.wait_recv()
         part = region(1, 0)
-        part[...] += far_buf[0]
-        c4 = links.push(part, near_buf.at[2], dst=plus)
+        part[...] += far_buf(0, 0)[...]
+        c4 = links.push(part, near_buf(2, 0), dst=plus)
         yield
         c1.wait_recv()
         part = region(-1, 1)
-        part[...] += far_buf[1]
-        c5 = links.push(part, near_buf.at[3], dst=minus)
+        part[...] += far_buf(1, 1)[...]
+        c5 = links.push(part, near_buf(3, 1), dst=minus)
+        yield
         for copy, index, piece in ((c2, 0, 1), (c3, 1, 0), (c4, 2, 0), (c5, 3, 1)):
             yield
             copy.wait_recv()
             part = region(0, piece)
-            part[...] += near_buf[index]
+            part[...] += near_buf(index, piece)[...]
 
     def grads(half):
-        rows = pl.ds(128 * half, 128)
+        rows = pl.ds(152 * half, 152)
 
         def wide(v, piece):
             if half == 0:
@@ -793,87 +816,59 @@
             return total.at[pl.ds(2 * piece, 2), lax.rem(x + v + 4, 4), rows]
 
         def narrow(u, piece):
-            span = pl.ds(128 * half + 64 * piece, 64)
+            span = pl.ds(152 * half + 80 * piece, 80 - 8 * piece)
             if half == 0:
                 return total.at[y, lax.rem(x + u + 4, 4), span]
             return total.at[lax.rem(y + u + 4, 4), x, span]
 
+        def short(buffer):
+            return lambda index, piece: buffer.at[half, index, pl.ds(0, 80 - 8 * piece)]
+
         along_y = (node(y + 1, x, k), node(y - 1, x, k))
         along_x = (node(y, x + 1, k), node(y, x - 1, k))
         first, then = (along_y, along_x) if half == 0 else (along_x, along_y)
-        yield from ring(wide, *first, far.at[half], near.at[half])
-        yield from ring(narrow, *then, far2.at[half], near2.at[half])
-
-    def weights():
-        for i in range(32):
-            pay[i // 2, i % 2, 0:16] = dp_ref[16 * i : 16 * i + 16, 0:128]
-            pay[i // 2, i % 2, 16:32] = dp_ref[16 * i : 16 * i + 16, 128:256]
-            pay[i // 2, i % 2, 32:40] = jnp.zeros((8, 128), F32)
-        for h in range(8):
-            for side in range(2):
-                i = 8 + h + 16 * side
-                pay[i // 2, i % 2, 32:33] = dp_ref[512 + h : 513 + h, 128 * side : 128 * side + 128]
-        yield
-        for copy in dst_copies:
-            copy.wait_recv()
-        dst_all[z] = ddst_ref[z]
-        dst_total = dst_all[0]
-        for t in range(1, 8):
-            dst_total = dst_total + dst_all[t]
-        dst_out[...] = dst_total
-        u = dot(dst_total, x_ref[...], NN, HIGHEST)
-        for h in range(8):
-            for side in range(2):
-                i = h + 16 * side
-                pay[i // 2, i % 2, 32:33] = u[h : h + 1, 128 * side : 128 * side + 128]
-        over = links.push(pay.at[:, 1 - k], twin_pay, dst=sibling)
-        yield
-        over.wait_recv()
-        merged[...] = pay[:, k] + twin_pay[...]
-        coming = []
-        for dy, dx in offsets:
-            target = lax.rem(y + dy, 4) * 4 + lax.rem(x + dx, 4)
-            coming.append(links.push(merged.at[target], plane.at[chip], dst=node(y + dy, x + dx, k)))
-        plane[chip] = merged[chip]
-        yield
-        for copy in coming:
-            copy.wait_recv()
-        value = plane[0]
-        for i in range(1, 16):
-            value = value + plane[i]
-        joined[...] = value
-        tower[z] = value
-        coming = [links.push(joined, tower.at[z], src=t) for t in others]
-        yield
-        for copy in coming:
-            copy.wait_recv()
-        value = tower[0]
-        for i in range(1, 8):
-            value = value + tower[i]
-        dp_out[chip, k] = value
-        coming = [
-            links.push(dp_out.at[chip, k], dp_out.at[chip, k], dst=node(y + dy, x + dx, k)) for dy, dx in offsets
-        ]
-        yield
-        for copy in coming:
-            copy.wait_recv()
-        over = links.push(dp_out.at[:, k], dp_out.at[:, k], dst=sibling)
-        yield
-        over.wait_recv()
-
-    small = weights()
-    next(small)
-    for dy, dx in cells:
-        yy, xx = lax.rem(y + dy, 4), lax.rem(x + dx, 4)
-        twin_copies[dy, dx].wait_recv()
-        total[yy, xx] = dx_ref[yy, xx, k] + twin_dx[yy, xx]
-    run_chains([grads(0), grads(1), small])
-    dx_out[...] = total[y, x]
+        yield from ring(wide, *first, lambda i, p: far.at[half, i], lambda i, p: near.at[half, i])
+        yield from ring(narrow, *then, short(far2), short(near2))
+
+    chains = [grads(0), grads(1)]
+    for wanted in range(3):
+        add_cells(wanted)
+        if wanted < 2:
+            for chain in chains:
+                next(chain)
+    run_chains(chains)
+
+    joined[0:24] = total[y, x, 128:152]
+    joined[24:40] = total[y, x, 280:296]
+    tower[z] = joined[...]
+    coming = [links.push(joined, tower.at[z], src=t) for t in others]
+    dx_out[0:128] = total[y, x, 0:128]
+    dx_out[128:256] = total[y, x, 152:280]
+    for copy in dst_copies:
+        copy.wait_recv()
+    dst_all[z] = ddst_ref[z]
+    dst_total = dst_all[0]
+    for t in range(1, 8):
+        dst_total = dst_total + dst_all[t]
+    dst_out[...] = dst_total
+    for copy in coming:
+        copy.wait_recv()
+    value = tower[0]
+    for i in range(1, 8):
+        value = value + tower[i]
+    dp_out[chip, k] = value
+    coming = [
+        links.push(dp_out.at[chip, k], dp_out.at[chip, k], dst=node(y + dy, x + dx, k)) for dy, dx in offsets
+    ]
+    for copy in coming:
+        copy.wait_recv()
+    over = links.push(dp_out.at[:, k], dp_out.at[:, k], dst=sibling)
+    over.wait_recv()
     links.drain()
 
 
-def reduce_grads(dx, dp, ddst, x):
-    count = 7 + 16 + 24 + 1 + 15 + 7 + 15 + 1
+def reduce_grads(dx, w, ddst):
+    count = 1 + 16 + 7 + 24 + 7 + 15 + 1
     return pl.pallas_call(
         reduce_body,
         out_shape=(
@@ -881,29 +876,26 @@
             jax.ShapeDtypeStruct((16, 2, 40, 128), F32),
             jax.ShapeDtypeStruct((8, 128), F32),
         ),
-        in_specs=[VMEM] * 4,
+        in_specs=[VMEM] * 3,
         out_specs=(VMEM,) * 3,
         scratch_shapes=[
             pltpu.SemaphoreType.DMA((count,)),
             pltpu.SemaphoreType.DMA((count,)),
             pltpu.VMEM((4, 4, 256, 128), F32),
-            pltpu.VMEM((4, 4, 256, 128), F32),
-            pltpu.VMEM((2, 2, 2, 128, 128), F32),
-            pltpu.VMEM((2, 4, 2, 128, 128), F32),
-            pltpu.VMEM((2, 2, 64, 128), F32),
-            pltpu.VMEM((2, 4, 64, 128), F32),
+            pltpu.VMEM((4, 4, 48, 128), F32),
+            pltpu.VMEM((4, 4, 304, 128), F32),
+            pltpu.VMEM((2, 2, 2, 152, 128), F32),
+            pltpu.VMEM((2, 4, 2, 152, 128), F32),
+            pltpu.VMEM((2, 2, 80, 128), F32),
+            pltpu.VMEM((2, 4, 80, 128), F32),
             pltpu.VMEM((8, 8, 128), F32),
-            pltpu.VMEM((16, 2, 40, 128), F32),
-            pltpu.VMEM((16, 40, 128), F32),
-            pltpu.VMEM((16, 40, 128), F32),
-            pltpu.VMEM((16, 40, 128), F32),
             pltpu.VMEM((40, 128), F32),
             pltpu.VMEM((8, 40, 128), F32),
         ],
         compiler_params=pltpu.CompilerParams(
-            collective_id=3, has_side_effects=True, vmem_limit_bytes=BIG_VMEM
+            collective_id=2, has_side_effects=True, vmem_limit_bytes=BIG_VMEM
         ),
-    )(dx.reshape(4, 4, 2, 256, 128), dp, ddst, x)
+    )(dx.reshape(4, 4, 2, 256, 128), w.reshape(4, 4, 2, 48, 128), ddst)
 
 
 def finish_body(dx_ref, w_ref, dst_ref, p_ref, dst_att_ref, in_ref, proj_ref, src_ref, dst_out):
@@ -946,21 +938,17 @@
 
 
 def shards(inputs, projection, att_src, att_dst, blocks, counts, tile_masks, cotangent):
-    coords = blocks[0, 0]
+    coords = blocks.reshape(64)
     live = counts.reshape(1)
     masks = tile_masks[0, 0]
-    z = lax.axis_index("src")
-    spot = jnp.stack([lax.axis_index("dst"), z]).astype(jnp.int32)
-    panel, a = gather_inputs(inputs, projection, att_src, att_dst)
-    acc = forward_local(coords, live, panel, projection, a, masks)
-    total = sum_over_src(acc)
-    a_own = lax.dynamic_index_in_dim(a, z, 0, keepdims=False)
-    output, pay, dh_self, d_self = owner_rows(total, inputs, projection, att_src, a_own, cotangent)
-    pays = gather_grads(pay)
-    dx, dp, ddst = backward_local(
-        coords, live, spot, panel, projection, att_src, a, masks, pays, dh_self, d_self
+    spot = jnp.stack([lax.axis_index("dst"), lax.axis_index("src")]).astype(jnp.int32)
+    panel, group, own = gather_inputs(inputs, projection, att_src, att_dst)
+    acc = forward_local(coords, live, panel, projection, group, masks)
+    output, pays, dh_self, d_self = exchange(acc, inputs, projection, own, cotangent)
+    dx, w, ddst = backward_local(
+        coords, live, spot, panel, projection, att_src, group, masks, pays, dh_self, d_self
     )
-    dx_own, weights, dst_total = reduce_grads(dx, dp, ddst, inputs)
+    dx_own, weights, dst_total = reduce_grads(dx, w, ddst)
     in_grad, proj_grad, src_grad, dst_grad = finish(dx_own, weights, dst_total, projection, att_dst)
     return (output, in_grad, proj_grad, src_grad, dst_grad)
 

time: 230 us -> 220 us (0.957)
  Pallas kernels: 225 us -> 215 us
    pallas_call x4 -> x2, Pallas kernels: 88.7 us -> 83 us  [the longest x1 55.3 us: exchange(): pl.pallas_call(exchange_body, out_shape=(jax.ShapeDtypeStruct((128, 512),...]
    pallas_call x1, Pallas kernels: 53.9 us -> 49.5 us  [reduce_grads(): pl.pallas_call(reduce_body, out_shape=(jax.ShapeDtypeStruct((256, 128), F...]
    squeeze x2 -> x0, local copies, waits for them, and re-layouts: 2.63 us -> none  [the longest x1 1.36 us: shards(): coords = blocks[0, 0]]
where the time goes in v3:
time: 220 us; the launch traced here: 219 us
  Pallas kernels  215 us (98%)
    pallas_call x1, Pallas kernels, exchange(): pl.pallas_call(exchange_body, out_shape=(jax.ShapeDtypeStruct((128, 512),...  55.3 us
    pallas_call x1, Pallas kernels, reduce_grads(): pl.pallas_call(reduce_body, out_shape=(jax.ShapeDtypeStruct((256, 128), F...  49.5 us
    pallas_call x1, Pallas kernels, backward_local(): pl.pallas_call(backward_body, out_shape=(jax.ShapeDtypeStruct((32, 256, 1...  44.6 us
    pallas_call x1, Pallas kernels, gather_inputs(): pl.pallas_call(gather_body, out_shape=(jax.ShapeDtypeStruct((32, 136, 256...  34 us
    pallas_call x1, Pallas kernels, forward_local(): pl.pallas_call(forward_body, out_shape=jax.ShapeDtypeStruct((8, 2, 4, 72,...  27.6 us
    pallas_call x1, Pallas kernels, finish(): pl.pallas_call(finish_body, out_shape=(jax.ShapeDtypeStruct((128, 256), F...  4.41 us

profile of v3, /device:TPU:1, one launch (start us, length us, event | category | flops | bytes accessed | tf_op | source)
XLA Modules:
  0.0 219.4 jit_solution(15911131370413490893)
XLA Ops:
  0.6 0.8 copy.14
  1.4 0.6 reshape.25.blocks
  2.7 34.0 %shard_map.119 = (f32[32,136,256]{2,1,0:T(8,128)}, f32[8,136,256]{2,1,0:T(8,128)}, f32[16,128]{1,0:T(8,128)}) custom-call(f32[128,256]{1,0:T(8,128)} %x_ref.3, f32[256,512]{1,0:T(8,128)} %p_ref.9, f32[8,64]{1,0:T(8,128)} %att_ref.1, f32[8,64]{1,0:T(8,128)} %dst_att_ref.1), custom_call_target="tpu_custom_call" | custom-call | tf_op jit(solution)/shard_map/pallas_call | solution.py:223
  36.7 27.6 %shard_map.120.acc_ref = f32[8,2,4,72,128]{4,3,2,1,0:T(8,128)} custom-call(s32[64]{0:T(128)} %reshape.25.blocks, s32[1]{0:T(128)} %bitcast.9.counts, f32[32,136,256]{2,1,0:T(8,128)} %get-tuple-element.22.panel, f32[256,512]{1,0:T(8,128)} %p_ref.9, f32[8,136,256]{2,1,0:T(8,128)} %get-tuple-element.23.group, s32[32,128,128]{2,1,0:T(8,128)} %bitcast.11), custom_call_target="tpu_custom_call" | custom-call | tf_op jit(solution)/shard_map/pallas_call | solution.py:385
  64.3 55.3 %shard_map.121 = (f32[128,512]{1,0:T(8,128)}, f32[8,136,512]{2,1,0:T(8,128)}, f32[512,128]{1,0:T(8,128)}, f32[8,128]{1,0:T(8,128)}) custom-call(f32[8,2,4,72,128]{4,3,2,1,0:T(8,128)} %shard_map.120.acc_ref, f32[128,256]{1,0:T(8,128)} %x_ref.3, f32[256,512]{1,0:T(8,128)} %p_ref.9, f32[16,128]{1,0:T(8,128)} %get-tuple-element.24.own_ref, f32[128,512]{1,0:T(8,128)} %cot_ref.1), custom_call_target="tpu_custom_call" | custom-call | tf_op jit(solution)/shard_map/pallas_call | solution.py:486
  119.7 0.6 pad_add_fusion.spot
  120.2 44.6 %shard_map.122 = (f32[32,256,128]{2,1,0:T(8,128)}, f32[32,48,128]{2,1,0:T(8,128)}, f32[8,8,128]{2,1,0:T(8,128)}) custom-call(s32[64]{0:T(128)} %reshape.25.blocks, s32[1]{0:T(128)} %bitcast.10.counts, s32[2]{0:T(128)} %pad_add_fusion.spot, f32[32,136,256]{2,1,0:T(8,128)} %get-tuple-element.22.panel, f32[256,512]{1,0:T(8,128)} %p_ref.9, f32[8,64]{1,0:T(8,128)} %att_ref.1, ...), custom_call_target="tpu_custom_call" | custom-call | tf_op jit(solution)/shard_map/pallas_call | solution.py:716
  164.8 0.0 copy-start
  164.8 49.5 %shard_map.123 = (f32[256,128]{1,0:T(8,128)}, f32[16,2,40,128]{3,2,1,0:T(8,128)}, f32[8,128]{1,0:T(8,128)}) custom-call(f32[4,4,2,256,128]{4,3,2,1,0:T(8,128)} %bitcast.13, f32[4,4,2,48,128]{4,3,2,1,0:T(8,128)} %bitcast.14, f32[8,8,128]{2,1,0:T(8,128)} %get-tuple-element.31.ddst_ref), custom_call_target="tpu_custom_call" | custom-call | tf_op jit(solution)/shard_map/pallas_call | solution.py:872
  214.3 4.4 %shard_map.124 = (f32[128,256]{1,0:T(8,128)}, f32[256,512]{1,0:T(8,128)}, f32[8,64]{1,0:T(8,128)}, f32[8,64]{1,0:T(8,128)}) custom-call(f32[256,128]{1,0:T(8,128)} %get-tuple-element.32.dx_ref, f32[32,40,128]{2,1,0:T(8,128)} %bitcast.15, f32[8,128]{1,0:T(8,128)} %get-tuple-element.34.dst_ref, f32[256,512]{1,0:T(8,128)} %p_ref.9, f32[8,64]{1,0:T(8,128)} %dst_att_ref.1), custom_call_target="tpu_custom_call" | custom-call | tf_op jit(solution)/shard_map/pallas_call | solution.py:927
  218.7 0.0 copy-done
  218.7 0.7 copy.17
Async XLA Ops:
  164.8 53.9 %copy-start = (f32[128,512]{1,0:T(8,128)S(1)}, f32[128,512]{1,0:T(8,128)}, u32[]{:S(2)}) copy-start(f32[128,512]{1,0:T(8,128)} %get-tuple-element.44) | copy-start | bytes 786436

commit v4 on v3

--- a/solution.py
+++ b/solution.py
@@ -258,9 +258,7 @@
     return part
 
 
-def prepare_features(x_ref, p_cat, hb, arrive):
-    even = (lanes((1, 128)) < 64).astype(BF16)
-    odd = (lanes((1, 128)) >= 64).astype(BF16)
+def prepare_features(x_ref, p_cat, hb, arrive, leave):
     n = 4
 
     def step(group, carry):
@@ -273,10 +271,9 @@
                 for side in range(2):
                     part = (slice(128 * s, 128 * s + 128), slice(128 * side, 128 * side + 128))
                     pair = 2 * wide + side
-                    hb[group * n + s, pair, 0:128] = h_high[part] * even
-                    hb[group * n + s, pair, 128:256] = h_high[part] * odd
-                    hb[group * n + s, pair, 256:384] = h_low[part] * even
-                    hb[group * n + s, pair, 384:512] = h_low[part] * odd
+                    hb[group * n + s, pair, 0:128] = h_high[part]
+                    hb[group * n + s, pair, 128:256] = h_low[part]
+        leave(group).start()
         return carry
 
     lax.fori_loop(0, 32 // n, step, 0)
@@ -309,68 +306,124 @@
                 put(k, b, h, out[128 * b : 128 * b + 128, 128 * k : 128 * k + 128])
 
 
+SPAN = 40.0
+
+
+def peaks(scores):
+    high, low = scores[0], scores[0]
+    for c in range(1, 32):
+        high, low = jnp.maximum(high, scores[c]), jnp.minimum(low, scores[c])
+    high, low = jnp.max(high, axis=1, keepdims=True), jnp.min(low, axis=1, keepdims=True)
+    return high, jnp.max(high - low)
+
+
+def source_factors(scores, high, factors):
+    for c in range(32):
+        below = scores[c] - high
+        factors[c, 0:8] = jnp.exp2(below)
+        factors[c, 8:16] = jnp.exp2(0.2 * below)
+
+
+def target_factors(a, high, shift):
+    best = a + high
+    return [jnp.exp2(jnp.minimum(part - shift, 100.0)) for part in (best, 0.2 * best)]
+
+
 def forward_body(
-    blocks, counts, panel, p_ref, group, masks, acc_out, p_cat, hb, top, abc, sums, acc, top_rows, a_ref, x_ref, mask_ref, sems
+    blocks, counts, panel, p_ref, group, masks, acc_out, hb_out, b_out,
+    p_cat, hb, top, abc, sums, acc, top_rows, factors, hb_sems, a_ref, x_ref, mask_ref, sems
 ):
     arrive = stream_in(panel, x_ref, masks, mask_ref, group, a_ref, sems)
+
+    def leave(i):
+        span = pl.ds(4 * i, 4)
+        return pltpu.make_async_copy(hb.at[span], hb_out.at[span], hb_sems.at[i])
+
     split_weights(p_ref, p_cat)
-    prepare_features(x_ref, p_cat, hb, arrive)
+    prepare_features(x_ref, p_cat, hb, arrive, leave)
     pltpu.make_async_copy(masks, mask_ref, sems.at[8]).wait()
     pltpu.make_async_copy(group.at[:, pl.ds(128, 8), pl.ds(128, 128)], a_ref, sems.at[9]).wait()
-    top[...] = jnp.full(top.shape, NEG, F32)
+    b_out[...] = x_ref[:, 128:136, 0:128]
     sums[...] = jnp.zeros(sums.shape, F32)
     acc[...] = jnp.zeros(acc.shape, F32)
     live = counts[0]
-
-    def find_top(k, carry):
-        b, c = blocks[2 * k], blocks[2 * k + 1]
-        keep = mask_ref[k] > 0
-        scores = x_ref[c, 128:136, 0:128]
-        for h in range(8):
-            top[b * 8 + h] = jnp.maximum(top[b * 8 + h], jnp.where(keep, scores[h : h + 1], NEG))
-        return carry
-
-    lax.fori_loop(0, live, find_top, 0)
-
-    def find_rows(b, carry):
-        best = jnp.concatenate([jnp.max(top[b * 8 + h].T, axis=0, keepdims=True) for h in range(8)], axis=0)
-        top_rows[b] = leaky(a_ref[b] + best)
-        return carry
-
-    lax.fori_loop(0, 8, find_rows, 0)
+    high, reach = peaks(b_out)
+    close = reach < SPAN
 
     def put(kind, b, h, tile):
         (abc, top)[kind][b * 8 + h] = tile
 
-    spread_rows(lambda b: [a_ref[b], top_rows[b]], put)
-
-    def accumulate(k, carry):
-        b, c = blocks[2 * k], blocks[2 * k + 1]
-        keep = mask_ref[k] > 0
-        scores = x_ref[c, 128:136, 0:128]
-        for pair in range(4):
-            highs, lows = [], []
-            for h in (2 * pair, 2 * pair + 1):
-                raw = abc[b * 8 + h] + jnp.where(keep, scores[h : h + 1], NEG)
-                w = jnp.exp2(leaky(raw) - top[b * 8 + h])
-                sums[b * 8 + h] += w
-                high, low = split(w)
-                highs.append(high)
-                lows.append(low)
-            left = jnp.concatenate(highs + highs + lows, axis=1)
-            right = jnp.concatenate([hb[c, pair], hb[c, pair, 0:256]], axis=0)
-            acc[b * 4 + pair] += dot(left, right)
-        return carry
-
-    lax.fori_loop(0, live, accumulate, 0)
+    def accumulate(weight):
+        lane = lanes((128, 128))
+
+        def step(k, carry):
+            b, c = blocks[2 * k], blocks[2 * k + 1]
+            keep = mask_ref[k] > 0
+            for pair in range(4):
+                sides = []
+                for h in (2 * pair, 2 * pair + 1):
+                    w = weight(b, c, h, keep)
+                    sums[b * 8 + h] += w
+                    w_high, w_low = split(w)
+                    sides.append(jnp.concatenate([w_high, w_high, w_low], axis=1))
+                right = jnp.concatenate([hb[c, pair], hb[c, pair, 0:128]], axis=0)
+                both = dot(jnp.concatenate(sides, axis=0), right)
+                acc[b * 4 + pair] += jnp.where(lane < 64, both[0:128], both[128:256])
+            return carry
+
+        lax.fori_loop(0, live, step, 0)
+
+    @pl.when(close)
+    def _():
+        source_factors(b_out, high, factors)
+        for b in range(8):
+            top_rows[b] = leaky(a_ref[b] + high)
+        spread_rows(lambda b: target_factors(a_ref[b], high, top_rows[b]), put)
+
+        def weight(b, c, h, keep):
+            one = abc[b * 8 + h] * factors[c, pl.ds(h, 1)]
+            two = top[b * 8 + h] * factors[c, pl.ds(8 + h, 1)]
+            return jnp.where(keep, jnp.maximum(one, two), 0.0)
+
+        accumulate(weight)
+
+    @pl.when(jnp.logical_not(close))
+    def _():
+        top[...] = jnp.full(top.shape, NEG, F32)
+
+        def find_top(k, carry):
+            b, c = blocks[2 * k], blocks[2 * k + 1]
+            keep = mask_ref[k] > 0
+            for h in range(8):
+                top[b * 8 + h] = jnp.maximum(top[b * 8 + h], jnp.where(keep, b_out[c, pl.ds(h, 1)], NEG))
+            return carry
+
+        lax.fori_loop(0, live, find_top, 0)
+
+        def find_rows(b, carry):
+            best = jnp.concatenate([jnp.max(top[b * 8 + h].T, axis=0, keepdims=True) for h in range(8)], axis=0)
+            top_rows[b] = leaky(a_ref[b] + best)
+            return carry
+
+        lax.fori_loop(0, 8, find_rows, 0)
+        spread_rows(lambda b: [a_ref[b], top_rows[b]], put)
+
+        def weight(b, c, h, keep):
+            raw = abc[b * 8 + h] + jnp.where(keep, b_out[c, pl.ds(h, 1)], NEG)
+            return jnp.exp2(leaky(raw) - top[b * 8 + h])
+
+        accumulate(weight)
 
     def pack(b, carry):
         totals = [jnp.sum(sums[b * 8 + h].T, axis=0, keepdims=True) for h in range(8)]
+        tops = [
+            jnp.where(totals[h] > 0, top_rows[b, h : h + 1], 0.2 * NEG) for h in range(8)
+        ]
         for way in range(2):
             for inner in range(2):
                 h = 4 * way + 2 * inner
                 packed = jnp.concatenate(
-                    [top_rows[b, h : h + 2]] + totals[h : h + 2] + [jnp.zeros((4, 128), F32)], axis=0
+                    tops[h : h + 2] + totals[h : h + 2] + [jnp.zeros((4, 128), F32)], axis=0
                 )
                 for half in range(2):
                     sub = 2 * inner + half
@@ -379,22 +432,30 @@
         return carry
 
     lax.fori_loop(0, 8, pack, 0)
+    for i in range(8):
+        leave(i).wait()
 
 
 def forward_local(blocks, counts, panel, proj, group, masks):
     return pl.pallas_call(
         forward_body,
-        out_shape=jax.ShapeDtypeStruct((8, 2, 4, 72, 128), F32),
+        out_shape=(
+            jax.ShapeDtypeStruct((8, 2, 4, 72, 128), F32),
+            jax.ShapeDtypeStruct((32, 4, 256, 128), BF16),
+            jax.ShapeDtypeStruct((32, 8, 128), F32),
+        ),
         in_specs=[SMEM, SMEM, ANY, VMEM, ANY, ANY],
-        out_specs=VMEM,
+        out_specs=(VMEM, ANY, VMEM),
         scratch_shapes=[
             pltpu.VMEM((768, 512), BF16),
-            pltpu.VMEM((32, 4, 512, 128), BF16),
+            pltpu.VMEM((32, 4, 256, 128), BF16),
             pltpu.VMEM((64, 128, 128), F32),
             pltpu.VMEM((64, 128, 128), F32),
             pltpu.VMEM((64, 128, 128), F32),
             pltpu.VMEM((32, 128, 128), F32),
             pltpu.VMEM((8, 8, 128), F32),
+            pltpu.VMEM((32, 16, 128), F32),
+            pltpu.SemaphoreType.DMA((8,)),
             pltpu.VMEM((8, 8, 128), F32),
             pltpu.VMEM((32, 136, 256), F32),
             pltpu.VMEM((32, 128, 128), jnp.int32),
@@ -558,76 +619,109 @@
 
 
 def backward_body(
-    blocks, counts, spot, panel, p_ref, att_ref, group, masks, pay_ref, self_ref, dself_ref,
-    dx_out, w_out, ddst_out, p_cat, hb, gn, gt, top, abc, dots, ddst, dsrc, dh, p_wide, att_wide,
-    dx_slots, dx_sems, dp_out, group_sems, a_ref, x_ref, mask_ref, sems,
+    blocks, counts, spot, panel, p_ref, att_ref, group, masks, pay_ref, self_ref, dself_ref, hb_in, b_ref,
+    dx_out, w_out, ddst_out, hb, gn, gt, top, abc, minus, ddst, dsrc, dh, p_wide, att_wide,
+    dx_slots, dx_sems, dp_out, group_sems, hb_sem, factors, a_ref, x_ref, mask_ref, sems,
 ):
+    features = pltpu.make_async_copy(hb_in, hb, hb_sem)
+    features.start()
     arrive = stream_in(panel, x_ref, masks, mask_ref, group, a_ref, sems)
-    split_weights(p_ref, p_cat)
-    prepare_features(x_ref, p_cat, hb, arrive)
-    pltpu.make_async_copy(masks, mask_ref, sems.at[8]).wait()
-    pltpu.make_async_copy(group.at[:, pl.ds(128, 8), pl.ds(128, 128)], a_ref, sems.at[9]).wait()
-    even = (lax.broadcasted_iota(jnp.int32, (128, 1), 0) < 64).astype(F32)
-    odd = 1.0 - even
+    lane = lanes((128, 128))
+    minus[...] = jnp.full(minus.shape, -1.0, BF16)
 
     def setup(b, carry):
-        dots[b] = columns_of(pay_ref[b, 128:136, 128:256])
+        row_dot = pay_ref[b, 128:136, 128:256]
+        high = row_dot.astype(BF16).astype(F32)
+        middle = (row_dot - high).astype(BF16).astype(F32)
+        dots = columns_of(jnp.concatenate([high, middle, row_dot - high - middle], axis=0))
         for pair in range(4):
             grad = pay_ref[b, 0:128, 128 * pair : 128 * pair + 128]
-            high, low = split(grad)
-            gn[b, pair, :, 0:128] = high
-            gn[b, pair, :, 128:256] = low
-            turned = grad.T
-            e_high, e_low = split(turned * even)
-            o_high, o_low = split(turned * odd)
-            gt[b, pair, :, 0:128] = e_high
-            gt[b, pair, :, 128:256] = o_high
-            gt[b, pair, :, 256:384] = e_low
-            gt[b, pair, :, 384:512] = o_low
+            for side in range(2):
+                rows = slice(128 * side, 128 * side + 128)
+                mine = lane >= 64 if side else lane < 64
+                g_high, g_low = split(jnp.where(mine, grad, 0.0))
+                gn[b, pair, rows, 0:128] = g_high
+                gn[b, pair, rows, 128:256] = g_low
+                own_dot = jnp.logical_and(lane < 24, lax.rem(lane, 8) == 2 * pair + side)
+                gn[b, pair, rows, 256:384] = jnp.where(own_dot, dots, 0.0).astype(BF16)
+            t_high, t_low = split(grad.T)
+            gt[b, pair, :, 0:128] = t_high
+            gt[b, pair, :, 128:256] = t_low
         return carry
 
     lax.fori_loop(0, 8, setup, 0)
 
-    def put(kind, b, h, tile):
-        (abc, top)[kind][b * 8 + h] = tile
-
-    spread_rows(lambda b: [a_ref[b], pay_ref[b, 128:136, 0:128]], put)
     ddst[...] = jnp.zeros(ddst.shape, F32)
     dsrc[...] = jnp.zeros(dsrc.shape, F32)
     dh[...] = jnp.zeros(dh.shape, F32)
     dh[spot[0]] = self_ref[...]
-
-    def step(k, carry):
-        b, c = blocks[2 * k], blocks[2 * k + 1]
-        keep = mask_ref[k] > 0
-        scores = x_ref[c, 128:136, 0:128]
-        cols = dots[b]
-        for pair in range(4):
-            g_high, g_low = gn[b, pair, :, 0:128], gn[b, pair, :, 128:256]
-            h_high, h_low = hb[c, pair, 0:256], hb[c, pair, 256:512]
-            d_alpha = dot(
-                jnp.concatenate([g_high, g_high, g_low], axis=1),
-                jnp.concatenate([h_high, h_low, h_high], axis=1),
-                NT,
-            )
-            highs, lows = [], []
-            for side in range(2):
-                h = 2 * pair + side
-                raw = abc[b * 8 + h] + jnp.where(keep, scores[h : h + 1], NEG)
-                w = jnp.exp2(leaky(raw) - top[b * 8 + h])
-                d_raw = w * (d_alpha[:, 128 * side : 128 * side + 128] - cols[:, h : h + 1])
-                d_raw = jnp.where(raw > 0, d_raw, 0.2 * d_raw)
-                ddst[b * 8 + h] += d_raw
-                dsrc[c * 8 + h] += jnp.sum(d_raw.reshape(16, 8, 128), axis=0)
-                high, low = split(w)
-                highs.append(high)
-                lows.append(low)
-            left = jnp.concatenate([gt[b, pair], gt[b, pair, :, 0:256]], axis=1)
-            right = jnp.concatenate(highs + highs + lows, axis=0)
-            dh[c, 128 * pair : 128 * pair + 128] += dot(left, right)
-        return carry
-
-    lax.fori_loop(0, counts[0], step, 0)
+    high, reach = peaks(b_ref)
+    close = reach < SPAN
+    pltpu.make_async_copy(masks, mask_ref, sems.at[8]).wait()
+    pltpu.make_async_copy(group.at[:, pl.ds(128, 8), pl.ds(128, 128)], a_ref, sems.at[9]).wait()
+
+    def put(kind, b, h, tile):
+        (abc, top)[kind][b * 8 + h] = tile
+
+    def accumulate(weight):
+        def step(k, carry):
+            b, c = blocks[2 * k], blocks[2 * k + 1]
+            keep = mask_ref[k] > 0
+            for pair in range(4):
+                g_high, h_high = gn[b, pair, :, 0:128], hb[c, pair, 0:128]
+                d_alpha = dot(
+                    jnp.concatenate([g_high, g_high, gn[b, pair, :, 128:384]], axis=1),
+                    jnp.concatenate([h_high, hb[c, pair, 128:256], h_high, minus[...]], axis=1),
+                    NT,
+                )
+                highs, lows = [], []
+                for side in range(2):
+                    h = 2 * pair + side
+                    w, positive = weight(b, c, h, keep)
+                    d_raw = w * d_alpha[128 * side : 128 * side + 128]
+                    d_raw = jnp.where(positive, d_raw, 0.2 * d_raw)
+                    ddst[b * 8 + h] += d_raw
+                    dsrc[c * 8 + h] += jnp.sum(d_raw.reshape(16, 8, 128), axis=0)
+                    w_high, w_low = split(w)
+                    highs.append(w_high)
+                    lows.append(w_low)
+                w_high, w_low = jnp.concatenate(highs, axis=1), jnp.concatenate(lows, axis=1)
+                both = dot(
+                    jnp.concatenate([gt[b, pair], gt[b, pair, :, 0:128]], axis=1),
+                    jnp.concatenate([w_high, w_high, w_low], axis=0),
+                )
+                dh[c, 128 * pair : 128 * pair + 64] += both[0:64, 0:128]
+                dh[c, 128 * pair + 64 : 128 * pair + 128] += both[64:128, 128:256]
+            return carry
+
+        lax.fori_loop(0, counts[0], step, 0)
+
+    @pl.when(close)
+    def _():
+        source_factors(b_ref, high, factors)
+        spread_rows(lambda b: target_factors(a_ref[b], high, pay_ref[b, 128:136, 0:128]), put)
+        features.wait()
+
+        def weight(b, c, h, keep):
+            one = abc[b * 8 + h] * factors[c, pl.ds(h, 1)]
+            two = top[b * 8 + h] * factors[c, pl.ds(8 + h, 1)]
+            return jnp.where(keep, jnp.maximum(one, two), 0.0), one > two
+
+        accumulate(weight)
+
+    @pl.when(jnp.logical_not(close))
+    def _():
+        spread_rows(lambda b: [a_ref[b], pay_ref[b, 128:136, 0:128]], put)
+        features.wait()
+
+        def weight(b, c, h, keep):
+            raw = abc[b * 8 + h] + jnp.where(keep, b_ref[c, pl.ds(h, 1)], NEG)
+            return jnp.exp2(leaky(raw) - top[b * 8 + h]), raw > 0
+
+        accumulate(weight)
+
+    for i in range(8):
+        arrive(i).wait()
 
     def group_half(b, side):
         part = group.at[b, pl.ds(0, 128), pl.ds(128 * side, 128)]
@@ -712,7 +806,7 @@
     leave(7, 1).wait()
 
 
-def backward_local(blocks, counts, spot, panel, proj, att_src, group, masks, pays, dh_self, d_self):
+def backward_local(blocks, counts, spot, panel, proj, att_src, group, masks, pays, dh_self, d_self, hb, b):
     return pl.pallas_call(
         backward_body,
         out_shape=(
@@ -720,16 +814,15 @@
             jax.ShapeDtypeStruct((32, 48, 128), F32),
             jax.ShapeDtypeStruct((8, 8, 128), F32),
         ),
-        in_specs=[SMEM] * 3 + [ANY, VMEM, VMEM, ANY, ANY, VMEM, VMEM, VMEM],
+        in_specs=[SMEM] * 3 + [ANY, VMEM, VMEM, ANY, ANY, VMEM, VMEM, VMEM, ANY, VMEM],
         out_specs=(ANY, VMEM, VMEM),
         scratch_shapes=[
-            pltpu.VMEM((768, 512), BF16),
-            pltpu.VMEM((32, 4, 512, 128), BF16),
+            pltpu.VMEM((32, 4, 256, 128), BF16),
+            pltpu.VMEM((8, 4, 256, 384), BF16),
             pltpu.VMEM((8, 4, 128, 256), BF16),
-            pltpu.VMEM((8, 4, 128, 512), BF16),
             pltpu.VMEM((64, 128, 128), F32),
             pltpu.VMEM((64, 128, 128), F32),
-            pltpu.VMEM((8, 128, 128), F32),
+            pltpu.VMEM((128, 128), BF16),
             pltpu.VMEM((64, 128, 128), F32),
             pltpu.VMEM((256, 8, 128), F32),
             pltpu.VMEM((32, 512, 128), F32),
@@ -739,13 +832,15 @@
             pltpu.SemaphoreType.DMA((2,)),
             pltpu.VMEM((528, 256), F32),
             pltpu.SemaphoreType.DMA((16,)),
+            pltpu.SemaphoreType.DMA,
+            pltpu.VMEM((32, 16, 128), F32),
             pltpu.VMEM((8, 8, 128), F32),
             pltpu.VMEM((32, 136, 256), F32),
             pltpu.VMEM((32, 128, 128), jnp.int32),
             pltpu.SemaphoreType.DMA((10,)),
         ],
         compiler_params=pltpu.CompilerParams(vmem_limit_bytes=BIG_VMEM),
-    )(blocks, counts, spot, panel, proj, att_src, group, masks, pays, dh_self, d_self)
+    )(blocks, counts, spot, panel, proj, att_src, group, masks, pays, dh_self, d_self, hb, b)
 
 
 def reduce_body(
@@ -943,10 +1038,10 @@
     masks = tile_masks[0, 0]
     spot = jnp.stack([lax.axis_index("dst"), lax.axis_index("src")]).astype(jnp.int32)
     panel, group, own = gather_inputs(inputs, projection, att_src, att_dst)
-    acc = forward_local(coords, live, panel, projection, group, masks)
+    acc, hb, b = forward_local(coords, live, panel, projection, group, masks)
     output, pays, dh_self, d_self = exchange(acc, inputs, projection, own, cotangent)
     dx, w, ddst = backward_local(
-        coords, live, spot, panel, projection, att_src, group, masks, pays, dh_self, d_self
+        coords, live, spot, panel, projection, att_src, group, masks, pays, dh_self, d_self, hb, b
     )
     dx_own, weights, dst_total = reduce_grads(dx, w, ddst)
     in_grad, proj_grad, src_grad, dst_grad = finish(dx_own, weights, dst_total, projection, att_dst)

time: 220 us -> 215 us (0.977)
  Pallas kernels: 215 us -> 211 us
    pallas_call x1, Pallas kernels: 44.6 us -> 32.8 us  [backward_local(): pl.pallas_call(backward_body, out_shape=(jax.ShapeDtypeStruct((32, 256, 1...]
    pallas_call x1, Pallas kernels: 49.5 us -> 58.3 us  [reduce_grads(): pl.pallas_call(reduce_body, out_shape=(jax.ShapeDtypeStruct((256, 128), F...]
    pallas_call x1, Pallas kernels: 27.6 us -> 21 us  [forward_local(): pl.pallas_call(forward_body, out_shape=(jax.ShapeDtypeStruct((8, 2, 4, 72...]
    pallas_call x1, Pallas kernels: 55.3 us -> 60.2 us  [exchange(): pl.pallas_call(exchange_body, out_shape=(jax.ShapeDtypeStruct((128, 512),...]
where the time goes in v4:
time: 215 us
  Pallas kernels  211 us (98%)
    pallas_call x1, Pallas kernels, exchange(): pl.pallas_call(exchange_body, out_shape=(jax.ShapeDtypeStruct((128, 512),...  60.2 us
    pallas_call x1, Pallas kernels, reduce_grads(): pl.pallas_call(reduce_body, out_shape=(jax.ShapeDtypeStruct((256, 128), F...  58.3 us
    pallas_call x1, Pallas kernels, gather_inputs(): pl.pallas_call(gather_body, out_shape=(jax.ShapeDtypeStruct((32, 136, 256...  34 us
    pallas_call x1, Pallas kernels, backward_local(): pl.pallas_call(backward_body, out_shape=(jax.ShapeDtypeStruct((32, 256, 1...  32.8 us
    pallas_call x1, Pallas kernels, forward_local(): pl.pallas_call(forward_body, out_shape=(jax.ShapeDtypeStruct((8, 2, 4, 72...  21 us
    pallas_call x1, Pallas kernels, finish(): pl.pallas_call(finish_body, out_shape=(jax.ShapeDtypeStruct((128, 256), F...  4.41 us

profile of v4, /device:TPU:1, one launch (start us, length us, event | category | flops | bytes accessed | tf_op | source)
XLA Modules:
  0.0 214.6 jit_solution(6260614662175059439)
XLA Ops:
  0.6 0.8 copy.14
  1.4 0.6 reshape.25.blocks
  2.7 34.0 %shard_map.119 = (f32[32,136,256]{2,1,0:T(8,128)}, f32[8,136,256]{2,1,0:T(8,128)}, f32[16,128]{1,0:T(8,128)}) custom-call(f32[128,256]{1,0:T(8,128)} %x_ref.3, f32[256,512]{1,0:T(8,128)} %p_ref.9, f32[8,64]{1,0:T(8,128)} %att_ref.1, f32[8,64]{1,0:T(8,128)} %dst_att_ref.1), custom_call_target="tpu_custom_call" | custom-call | tf_op jit(solution)/shard_map/pallas_call | solution.py:223
  36.7 21.0 %shard_map.120 = (f32[8,2,4,72,128]{4,3,2,1,0:T(8,128)}, bf16[32,4,256,128]{3,2,1,0:T(8,128)(2,1)}, f32[32,8,128]{2,1,0:T(8,128)}) custom-call(s32[64]{0:T(128)} %reshape.25.blocks, s32[1]{0:T(128)} %bitcast.9.counts, f32[32,136,256]{2,1,0:T(8,128)} %get-tuple-element.25.panel, f32[256,512]{1,0:T(8,128)} %p_ref.9, f32[8,136,256]{2,1,0:T(8,128)} %get-tuple-element.26.group, ...), custom_call_target="tpu_custom_call" | custom-call | tf_op jit(solution)/shard_map/pallas_call | solution.py:440
  57.7 60.2 %shard_map.121 = (f32[128,512]{1,0:T(8,128)}, f32[8,136,512]{2,1,0:T(8,128)}, f32[512,128]{1,0:T(8,128)}, f32[8,128]{1,0:T(8,128)}) custom-call(f32[8,2,4,72,128]{4,3,2,1,0:T(8,128)} %get-tuple-element.27.acc_ref, f32[128,256]{1,0:T(8,128)} %x_ref.3, f32[256,512]{1,0:T(8,128)} %p_ref.9, f32[16,128]{1,0:T(8,128)} %get-tuple-element.28.own_ref, f32[128,512]{1,0:T(8,128)} %cot_ref.1), custom_call_target="tpu_custom_call" | custom-call | tf_op jit(solution)/shard_map/pallas_call | solution.py:547
  117.9 0.6 pad_add_fusion.spot
  118.4 32.8 %shard_map.122 = (f32[32,256,128]{2,1,0:T(8,128)}, f32[32,48,128]{2,1,0:T(8,128)}, f32[8,8,128]{2,1,0:T(8,128)}) custom-call(s32[64]{0:T(128)} %reshape.25.blocks, s32[1]{0:T(128)} %bitcast.10.counts, s32[2]{0:T(128)} %pad_add_fusion.spot, f32[32,136,256]{2,1,0:T(8,128)} %get-tuple-element.25.panel, f32[256,512]{1,0:T(8,128)} %p_ref.9, f32[8,64]{1,0:T(8,128)} %att_ref.1, ...), custom_call_target="tpu_custom_call" | custom-call | tf_op jit(solution)/shard_map/pallas_call | solution.py:810
  151.2 0.0 copy-start
  151.2 58.3 %shard_map.123 = (f32[256,128]{1,0:T(8,128)}, f32[16,2,40,128]{3,2,1,0:T(8,128)}, f32[8,128]{1,0:T(8,128)}) custom-call(f32[4,4,2,256,128]{4,3,2,1,0:T(8,128)} %bitcast.13, f32[4,4,2,48,128]{4,3,2,1,0:T(8,128)} %bitcast.14, f32[8,8,128]{2,1,0:T(8,128)} %get-tuple-element.37.ddst_ref), custom_call_target="tpu_custom_call" | custom-call | tf_op jit(solution)/shard_map/pallas_call | solution.py:967
  209.5 4.4 %shard_map.124 = (f32[128,256]{1,0:T(8,128)}, f32[256,512]{1,0:T(8,128)}, f32[8,64]{1,0:T(8,128)}, f32[8,64]{1,0:T(8,128)}) custom-call(f32[256,128]{1,0:T(8,128)} %get-tuple-element.38.dx_ref, f32[32,40,128]{2,1,0:T(8,128)} %bitcast.15, f32[8,128]{1,0:T(8,128)} %get-tuple-element.40.dst_ref, f32[256,512]{1,0:T(8,128)} %p_ref.9, f32[8,64]{1,0:T(8,128)} %dst_att_ref.1), custom_call_target="tpu_custom_call" | custom-call | tf_op jit(solution)/shard_map/pallas_call | solution.py:1022
  213.9 0.0 copy-done
  213.9 0.7 copy.17
Async XLA Ops:
  151.2 62.8 %copy-start = (f32[128,512]{1,0:T(8,128)S(1)}, f32[128,512]{1,0:T(8,128)}, u32[]{:S(2)}) copy-start(f32[128,512]{1,0:T(8,128)} %get-tuple-element.50) | copy-start | bytes 786436

commit v5 on v4

--- a/solution.py
+++ b/solution.py
@@ -796,7 +796,7 @@
     for i in range(32):
         w_out[i, 0:16] = dp_out[16 * i : 16 * i + 16, 0:128]
         w_out[i, 16:32] = dp_out[16 * i : 16 * i + 16, 128:256]
-        w_out[i, 32:48] = jnp.zeros((16, 128), F32)
+        w_out[i, 32:40] = jnp.zeros((8, 128), F32)
     for h in range(8):
         for side in range(2):
             span = slice(128 * side, 128 * side + 128)
@@ -811,7 +811,7 @@
         backward_body,
         out_shape=(
             jax.ShapeDtypeStruct((32, 256, 128), F32),
-            jax.ShapeDtypeStruct((32, 48, 128), F32),
+            jax.ShapeDtypeStruct((32, 40, 128), F32),
             jax.ShapeDtypeStruct((8, 8, 128), F32),
         ),
         in_specs=[SMEM] * 3 + [ANY, VMEM, VMEM, ANY, ANY, VMEM, VMEM, VMEM, ANY, VMEM],
@@ -845,7 +845,7 @@
 
 def reduce_body(
     dx_ref, w_ref, ddst_ref, dx_out, dp_out, dst_out,
-    send, recv, twin_dx, twin_w, total, far, near, far2, near2, dst_all, joined, tower,
+    send, recv, twin_dx, twin_w, total, far, near, far2, near2, dst_all, merged, plane, joined, tower,
 ):
     d, y, x, k, z = place()
     sibling = node(y, x, 1 - k)
@@ -860,50 +860,50 @@
         return 0 if 2 in offset else (2 if offset == (0, 0) else 1)
 
     cells = sorted([(0, 0)] + offsets, key=rank)
-    twin_weights = links.push(w_ref.at[:, :, 1 - k], twin_w, dst=sibling)
+    twin_weights = links.push(w_ref.at[:, 1 - k], twin_w, dst=sibling)
     twin_copies = {}
     for dy, dx in cells:
         yy, xx = lax.rem(y + dy, 4), lax.rem(x + dx, 4)
         twin_copies[dy, dx] = links.push(dx_ref.at[yy, xx, 1 - k], twin_dx.at[yy, xx], dst=sibling)
+    twin_weights.wait_recv()
+    merged[...] = w_ref[:, k] + twin_w[...]
+    plane_copies = []
+    for dy, dx in offsets:
+        target = lax.rem(y + dy, 4) * 4 + lax.rem(x + dx, 4)
+        plane_copies.append(links.push(merged.at[target], plane.at[chip], dst=node(y + dy, x + dx, k)))
     dst_copies = [links.push(ddst_ref.at[t], dst_all.at[z], src=t) for t in others]
-    twin_weights.wait_recv()
 
     def add_cells(wanted):
         for dy, dx in cells:
-            if rank((dy, dx)) != wanted:
-                continue
-            yy, xx = lax.rem(y + dy, 4), lax.rem(x + dx, 4)
-            twin_copies[dy, dx].wait_recv()
-            total[yy, xx, 0:128] = dx_ref[yy, xx, k, 0:128] + twin_dx[yy, xx, 0:128]
-            total[yy, xx, 128:152] = w_ref[yy, xx, k, 0:24] + twin_w[yy, xx, 0:24]
-            total[yy, xx, 152:280] = dx_ref[yy, xx, k, 128:256] + twin_dx[yy, xx, 128:256]
-            total[yy, xx, 280:304] = w_ref[yy, xx, k, 24:48] + twin_w[yy, xx, 24:48]
+            if rank((dy, dx)) == wanted:
+                yy, xx = lax.rem(y + dy, 4), lax.rem(x + dx, 4)
+                twin_copies[dy, dx].wait_recv()
+                total[yy, xx] = dx_ref[yy, xx, k] + twin_dx[yy, xx]
 
     def ring(region, plus, minus, far_buf, near_buf):
-        c0 = links.push(region(2, 0), far_buf(0, 0), dst=plus)
-        c1 = links.push(region(2, 1), far_buf(1, 1), dst=minus)
+        c0 = links.push(region(2, 0), far_buf.at[0], dst=plus)
+        c1 = links.push(region(2, 1), far_buf.at[1], dst=minus)
         yield
-        c2 = links.push(region(1, 1), near_buf(0, 1), dst=plus)
-        c3 = links.push(region(-1, 0), near_buf(1, 0), dst=minus)
+        c2 = links.push(region(1, 1), near_buf.at[0], dst=plus)
+        c3 = links.push(region(-1, 0), near_buf.at[1], dst=minus)
         yield
         c0.wait_recv()
         part = region(1, 0)
-        part[...] += far_buf(0, 0)[...]
-        c4 = links.push(part, near_buf(2, 0), dst=plus)
+        part[...] += far_buf[0]
+        c4 = links.push(part, near_buf.at[2], dst=plus)
         yield
         c1.wait_recv()
         part = region(-1, 1)
-        part[...] += far_buf(1, 1)[...]
-        c5 = links.push(part, near_buf(3, 1), dst=minus)
-        yield
+        part[...] += far_buf[1]
+        c5 = links.push(part, near_buf.at[3], dst=minus)
         for copy, index, piece in ((c2, 0, 1), (c3, 1, 0), (c4, 2, 0), (c5, 3, 1)):
             yield
             copy.wait_recv()
             part = region(0, piece)
-            part[...] += near_buf(index, piece)[...]
+            part[...] += near_buf[index]
 
     def grads(half):
-        rows = pl.ds(152 * half, 152)
+        rows = pl.ds(128 * half, 128)
 
         def wide(v, piece):
             if half == 0:
@@ -911,34 +911,54 @@
             return total.at[pl.ds(2 * piece, 2), lax.rem(x + v + 4, 4), rows]
 
         def narrow(u, piece):
-            span = pl.ds(152 * half + 80 * piece, 80 - 8 * piece)
+            span = pl.ds(128 * half + 64 * piece, 64)
             if half == 0:
                 return total.at[y, lax.rem(x + u + 4, 4), span]
             return total.at[lax.rem(y + u + 4, 4), x, span]
 
-        def short(buffer):
-            return lambda index, piece: buffer.at[half, index, pl.ds(0, 80 - 8 * piece)]
-
         along_y = (node(y + 1, x, k), node(y - 1, x, k))
         along_x = (node(y, x + 1, k), node(y, x - 1, k))
         first, then = (along_y, along_x) if half == 0 else (along_x, along_y)
-        yield from ring(wide, *first, lambda i, p: far.at[half, i], lambda i, p: near.at[half, i])
-        yield from ring(narrow, *then, short(far2), short(near2))
+        yield from ring(wide, *first, far.at[half], near.at[half])
+        yield from ring(narrow, *then, far2.at[half], near2.at[half])
 
     chains = [grads(0), grads(1)]
-    for wanted in range(3):
-        add_cells(wanted)
-        if wanted < 2:
+
+    def advance(count):
+        for _ in range(count):
             for chain in chains:
                 next(chain)
+
+    add_cells(0)
+    advance(1)
+    add_cells(1)
+    advance(1)
+    add_cells(2)
+    plane[chip] = merged[chip]
+    for copy in plane_copies:
+        copy.wait_recv()
+    value = plane[0]
+    for i in range(1, 16):
+        value = value + plane[i]
+    joined[...] = value
+    tower[z] = value
+    tower_copies = [links.push(joined, tower.at[z], src=t) for t in others]
+    advance(2)
+    for copy in tower_copies:
+        copy.wait_recv()
+    value = tower[0]
+    for i in range(1, 8):
+        value = value + tower[i]
+    dp_out[chip, k] = value
+    spread_copies = [
+        links.push(dp_out.at[chip, k], dp_out.at[chip, k], dst=node(y + dy, x + dx, k)) for dy, dx in offsets
+    ]
+    advance(7)
+    for copy in spread_copies:
+        copy.wait_recv()
+    over = links.push(dp_out.at[:, k], dp_out.at[:, k], dst=sibling)
     run_chains(chains)
-
-    joined[0:24] = total[y, x, 128:152]
-    joined[24:40] = total[y, x, 280:296]
-    tower[z] = joined[...]
-    coming = [links.push(joined, tower.at[z], src=t) for t in others]
-    dx_out[0:128] = total[y, x, 0:128]
-    dx_out[128:256] = total[y, x, 152:280]
+    dx_out[...] = total[y, x]
     for copy in dst_copies:
         copy.wait_recv()
     dst_all[z] = ddst_ref[z]
@@ -946,24 +966,12 @@
     for t in range(1, 8):
         dst_total = dst_total + dst_all[t]
     dst_out[...] = dst_total
-    for copy in coming:
-        copy.wait_recv()
-    value = tower[0]
-    for i in range(1, 8):
-        value = value + tower[i]
-    dp_out[chip, k] = value
-    coming = [
-        links.push(dp_out.at[chip, k], dp_out.at[chip, k], dst=node(y + dy, x + dx, k)) for dy, dx in offsets
-    ]
-    for copy in coming:
-        copy.wait_recv()
-    over = links.push(dp_out.at[:, k], dp_out.at[:, k], dst=sibling)
     over.wait_recv()
     links.drain()
 
 
 def reduce_grads(dx, w, ddst):
-    count = 1 + 16 + 7 + 24 + 7 + 15 + 1
+    count = 1 + 16 + 15 + 7 + 24 + 7 + 15 + 1
     return pl.pallas_call(
         reduce_body,
         out_shape=(
@@ -977,20 +985,22 @@
             pltpu.SemaphoreType.DMA((count,)),
             pltpu.SemaphoreType.DMA((count,)),
             pltpu.VMEM((4, 4, 256, 128), F32),
-            pltpu.VMEM((4, 4, 48, 128), F32),
-            pltpu.VMEM((4, 4, 304, 128), F32),
-            pltpu.VMEM((2, 2, 2, 152, 128), F32),
-            pltpu.VMEM((2, 4, 2, 152, 128), F32),
-            pltpu.VMEM((2, 2, 80, 128), F32),
-            pltpu.VMEM((2, 4, 80, 128), F32),
+            pltpu.VMEM((16, 40, 128), F32),
+            pltpu.VMEM((4, 4, 256, 128), F32),
+            pltpu.VMEM((2, 2, 2, 128, 128), F32),
+            pltpu.VMEM((2, 4, 2, 128, 128), F32),
+            pltpu.VMEM((2, 2, 64, 128), F32),
+            pltpu.VMEM((2, 4, 64, 128), F32),
             pltpu.VMEM((8, 8, 128), F32),
+            pltpu.VMEM((16, 40, 128), F32),
+            pltpu.VMEM((16, 40, 128), F32),
             pltpu.VMEM((40, 128), F32),
             pltpu.VMEM((8, 40, 128), F32),
         ],
         compiler_params=pltpu.CompilerParams(
             collective_id=2, has_side_effects=True, vmem_limit_bytes=BIG_VMEM
         ),
-    )(dx.reshape(4, 4, 2, 256, 128), w.reshape(4, 4, 2, 48, 128), ddst)
+    )(dx.reshape(4, 4, 2, 256, 128), w.reshape(16, 2, 40, 128), ddst)
 
 
 def finish_body(dx_ref, w_ref, dst_ref, p_ref, dst_att_ref, in_ref, proj_ref, src_ref, dst_out):

time: 215 us -> 204 us (0.949)
  Pallas kernels: 211 us -> 200 us
    pallas_call x1, Pallas kernels: 58.3 us -> 40.4 us  [reduce_grads(): pl.pallas_call(reduce_body, out_shape=(jax.ShapeDtypeStruct((256, 128), F...]
    pallas_call x1, Pallas kernels: 32.8 us -> 40.4 us  [backward_local(): pl.pallas_call(backward_body, out_shape=(jax.ShapeDtypeStruct((32, 256, 1...]
    pallas_call x1, Pallas kernels: 60.2 us -> 53.7 us  [exchange(): pl.pallas_call(exchange_body, out_shape=(jax.ShapeDtypeStruct((128, 512),...]
    pallas_call x1, Pallas kernels: 21 us -> 26.6 us  [forward_local(): pl.pallas_call(forward_body, out_shape=(jax.ShapeDtypeStruct((8, 2, 4, 72...]
where the time goes in v5:
time: 204 us
  Pallas kernels  200 us (98%)
  local copies, waits for them, and re-layouts  2.09 us (1%)
    pallas_call x1, Pallas kernels, exchange(): pl.pallas_call(exchange_body, out_shape=(jax.ShapeDtypeStruct((128, 512),...  53.7 us
    pallas_call x1, Pallas kernels, backward_local(): pl.pallas_call(backward_body, out_shape=(jax.ShapeDtypeStruct((32, 256, 1...  40.4 us
    pallas_call x1, Pallas kernels, reduce_grads(): pl.pallas_call(reduce_body, out_shape=(jax.ShapeDtypeStruct((256, 128), F...  40.4 us
    pallas_call x1, Pallas kernels, gather_inputs(): pl.pallas_call(gather_body, out_shape=(jax.ShapeDtypeStruct((32, 136, 256...  34 us
    pallas_call x1, Pallas kernels, forward_local(): pl.pallas_call(forward_body, out_shape=(jax.ShapeDtypeStruct((8, 2, 4, 72...  26.6 us
    pallas_call x1, Pallas kernels, finish(): pl.pallas_call(finish_body, out_shape=(jax.ShapeDtypeStruct((128, 256), F...  4.41 us

profile of v5, /device:TPU:1, one launch (start us, length us, event | category | flops | bytes accessed | tf_op | source)
XLA Modules:
  0.0 203.7 jit_solution(2673005577810005992)
XLA Ops:
  0.6 0.8 copy.14
  1.4 0.6 reshape.25.blocks
  2.7 34.0 %shard_map.119 = (f32[32,136,256]{2,1,0:T(8,128)}, f32[8,136,256]{2,1,0:T(8,128)}, f32[16,128]{1,0:T(8,128)}) custom-call(f32[128,256]{1,0:T(8,128)} %x_ref.3, f32[256,512]{1,0:T(8,128)} %p_ref.9, f32[8,64]{1,0:T(8,128)} %att_ref.1, f32[8,64]{1,0:T(8,128)} %dst_att_ref.1), custom_call_target="tpu_custom_call" | custom-call | tf_op jit(solution)/shard_map/pallas_call | solution.py:223
  36.7 26.6 %shard_map.120 = (f32[8,2,4,72,128]{4,3,2,1,0:T(8,128)}, bf16[32,4,256,128]{3,2,1,0:T(8,128)(2,1)}, f32[32,8,128]{2,1,0:T(8,128)}) custom-call(s32[64]{0:T(128)} %reshape.25.blocks, s32[1]{0:T(128)} %bitcast.9.counts, f32[32,136,256]{2,1,0:T(8,128)} %get-tuple-element.25.panel, f32[256,512]{1,0:T(8,128)} %p_ref.9, f32[8,136,256]{2,1,0:T(8,128)} %get-tuple-element.26.group, ...), custom_call_target="tpu_custom_call" | custom-call | tf_op jit(solution)/shard_map/pallas_call | solution.py:440
  63.3 53.7 %shard_map.121 = (f32[128,512]{1,0:T(8,128)}, f32[8,136,512]{2,1,0:T(8,128)}, f32[512,128]{1,0:T(8,128)}, f32[8,128]{1,0:T(8,128)}) custom-call(f32[8,2,4,72,128]{4,3,2,1,0:T(8,128)} %get-tuple-element.27.acc_ref, f32[128,256]{1,0:T(8,128)} %x_ref.3, f32[256,512]{1,0:T(8,128)} %p_ref.9, f32[16,128]{1,0:T(8,128)} %get-tuple-element.28.own_ref, f32[128,512]{1,0:T(8,128)} %cot_ref.1), custom_call_target="tpu_custom_call" | custom-call | tf_op jit(solution)/shard_map/pallas_call | solution.py:547
  117.0 0.7 pad_add_fusion.spot
  117.6 40.4 %shard_map.122 = (f32[32,256,128]{2,1,0:T(8,128)}, f32[32,40,128]{2,1,0:T(8,128)}, f32[8,8,128]{2,1,0:T(8,128)}) custom-call(s32[64]{0:T(128)} %reshape.25.blocks, s32[1]{0:T(128)} %bitcast.10.counts, s32[2]{0:T(128)} %pad_add_fusion.spot, f32[32,136,256]{2,1,0:T(8,128)} %get-tuple-element.25.panel, f32[256,512]{1,0:T(8,128)} %p_ref.9, f32[8,64]{1,0:T(8,128)} %att_ref.1, ...), custom_call_target="tpu_custom_call" | custom-call | tf_op jit(solution)/shard_map/pallas_call | solution.py:810
  158.1 0.0 copy-start
  158.1 40.4 %shard_map.123 = (f32[256,128]{1,0:T(8,128)}, f32[16,2,40,128]{3,2,1,0:T(8,128)}, f32[8,128]{1,0:T(8,128)}) custom-call(f32[4,4,2,256,128]{4,3,2,1,0:T(8,128)} %bitcast.13, f32[16,2,40,128]{3,2,1,0:T(8,128)} %bitcast.14, f32[8,8,128]{2,1,0:T(8,128)} %get-tuple-element.37.ddst_ref), custom_call_target="tpu_custom_call" | custom-call | tf_op jit(solution)/shard_map/pallas_call | solution.py:975
  198.5 4.4 %shard_map.124 = (f32[128,256]{1,0:T(8,128)}, f32[256,512]{1,0:T(8,128)}, f32[8,64]{1,0:T(8,128)}, f32[8,64]{1,0:T(8,128)}) custom-call(f32[256,128]{1,0:T(8,128)} %get-tuple-element.38.dx_ref, f32[32,40,128]{2,1,0:T(8,128)} %bitcast.15, f32[8,128]{1,0:T(8,128)} %get-tuple-element.40.dst_ref, f32[256,512]{1,0:T(8,128)} %p_ref.9, f32[8,64]{1,0:T(8,128)} %dst_att_ref.1), custom_call_target="tpu_custom_call" | custom-call | tf_op jit(solution)/shard_map/pallas_call | solution.py:1032
  202.9 0.0 copy-done
  202.9 0.7 copy.17
Async XLA Ops:
  158.1 44.8 %copy-start = (f32[128,512]{1,0:T(8,128)S(1)}, f32[128,512]{1,0:T(8,128)}, u32[]{:S(2)}) copy-start(f32[128,512]{1,0:T(8,128)} %get-tuple-element.50) | copy-start | bytes 786436

commit v6 on v5

--- a/solution.py
+++ b/solution.py
@@ -356,9 +356,8 @@
     def accumulate(weight):
         lane = lanes((128, 128))
 
-        def step(k, carry):
+        def slot(k, keep):
             b, c = blocks[2 * k], blocks[2 * k + 1]
-            keep = mask_ref[k] > 0
             for pair in range(4):
                 sides = []
                 for h in (2 * pair, 2 * pair + 1):
@@ -369,9 +368,13 @@
                 right = jnp.concatenate([hb[c, pair], hb[c, pair, 0:128]], axis=0)
                 both = dot(jnp.concatenate(sides, axis=0), right)
                 acc[b * 4 + pair] += jnp.where(lane < 64, both[0:128], both[128:256])
+
+        def step(two, carry):
+            slot(2 * two, mask_ref[2 * two] > 0)
+            slot(2 * two + 1, mask_ref[2 * two + 1] * jnp.where(2 * two + 1 < live, 1, 0) > 0)
             return carry
 
-        lax.fori_loop(0, live, step, 0)
+        lax.fori_loop(0, (live + 1) // 2, step, 0)
 
     @pl.when(close)
     def _():
@@ -664,9 +667,8 @@
         (abc, top)[kind][b * 8 + h] = tile
 
     def accumulate(weight):
-        def step(k, carry):
+        def slot(k, keep):
             b, c = blocks[2 * k], blocks[2 * k + 1]
-            keep = mask_ref[k] > 0
             for pair in range(4):
                 g_high, h_high = gn[b, pair, :, 0:128], hb[c, pair, 0:128]
                 d_alpha = dot(
@@ -692,9 +694,13 @@
                 )
                 dh[c, 128 * pair : 128 * pair + 64] += both[0:64, 0:128]
                 dh[c, 128 * pair + 64 : 128 * pair + 128] += both[64:128, 128:256]
+
+        def step(two, carry):
+            slot(2 * two, mask_ref[2 * two] > 0)
+            slot(2 * two + 1, mask_ref[2 * two + 1] * jnp.where(2 * two + 1 < counts[0], 1, 0) > 0)
             return carry
 
-        lax.fori_loop(0, counts[0], step, 0)
+        lax.fori_loop(0, (counts[0] + 1) // 2, step, 0)
 
     @pl.when(close)
     def _():
@@ -792,7 +798,7 @@
     for b in range(8):
         for side in range(2):
             group_half(b, side).wait()
-        u += dot(ddst_out[b], jnp.concatenate([abc[2 * b], abc[2 * b + 1]], axis=1), NN, HIGHEST)
+        u += dot(ddst_out[b], jnp.concatenate([abc[2 * b], abc[2 * b + 1]], axis=1), NN, lax.Precision.HIGH)
     for i in range(32):
         w_out[i, 0:16] = dp_out[16 * i : 16 * i + 16, 0:128]
         w_out[i, 16:32] = dp_out[16 * i : 16 * i + 16, 128:256]
@@ -1010,7 +1016,7 @@
     pad = jnp.zeros((120, 256), F32)
     score_t = jnp.concatenate([score, pad], axis=0).T
     dst_wide = jnp.concatenate([dst_ref[...], jnp.zeros((120, 128), F32)], axis=0)
-    in_ref[...] = (dx_ref[...] + dot(score_t, dst_wide, NN, HIGHEST)).T
+    in_ref[...] = (dx_ref[...] + dot(score_t, dst_wide, NN, lax.Precision.HIGH)).T
 
     def row(i):
         return jnp.concatenate([w_ref[i, 32:33], w_ref[i + 16, 32:33]], axis=1)
@@ -1022,8 +1028,8 @@
     grad_t = jnp.concatenate(
         [jnp.concatenate([w_ref[i, 0:16], w_ref[i, 16:32]], axis=1) for i in range(32)], axis=0
     )
-    proj_ref[...] = (grad_t + dot(att.T, wide_u, NN, HIGHEST)).T
-    both = dot(jnp.concatenate([u, v], axis=0), proj, NN, HIGHEST)
+    proj_ref[...] = (grad_t + dot(att.T, wide_u, NN, lax.Precision.HIGH)).T
+    both = dot(jnp.concatenate([u, v], axis=0), proj, NN, lax.Precision.HIGH)
     dst_out[...] = jnp.concatenate([both[h : h + 1, 64 * h : 64 * h + 64] for h in range(8)], axis=0)
     src_ref[...] = jnp.concatenate([both[8 + h : 9 + h, 64 * h : 64 * h + 64] for h in range(8)], axis=0)
 

time: 204 us -> 198 us (0.971)
  Pallas kernels: 200 us -> 194 us
    pallas_call x1, Pallas kernels: 40.4 us -> 33.9 us  [backward_local(): pl.pallas_call(backward_body, out_shape=(jax.ShapeDtypeStruct((32, 256, 1...]
    pallas_call x1, Pallas kernels: 26.6 us -> 21.8 us  [forward_local(): pl.pallas_call(forward_body, out_shape=(jax.ShapeDtypeStruct((8, 2, 4, 72...]
    pallas_call x1, Pallas kernels: 53.7 us -> 58.3 us  [exchange(): pl.pallas_call(exchange_body, out_shape=(jax.ShapeDtypeStruct((128, 512),...]
where the time goes in v6:
time: 198 us
  Pallas kernels  194 us (98%)
  local copies, waits for them, and re-layouts  2.09 us (1%)
    pallas_call x1, Pallas kernels, exchange(): pl.pallas_call(exchange_body, out_shape=(jax.ShapeDtypeStruct((128, 512),...  58.3 us
    pallas_call x1, Pallas kernels, reduce_grads(): pl.pallas_call(reduce_body, out_shape=(jax.ShapeDtypeStruct((256, 128), F...  41.6 us
    pallas_call x1, Pallas kernels, gather_inputs(): pl.pallas_call(gather_body, out_shape=(jax.ShapeDtypeStruct((32, 136, 256...  34 us
    pallas_call x1, Pallas kernels, backward_local(): pl.pallas_call(backward_body, out_shape=(jax.ShapeDtypeStruct((32, 256, 1...  33.9 us
    pallas_call x1, Pallas kernels, forward_local(): pl.pallas_call(forward_body, out_shape=(jax.ShapeDtypeStruct((8, 2, 4, 72...  21.8 us

profile of v6, /device:TPU:1, one launch (start us, length us, event | category | flops | bytes accessed | tf_op | source)
XLA Modules:
  0.0 197.6 jit_solution(17270906134575607899)
XLA Ops:
  0.6 0.8 copy.14
  1.4 0.6 reshape.25.blocks
  2.7 34.0 %shard_map.119 = (f32[32,136,256]{2,1,0:T(8,128)}, f32[8,136,256]{2,1,0:T(8,128)}, f32[16,128]{1,0:T(8,128)}) custom-call(f32[128,256]{1,0:T(8,128)} %x_ref.3, f32[256,512]{1,0:T(8,128)} %p_ref.9, f32[8,64]{1,0:T(8,128)} %att_ref.1, f32[8,64]{1,0:T(8,128)} %dst_att_ref.1), custom_call_target="tpu_custom_call" | custom-call | tf_op jit(solution)/shard_map/pallas_call | solution.py:223
  36.7 21.8 %shard_map.120 = (f32[8,2,4,72,128]{4,3,2,1,0:T(8,128)}, bf16[32,4,256,128]{3,2,1,0:T(8,128)(2,1)}, f32[32,8,128]{2,1,0:T(8,128)}) custom-call(s32[64]{0:T(128)} %reshape.25.blocks, s32[1]{0:T(128)} %bitcast.9.counts, f32[32,136,256]{2,1,0:T(8,128)} %get-tuple-element.25.panel, f32[256,512]{1,0:T(8,128)} %p_ref.9, f32[8,136,256]{2,1,0:T(8,128)} %get-tuple-element.26.group, ...), custom_call_target="tpu_custom_call" | custom-call | tf_op jit(solution)/shard_map/pallas_call | solution.py:443
  58.5 58.3 %shard_map.121 = (f32[128,512]{1,0:T(8,128)}, f32[8,136,512]{2,1,0:T(8,128)}, f32[512,128]{1,0:T(8,128)}, f32[8,128]{1,0:T(8,128)}) custom-call(f32[8,2,4,72,128]{4,3,2,1,0:T(8,128)} %get-tuple-element.27.acc_ref, f32[128,256]{1,0:T(8,128)} %x_ref.3, f32[256,512]{1,0:T(8,128)} %p_ref.9, f32[16,128]{1,0:T(8,128)} %get-tuple-element.28.own_ref, f32[128,512]{1,0:T(8,128)} %cot_ref.1), custom_call_target="tpu_custom_call" | custom-call | tf_op jit(solution)/shard_map/pallas_call | solution.py:550
  116.8 0.7 pad_add_fusion.spot
  117.4 33.9 %shard_map.122 = (f32[32,256,128]{2,1,0:T(8,128)}, f32[32,40,128]{2,1,0:T(8,128)}, f32[8,8,128]{2,1,0:T(8,128)}) custom-call(s32[64]{0:T(128)} %reshape.25.blocks, s32[1]{0:T(128)} %bitcast.10.counts, s32[2]{0:T(128)} %pad_add_fusion.spot, f32[32,136,256]{2,1,0:T(8,128)} %get-tuple-element.25.panel, f32[256,512]{1,0:T(8,128)} %p_ref.9, f32[8,64]{1,0:T(8,128)} %att_ref.1, ...), custom_call_target="tpu_custom_call" | custom-call | tf_op jit(solution)/shard_map/pallas_call | solution.py:816
  151.4 0.0 copy-start
  151.4 41.6 %shard_map.123 = (f32[256,128]{1,0:T(8,128)}, f32[16,2,40,128]{3,2,1,0:T(8,128)}, f32[8,128]{1,0:T(8,128)}) custom-call(f32[4,4,2,256,128]{4,3,2,1,0:T(8,128)} %bitcast.13, f32[16,2,40,128]{3,2,1,0:T(8,128)} %bitcast.14, f32[8,8,128]{2,1,0:T(8,128)} %get-tuple-element.37.ddst_ref), custom_call_target="tpu_custom_call" | custom-call | tf_op jit(solution)/shard_map/pallas_call | solution.py:981
  193.0 3.9 %shard_map.124 = (f32[128,256]{1,0:T(8,128)}, f32[256,512]{1,0:T(8,128)}, f32[8,64]{1,0:T(8,128)}, f32[8,64]{1,0:T(8,128)}) custom-call(f32[256,128]{1,0:T(8,128)} %get-tuple-element.38.dx_ref, f32[32,40,128]{2,1,0:T(8,128)} %bitcast.15, f32[8,128]{1,0:T(8,128)} %get-tuple-element.40.dst_ref, f32[256,512]{1,0:T(8,128)} %p_ref.9, f32[8,64]{1,0:T(8,128)} %dst_att_ref.1), custom_call_target="tpu_custom_call" | custom-call | tf_op jit(solution)/shard_map/pallas_call | solution.py:1038
  196.9 0.0 copy-done
  196.9 0.7 copy.17
Async XLA Ops:
  151.4 45.5 %copy-start = (f32[128,512]{1,0:T(8,128)S(1)}, f32[128,512]{1,0:T(8,128)}, u32[]{:S(2)}) copy-start(f32[128,512]{1,0:T(8,128)} %get-tuple-element.50) | copy-start | bytes 786436
